TPU v7x, 32 devices: a whole 2x2x4 slice. The times are simulated.
32 devices in a mesh: seq: 8 (over y, x, core), exp: 4 (over z).
Axes of the slice: x: 2, y: 2, z: 4, core: 2. Of those that a mesh axis runs over, the one named last changes fastest.
Arguments:
- hidden_in: float32 [24, 4, 2048], P('seq'), may hold values from -6 to 6
- cache_lens: int32 [24], replicated, may hold values from 64 to 16384, as said below
- slot_request: int32 [368], P('seq'), may hold values from -1 to 23, as said below
- slot_block: int32 [368], P('seq'), may hold values from 0 to 128, as said below
- key_cache: bfloat16 [368, 128, 2048], P('seq', None, 'exp'), may hold values from -70 to 70
- value_cache: bfloat16 [368, 128, 2048], P('seq', None, 'exp'), may hold values from -6 to 6
- attn_gain: float32 [2048], replicated, may hold values from 0.5 to 1.5
- query_weight: bfloat16 [2048, 2048], P(None, 'exp'), may hold values from -0.125 to 0.125
- key_weight: bfloat16 [2048, 2048], P(None, 'exp'), may hold values from -0.125 to 0.125
- value_weight: bfloat16 [2048, 2048], P(None, 'exp'), may hold values from -0.125 to 0.125
- out_weight: bfloat16 [2048, 2048], P('exp'), may hold values from -0.125 to 0.125
- ffn_gain: float32 [2048], replicated, may hold values from 0.5 to 1.5
- expert_ids: int32 [24, 4, 6], P('seq'), may hold values from 0 to 63, all different within a row; in each aligned block of 12 rows (0 to 11, 12 to 23, ..., all dimensions but the last counted through in order) at most 3 rows name the same one
- expert_weights: float32 [24, 4, 6], P('seq'), may hold values from 0.05 to 0.6
- gate_experts: bfloat16 [64, 2048, 1408], P('seq', None, 'exp'), may hold values from -0.125 to 0.125
- up_experts: bfloat16 [64, 2048, 1408], P('seq', None, 'exp'), may hold values from -0.125 to 0.125
- down_experts: bfloat16 [64, 1408, 2048], P('seq', 'exp'), may hold values from -0.15625 to 0.15625
- gate_shared: bfloat16 [2048, 2816], P(None, 'exp'), may hold values from -0.125 to 0.125
- up_shared: bfloat16 [2048, 2816], P(None, 'exp'), may hold values from -0.125 to 0.125
- down_shared: bfloat16 [2816, 2048], P('exp'), may hold values from -0.109375 to 0.109375
Outputs:
- hidden_out: float32 [24, 4, 2048], P('seq', None, 'exp')
- key_cache_out: bfloat16 [368, 128, 2048], P('seq', None, 'exp')
- value_cache_out: bfloat16 [368, 128, 2048], P('seq', None, 'exp')
Inputs may be any that keep to these rules, and one draw needn't show every extreme that they name: `cache_lens`: exactly two requests have 16384 positions and one has 512; the others lie between 64 and 512. `slot_request`: each block of 128 positions of each request, up to position cache_lens + 3, is held by exactly one slot; -1 marks an empty slot. `slot_block`: empty slots carry 0. `expert_ids`: among the rows of one index of seq, no expert is named more than 3 times.
All inputs are finite; a program needn't handle non-finite values.
Results may differ from a plain program's by a relative error of at most 0.02.
Values may be sent and summed in bfloat16 or wider, within the bound.
No kernel may reach another device: no remote copies, remote signals or barrier semaphores. Data moves between devices by JAX's collectives and lax.ppermute only.
A program may use at most 128 MiB of HBM per device.

v0:
```python
import math

import jax
import jax.numpy as jnp
from jax import lax
from jax.sharding import PartitionSpec as P

HD = 128
EXPERTS = 64
CAP = 3


def merged_2(array, axis, combine):
    everything = jax.tree.map(lambda part: lax.all_gather(part, axis), array)
    initial = jax.tree.map(lambda part: part[0], everything)

    def lap(k, so_far):
        return combine(so_far, jax.tree.map(lambda part: part[k], everything))

    return lax.fori_loop(1, lax.axis_size(axis), lap, initial)


def rms_scale(values, gain):
    mean_square = jnp.mean(values * values, axis=-1, keepdims=True)
    return values * lax.rsqrt(mean_square + 1e-06) * gain


def rotate(vectors, positions):
    half_size = vectors.shape[-1] // 2
    exponent = jnp.arange(half_size, dtype=jnp.float32) * (2.0 / vectors.shape[-1])
    frequency = jnp.power(jnp.float32(10000.0), -exponent)
    angles = positions.astype(jnp.float32)[..., None] * frequency
    cosine = jnp.cos(angles)[..., None, :]
    sine = jnp.sin(angles)[..., None, :]
    first_half = vectors[..., :half_size]
    second_half = vectors[..., half_size:]
    return jnp.concatenate(
        [first_half * cosine - second_half * sine, second_half * cosine + first_half * sine],
        axis=-1,
    )


def append_rows(cache, new_rows, slot_valid, slot_req, rel_pos):
    updated = cache
    for step_index in range(new_rows.shape[1]):
        hit_mask = slot_valid[:, None] & (rel_pos == step_index)
        updated = jnp.where(
            hit_mask[..., None], new_rows[slot_req, step_index][:, None, :], updated
        )
    return updated


def slot_partials(queries, keys, values, slot_valid, slot_req, slot_block, lengths):
    pool_count, block_size, full_width = keys.shape
    steps, heads, head_size = (queries.shape[1], queries.shape[2], queries.shape[3])
    slot_queries = queries[slot_req]
    key_heads = keys.reshape(pool_count, block_size, heads, head_size)
    value_heads = values.reshape(pool_count, block_size, heads, head_size)
    scores = jnp.einsum(
        "pthd,pkhd->pthk", slot_queries, key_heads, preferred_element_type=jnp.float32
    ) / math.sqrt(head_size)
    positions = slot_block[:, None] * block_size + jnp.arange(block_size, dtype=jnp.int32)[None, :]
    limits = lengths[slot_req][:, None] + jnp.arange(steps, dtype=jnp.int32)[None, :] + 1
    allowed = slot_valid[:, None, None] & (positions[:, None, :] < limits[:, :, None])
    allowed = allowed[:, :, None, :]
    block_max = jnp.max(jnp.where(allowed, scores, -1e30), axis=-1)
    safe_max = jnp.where(block_max > -1e29, block_max, 0.0)
    weights = jnp.where(allowed, jnp.exp(scores - safe_max[..., None]), 0.0)
    totals = jnp.sum(weights, axis=-1)
    rounded = weights.astype(jnp.bfloat16)
    outputs = jnp.einsum(
        "pthk,pkhd->pthd", rounded, value_heads, preferred_element_type=jnp.float32
    )
    return (block_max, totals, outputs)


def request_partials(block_max, totals, outputs, slot_valid, slot_req, requests):
    owner = slot_valid[:, None] & (
        slot_req[:, None] == jnp.arange(requests, dtype=jnp.int32)[None, :]
    )
    request_max = jnp.max(jnp.where(owner[:, :, None, None], block_max[:, None], -1e30), axis=0)
    factor = jnp.where(slot_valid[:, None, None], jnp.exp(block_max - request_max[slot_req]), 0.0)
    owner_float = owner.astype(jnp.float32)
    request_total = jnp.einsum(
        "pb,pth->bth", owner_float, totals * factor, precision=lax.Precision.HIGHEST
    )
    request_output = jnp.einsum(
        "pb,pthd->bthd", owner_float, outputs * factor[..., None], precision=lax.Precision.HIGHEST
    )
    return (request_max, request_total, request_output)


def merge_partials(earlier, later):
    first_max, first_total, first_output = earlier
    second_max, second_total, second_output = later
    joint_max = jnp.maximum(first_max, second_max)
    first_scale = jnp.exp(first_max - joint_max)
    second_scale = jnp.exp(second_max - joint_max)
    joint_total = first_total * first_scale + second_total * second_scale
    joint_output = first_output * first_scale[..., None] + second_output * second_scale[..., None]
    return (joint_max, joint_total, joint_output)


def route_tables(expert_ids, expert_weights, capacity):
    top_count = expert_ids.shape[-1]
    flat_ids = expert_ids.reshape(-1)
    assignments = flat_ids.shape[0]
    order = jnp.arange(assignments, dtype=jnp.int32)
    same_expert = flat_ids[:, None] == flat_ids[None, :]
    earlier_one = order[None, :] < order[:, None]
    rank = jnp.sum((same_expert & earlier_one).astype(jnp.int32), axis=1)
    slot_index = (flat_ids * capacity + rank).reshape(-1, top_count)
    slot_range = jnp.arange(EXPERTS * capacity, dtype=jnp.int32)
    hits = slot_index[:, :, None] == slot_range[None, None, :]
    gate_rows = expert_weights.reshape(-1, top_count)
    weighting = jnp.sum(jnp.where(hits, gate_rows[:, :, None], 0.0), axis=1)
    dispatch = jnp.any(hits, axis=1).T
    return (dispatch, weighting)


def body(
    hidden_in,
    cache_lens,
    slot_request,
    slot_block,
    key_cache,
    value_cache,
    attn_gain,
    query_weight,
    key_weight,
    value_weight,
    out_weight,
    ffn_gain,
    expert_ids,
    expert_weights,
    gate_experts,
    up_experts,
    down_experts,
    gate_shared,
    up_shared,
    down_shared,
):
    local_requests, steps, width = hidden_in.shape
    seq_count = lax.axis_size("seq")
    seq_rank = lax.axis_index("seq")
    exp_count = lax.axis_size("exp")
    exp_rank = lax.axis_index("exp")
    local_heads = query_weight.shape[1] // HD
    all_requests = cache_lens.shape[0]
    flat = hidden_in.reshape(local_requests * steps, width)
    normed = rms_scale(flat, attn_gain).astype(jnp.bfloat16)
    own_lengths = lax.dynamic_slice_in_dim(cache_lens, seq_rank * local_requests, local_requests)
    positions = own_lengths[:, None] + jnp.arange(steps, dtype=jnp.int32)[None, :]
    query_full = jnp.dot(normed, query_weight, preferred_element_type=jnp.float32).reshape(
        local_requests, steps, local_heads, HD
    )
    query_local = (
        rotate(query_full, positions)
        .astype(jnp.bfloat16)
        .reshape(local_requests * steps, local_heads * HD)
    )
    key_full = jnp.dot(normed, key_weight, preferred_element_type=jnp.float32).reshape(
        local_requests, steps, local_heads, HD
    )
    key_local = (
        rotate(key_full, positions)
        .astype(jnp.bfloat16)
        .reshape(local_requests * steps, local_heads * HD)
    )
    value_local = jnp.dot(normed, value_weight, preferred_element_type=jnp.float32).astype(
        jnp.bfloat16
    )
    gathered = (
        lax.all_gather(query_local, "seq", axis=0, tiled=True),
        lax.all_gather(key_local, "seq", axis=0, tiled=True),
        lax.all_gather(value_local, "seq", axis=0, tiled=True),
    )
    queries = gathered[0].reshape(all_requests, steps, local_heads, HD)
    new_keys = gathered[1].reshape(all_requests, steps, local_heads * HD)
    new_values = gathered[2].reshape(all_requests, steps, local_heads * HD)
    slot_valid = slot_request >= 0
    slot_req = jnp.where(slot_valid, slot_request, 0)
    block_size = key_cache.shape[1]
    rel_pos = (
        slot_block[:, None] * block_size
        + jnp.arange(block_size, dtype=jnp.int32)[None, :]
        - cache_lens[slot_req][:, None]
    )
    key_out = append_rows(key_cache, new_keys, slot_valid, slot_req, rel_pos)
    value_out = append_rows(value_cache, new_values, slot_valid, slot_req, rel_pos)
    block_max, totals, outputs = slot_partials(
        queries, key_out, value_out, slot_valid, slot_req, slot_block, cache_lens
    )
    local_parts = request_partials(block_max, totals, outputs, slot_valid, slot_req, all_requests)
    merged = merged_2(local_parts, "seq", merge_partials)
    own_total = lax.dynamic_slice_in_dim(merged[1], seq_rank * local_requests, local_requests, 0)
    own_output = lax.dynamic_slice_in_dim(merged[2], seq_rank * local_requests, local_requests, 0)
    attended = (
        (own_output / own_total[..., None])
        .astype(jnp.bfloat16)
        .reshape(local_requests * steps, local_heads * HD)
    )
    head_terms = jnp.dot(attended, out_weight, preferred_element_type=jnp.float32)
    residual = flat + lax.psum(head_terms, "exp")
    ffn_in = rms_scale(residual, ffn_gain).astype(jnp.bfloat16)
    shared_inner = (
        jax.nn.silu(jnp.dot(ffn_in, gate_shared, preferred_element_type=jnp.float32))
        * jnp.dot(ffn_in, up_shared, preferred_element_type=jnp.float32)
    ).astype(jnp.bfloat16)
    shared_term = jnp.dot(shared_inner, down_shared, preferred_element_type=jnp.float32)
    dispatch, weighting = route_tables(expert_ids, expert_weights, CAP)
    outgoing = jnp.dot(
        dispatch.astype(jnp.bfloat16), ffn_in, preferred_element_type=jnp.float32
    ).astype(jnp.bfloat16)
    outgoing = outgoing.reshape(seq_count, gate_experts.shape[0], CAP, width)
    column_width = width // exp_count
    residual_cols = lax.dynamic_slice_in_dim(residual, exp_rank * column_width, column_width, 1)
    slot_rows = lax.all_to_all(outgoing, "seq", split_axis=0, concat_axis=0, tiled=True)
    gate_values = jnp.einsum(
        "sekd,edf->sekf", slot_rows, gate_experts, preferred_element_type=jnp.float32
    )
    up_values = jnp.einsum(
        "sekd,edf->sekf", slot_rows, up_experts, preferred_element_type=jnp.float32
    )
    inner = (jax.nn.silu(gate_values) * up_values).astype(jnp.bfloat16)
    returned = lax.all_to_all(
        jnp.einsum(
            "sekf,efd->sekd", inner, down_experts, preferred_element_type=jnp.float32
        ).astype(jnp.bfloat16),
        "seq",
        split_axis=0,
        concat_axis=0,
        tiled=True,
    ).astype(jnp.float32)
    routed = jnp.dot(weighting, returned.reshape(-1, width), precision=lax.Precision.HIGHEST)
    output_cols = residual_cols + lax.psum_scatter(
        (routed + shared_term).astype(jnp.bfloat16), "exp", scatter_dimension=1, tiled=True
    ).astype(jnp.float32)
    return (output_cols.reshape(local_requests, steps, column_width), key_out, value_out)


def solution(mesh):
    in_specs = (
        P("seq", None, None),
        P(),
        P("seq"),
        P("seq"),
        P("seq", None, "exp"),
        P("seq", None, "exp"),
        P(),
        P(None, "exp"),
        P(None, "exp"),
        P(None, "exp"),
        P("exp", None),
        P(),
        P("seq", None, None),
        P("seq", None, None),
        P("seq", None, "exp"),
        P("seq", None, "exp"),
        P("seq", "exp", None),
        P(None, "exp"),
        P(None, "exp"),
        P("exp", None),
    )
    out_specs = (P("seq", None, "exp"), P("seq", None, "exp"), P("seq", None, "exp"))
    return jax.shard_map(body, mesh=mesh, in_specs=in_specs, out_specs=out_specs, check_vma=False)
```

profile of v0, /device:TPU:1, one launch (start us, length us, event | category | flops | bytes accessed | tf_op | source)
XLA Modules:
  0.0 284.2 jit_solution(13367473993264623797)
XLA Ops:
  13.2 3.9 %copy.195 = bf16[512,2048]{1,0:T(8,128)(2,1)} copy(bf16[512,2048]{0,1:T(8,128)(2,1)} %bitcast.139) | data formatting | bytes 4194304 | tf_op jit(solution)/shard_map/dot_general | solution.py:154
  17.1 3.9 %copy.194 = bf16[512,2048]{1,0:T(8,128)(2,1)} copy(bf16[512,2048]{0,1:T(8,128)(2,1)} %bitcast.140) | data formatting | bytes 4194304 | tf_op jit(solution)/shard_map/dot_general | solution.py:162
  21.1 2.2 fusion.87
  23.3 2.3 fusion.89
  26.6 10.6 %all-gather.3 = bf16[8,12,512]{2,1,0:T(8,128)(2,1)S(1)} all-gather(bf16[1,12,512]{2,1,0:T(8,128)(2,1)S(1)} %reshape.536), channel_id=1, replica_groups=mesh['seq'=8,'exp'=4] {'seq'}, dimensions={0}, use_global_device_ids=true | all-gather | bytes 110592 | tf_op jit(solution)/shard_map/all_gather | solution.py:175
  39.3 2.0 fusion.48
  41.4 9.2 %all-gather.5 = bf16[8,12,512]{2,1,0:T(8,128)(2,1)S(1)} all-gather(bf16[1,12,512]{2,1,0:T(8,128)(2,1)S(1)} %fusion.48), channel_id=1, replica_groups=mesh['seq'=8,'exp'=4] {'seq'}, dimensions={0}, use_global_device_ids=true | all-gather | bytes 110592 | tf_op jit(solution)/shard_map/all_gather | solution.py:176
  62.7 8.4 %all-gather.4 = bf16[8,12,512]{2,1,0:T(8,128)(2,1)S(1)} all-gather(bf16[1,12,512]{2,1,0:T(8,128)(2,1)S(1)} %reshape.538), channel_id=1, replica_groups=mesh['seq'=8,'exp'=4] {'seq'}, dimensions={0}, use_global_device_ids=true | all-gather | bytes 110592 | tf_op jit(solution)/shard_map/all_gather | solution.py:174
  73.6 7.7 %select_select_fusion = (bf16[46,128,512]{2,1,0:T(8,128)(2,1)}, bf16[46,128,512]{2,1,0:T(8,128)(2,1)S(1)}) fusion(bf16[46,128,512]{2,1,0:T(8,128)(2,1)} %param.27, pred[46,128]{1,0:T(8,128)(4,1)} %get-tuple-element.259, pred[46,128]{1,0:T(8,128)(4,1)} %get-tuple-element.260, pred[46,128]{1,0:T(8,128)(4,1)} %get-tuple-element.261, ...), kind=kLoop, calls=%fused_computation.33 | loop fusion | flops 24117248 | bytes 24517632 | tf_op jit(solution)/shard_map/jit(_where)/select_n | solution.py:47
  81.4 2.6 copy-done.3
  84.0 3.4 %select_reduce_fusion = (f32[46,4,4]{1,2,0:T(4,128)S(1)}, f32[46,4,4,128]{3,1,2,0:T(4,128)S(1)}) fusion(pred[46,4,128]{2,1,0:T(4,128)(4,1)S(1)} %compare_and_fusion, bf16[46,4,4,128]{3,2,1,0:T(4,128)(2,1)S(1)} %copy-done.5, bf16[46,128,512]{2,1,0:T(8,128)(2,1)S(1)} %get-tuple-element.253), kind=kOutput, calls=%fused_computation.57 | convolution fusion | flops 24399136 | bytes 6621056 | tf_op jit(solution)/shard_map/pthd,pkhd->pthk/dot_general | solution.py:59
  87.6 1.9 fusion.60
  97.2 4.4 %fusion.32 = f32[46,4,4,128]{3,1,2,0:T(4,128)S(1)} fusion(f32[46,4,4,128]{3,1,2,0:T(4,128)S(1)} %get-tuple-element.267, f32[46,4,4]{1,2,0:T(4,128)} %copy.174, f32[46,4,4]{1,2,0:T(4,128)S(1)} %copy.167, pred[46,4,128]{2,1,0:T(4,128)(4,1)} %copy-done.6, bf16[46,128,512]{2,1,0:T(8,128)(2,1)} %get-tuple-element.252), kind=kOutput, calls=%fused_computation.43 | convolution fusion | flops 24494080 | bytes 6812416 | tf_op jit(solution)/shard_map/pthk,pkhd->pthd/dot_general | solution.py:71
  104.3 9.6 %all-gather.1 = f32[192,4,4]{2,1,0:T(4,128)S(1)} all-gather(f32[24,4,4]{2,1,0:T(4,128)S(1)} %copy.172), channel_id=3, replica_groups=mesh['seq'=8,'exp'=4] {'seq'}, dimensions={0}, use_global_device_ids=true | all-gather | bytes 13824 | tf_op jit(solution)/shard_map/all_gather | solution.py:14
  114.9 8.6 %all-gather = f32[192,4,4]{2,1,0:T(4,128)S(1)} all-gather(f32[24,4,4]{2,1,0:T(4,128)S(1)} %copy.164), channel_id=2, replica_groups=mesh['seq'=8,'exp'=4] {'seq'}, dimensions={0}, use_global_device_ids=true | all-gather | bytes 13824 | tf_op jit(solution)/shard_map/all_gather | solution.py:14
  126.2 3.2 %all-gather.8.cloned.1.call-done = f32[192,4,4,128]{3,0,2,1:T(8,128)} async-done(((f32[24,4,4,128]{3,0,2,1:T(8,128)}), f32[192,4,4,128]{3,0,2,1:T(8,128)}) %all-gather.8.cloned.1.call-update) | async-done | bytes 1572880 | tf_op jit(solution)/shard_map/all_gather | solution.py:14
  130.4 17.8 %while.19 = (s32[]{:T(128)}, f32[24,4,4]{0,2,1:T(4,128)S(1)}, f32[24,4,4]{0,2,1:T(4,128)S(1)}, f32[24,4,4,128]{3,2,1,0:T(4,128)S(1)}, f32[8,24,4,4]{1,3,2,0:T(4,...) while((s32[]{:T(128)}, f32[24,4,4]{0,2,1:T(4,128)S(1)}, ...), condition=%wide.region_5.6_spmd, body=%wide.region_4.5_spmd.sunk | while | flops 149765 | bytes 1004695 | solution.py:20
  148.6 2.6 fusion.93
  151.3 31.9 %all-reduce.6.cloned.1.call-done = f32[12,2048]{1,0:T(8,128)} async-done(((f32[12,2048]{1,0:T(8,128)}), f32[12,2048]{1,0:T(8,128)}) %all-reduce.6.cloned.1.call-update) | async-done | bytes 98320 | tf_op jit(solution)/shard_map/psum | solution.py:204
  185.7 3.3 %reshape.434 = bf16[8,8,3,2048]{3,2,1,0:T(4,128)(2,1)} reshape(bf16[192,2048]{1,0:T(8,128)(2,1)} %convolution_convert_fusion) | data formatting | bytes 1572864 | tf_op jit(solution)/shard_map/reshape | solution.py:215
  189.0 1.8 copy.184
  190.8 17.4 %all_to_all.10 = bf16[8,8,3,2048]{3,1,2,0:T(8,128)(2,1)S(1)} all-to-all(bf16[8,8,3,2048]{3,1,2,0:T(8,128)(2,1)S(1)} %copy.184), channel_id=1, replica_groups=mesh['seq'=8,'exp'=4] {'seq'}, dimensions={0} | all-to-all | bytes 1572864 | tf_op jit(solution)/shard_map/all_to_all | solution.py:218
  209.1 7.4 %fusion.26 = f32[8,8,3,352]{3,0,2,1:T(8,128)S(1)} fusion(bf16[8,2048,352]{1,2,0:T(8,128)(2,1)} %param.36, bf16[8,8,3,2048]{3,1,2,0:T(8,128)(2,1)S(1)} %all_to_all.10), kind=kOutput, calls=%fused_computation.41 | convolution fusion | flops 276824064 | bytes 12591104 | tf_op jit(solution)/shard_map/sekd,edf->sekf/dot_general | solution.py:219
  216.5 13.4 %fusion.19 = bf16[8,8,3,2048]{3,0,2,1:T(8,128)(2,1)} fusion(bf16[8,352,2048]{2,1,0:T(8,128)(2,1)} %param.38, bf16[8,2048,352]{1,2,0:T(8,128)(2,1)} %param.37, bf16[8,8,3,2048]{3,1,2,0:T(8,128)(2,1)} %copy-done.2, f32[8,8,3,352]{3,0,2,1:T(8,128)S(1)} %fusion.26), kind=kOutput, calls=%fused_computation.37 | convolution fusion | flops 554446848 | bytes 24911872 | tf_op jit(solution)/shard_map/sekf,efd->sekd/dot_general | solution.py:227
  229.9 2.5 copy.187
  232.4 5.4 %all-to-all-start.1 = ((bf16[8,8,3,2048]{3,1,2,0:T(8,128)(2,1)}), bf16[8,8,3,2048]{3,1,2,0:T(8,128)(2,1)}, u32[]{:S(2)}, u32[]{:S(2)}) async-start(bf16[8,8,3,2048]{3,1,2,0:T(8,128)(2,1)} %copy.187), calls=%async_computation.1 | async-start | bytes 1572864 | tf_op jit(solution)/shard_map/all_to_all | solution.py:226
  238.0 2.7 fusion.95
  240.6 6.3 %all-to-all-done.1 = bf16[8,8,3,2048]{3,1,2,0:T(8,128)(2,1)} async-done(((bf16[8,8,3,2048]{3,1,2,0:T(8,128)(2,1)}), bf16[8,8,3,2048]{3,1,2,0:T(8,128)(2,1)}, u32[]{:S(2)}, u32[]{:S(2)}) %all-to-all-start.1) | async-done | bytes 786464 | tf_op jit(solution)/shard_map/all_to_all | solution.py:226
  246.9 2.8 copy.188
  249.7 3.2 %reshape.435 = bf16[192,2048]{1,0:T(8,128)(2,1)} reshape(bf16[8,8,3,2048]{3,2,1,0:T(4,128)(2,1)} %copy.188) | data formatting | bytes 1572864 | tf_op jit(solution)/shard_map/reshape | solution.py:235
  254.4 4.1 %fusion.22 = bf16[12,2048]{1,0:T(8,128)(2,1)} fusion(f32[12,2048]{1,0:T(8,128)S(1)} %fusion.94, bf16[704,2048]{1,0:T(8,128)(2,1)S(1)} %copy-done, bf16[12,2048]{1,0:T(8,128)(2,1)S(1)} %multiply_convert_fusion, bf16[2048,704]{0,1:T(8,128)(2,1)} %param.40, f32[12,704]{1,0:T(8,128)S(1)} %fusion.95), kind=kOutput, calls=%fused_computation.39 | convolution fusion | flops 69305856 | bytes 5997568 | tf_op jit(solution)/shard_map/dot_general | solution.py:210
  258.6 17.8 %reduce-scatter.2.cloned.1.call-done = bf16[12,512]{1,0:T(8,128)(2,1)} async-done(((bf16[12,2048]{1,0:T(8,128)(2,1)}), bf16[12,512]{1,0:T(8,128)(2,1)}) %reduce-scatter.2.cloned.1.call-update) | async-done | bytes 12304 | tf_op jit(solution)/shard_map/reduce_scatter | solution.py:236
  (145 shorter events, 63.6 us)
Async XLA Ops:
  7.2 247.2 %copy-start = (bf16[704,2048]{1,0:T(8,128)(2,1)S(1)}, bf16[704,2048]{1,0:T(8,128)(2,1)}, u32[]{:S(2)}) copy-start(bf16[704,2048]{1,0:T(8,128)(2,1)} %param.41) | copy-start | bytes 8650756
  7.2 13.9 %copy-start.4 = (f32[3,4,2048]{2,1,0:T(4,128)S(1)}, f32[3,4,2048]{2,1,0:T(4,128)}, u32[]{:S(2)}) copy-start(f32[3,4,2048]{2,1,0:T(4,128)} %param.22) | copy-start | bytes 294916
  7.2 13.9 %copy-start.7 = (f32[2048]{0:T(1024)S(1)}, f32[2048]{0:T(1024)}, u32[]{:S(2)}) copy-start(f32[2048]{0:T(1024)} %param.28) | copy-start | bytes 24580
  7.2 122.2 %all-gather.8.cloned.1.call-start = ((), (), s32[]{:S(2)}) async-start(), calls=%async_computation.5 | async-start | bytes 1769472 | tf_op jit(solution)/shard_map/all_gather | solution.py:14
  21.0 37.4 %copy-start.1 = (s32[24]{0:T(128)S(1)}, s32[24]{0:T(128)}, u32[]{:S(2)}) copy-start(s32[24]{0:T(128)} %param.23) | copy-start | bytes 292
  26.5 36.1 %copy-start.8 = (bf16[3,4,4,128]{3,1,2,0:T(4,128)(2,1)S(1)}, bf16[3,4,4,128]{3,1,2,0:T(4,128)(2,1)}, u32[]{:S(2)}) copy-start(bf16[3,4,4,128]{3,1,2,0:T(4,128)(2,1)} %get-tuple-element.269) | copy-start | bytes 36868
  73.6 7.8 %copy-start.6 = (pred[46,4,128]{2,1,0:T(4,128)(4,1)}, pred[46,4,128]{2,1,0:T(4,128)(4,1)S(1)}, u32[]{:S(2)}) copy-start(pred[46,4,128]{2,1,0:T(4,128)(4,1)S(1)} %compare_and_fusion) | copy-start | bytes 70660
  73.6 10.4 %copy-start.5 = (bf16[46,4,4,128]{3,2,1,0:T(4,128)(2,1)S(1)}, bf16[46,4,4,128]{3,2,1,0:T(4,128)(2,1)}, u32[]{:S(2)}) copy-start(bf16[46,4,4,128]{3,2,1,0:T(4,128)(2,1)} %gather_fusion.5) | copy-start | bytes 565252
  81.4 2.6 copy-start.3
  81.4 9.7 %copy-start.10 = (pred[46]{0:T(512)(128)(4,1)S(1)}, pred[46]{0:T(512)(128)(4,1)}, u32[]{:S(2)}) copy-start(pred[46]{0:T(512)(128)(4,1)} %broadcast_compare_fusion) | copy-start | bytes 142
  95.7 7.7 %copy-start.9 = (f32[46,4,4]{0,2,1:T(4,128)S(1)}, f32[46,4,4]{0,2,1:T(4,128)}, u32[]{:S(2)}) copy-start(f32[46,4,4]{0,2,1:T(4,128)} %get-tuple-element.244) | copy-start | bytes 8836
  103.3 79.9 %all-reduce.6.cloned.1.call-start = ((), (), s32[]{:S(2)}) async-start(), calls=%async_computation.3 | async-start | bytes 262144 | tf_op jit(solution)/shard_map/psum | solution.py:204
  113.9 70.4 %copy-start.11 = (f32[2048]{0:T(1024)S(1)}, f32[2048]{0:T(1024)}, u32[]{:S(2)}) copy-start(f32[2048]{0:T(1024)} %param.33) | copy-start | bytes 24580
  208.2 0.9 copy-start.2
  216.5 21.3 %copy-start.12 = (f32[3,4,6]{2,1,0:T(4,128)S(1)}, f32[3,4,6]{2,1,0:T(4,128)}, u32[]{:S(2)}) copy-start(f32[3,4,6]{2,1,0:T(4,128)} %param.35) | copy-start | bytes 868
  232.4 14.5 %all-to-all-start.1 = ((bf16[8,8,3,2048]{3,1,2,0:T(8,128)(2,1)}), bf16[8,8,3,2048]{3,1,2,0:T(8,128)(2,1)}, u32[]{:S(2)}, u32[]{:S(2)}) async-start(bf16[8,8,3,2048]{3,1,2,0:T(8,128)(2,1)} %copy.187), calls=%async_computation.1 | async-start | bytes 1572864 | tf_op jit(solution)/shard_map/all_to_all | solution.py:226
  237.8 38.5 %reduce-scatter.2.cloned.1.call-start = ((), (), s32[]{:S(2)}) async-start(), calls=%async_computation.4 | async-start | bytes 81920 | tf_op jit(solution)/shard_map/reduce_scatter | solution.py:236
Sparse Core Ops, SparseCore 0:
  103.5 25.9 all-gather.7
  151.3 31.8 all-reduce.5
  258.7 17.6 reduce-scatter.1
where the time goes:
time: 289 us; the launch traced here: 284 us
  blocking collectives  63.8 us (22%)
  waiting for transfers between devices  59.2 us (20%)
  local copies, waits for them, and re-layouts  57.9 us (20%)
  matrix products  49.9 us (17%)
  other arithmetic  33.7 us (12%)
  between operations  14 us (5%)
  starting transfers between devices  5.5 us (2%)
    psum x1, waiting for transfers between devices, body(): residual = flat + lax.psum(head_terms, 'exp')  31.9 us
    all_gather x2, blocking collectives, merged_2(): everything = jax.tree.map(lambda part: lax.all_gather(part, axis), array)  18.2 us
    reduce_scatter x1, waiting for transfers between devices, body(): lax.psum_scatter((routed + shared_term).astype(jnp.bfloat16), 'exp', scat...  17.8 us
    all_to_all x1, blocking collectives, body(): lax.all_to_all(outgoing, 'seq', split_axis=0, concat_axis=0, tiled=True)  17.4 us
    dot_general x1, matrix products, body(): jnp.einsum('sekf,efd->sekd', inner, down_experts, preferred_element_type=...  13.4 us
    all_gather x1, blocking collectives, body(): lax.all_gather(key_local, 'seq', axis=0, tiled=True)  10.6 us
    gather x8, local copies, waits for them, and re-layouts, append_rows(): new_rows[slot_req, step_index][:, None, :]  9.97 us
    all_gather x1, blocking collectives, body(): lax.all_gather(value_local, 'seq', axis=0, tiled=True)  9.19 us
  transfers between devices with their start and end apart: 4, of which 4 were waited for; matrix products, arithmetic and copies ran while one was open for 3% of the time, Pallas kernels for 0%

commit v1 on v0

v1 whole, which is shorter than its diff:
```python
import functools
import math

import jax
import jax.numpy as jnp
import numpy as np
from jax import lax
from jax.experimental import pallas as pl
from jax.experimental.pallas import tpu as pltpu
from jax.sharding import PartitionSpec as P

HD = 128
EXPERTS = 64
GROUP = 16
CHUNK = 8
NEG = -1e30
MIB = 1 << 20
F32 = jnp.float32
BF16 = jnp.bfloat16


def vmem():
    return pl.BlockSpec(memory_space=pltpu.VMEM)


def smem():
    return pl.BlockSpec(memory_space=pltpu.SMEM)


def hbm():
    return pl.BlockSpec(memory_space=pl.ANY)


def dot_nt(a, b):
    return lax.dot_general(a, b, (((1,), (1,)), ((), ())), preferred_element_type=F32)


def dot_nn(a, b):
    return jnp.dot(a, b, preferred_element_type=F32)


def iota(shape, dim):
    return lax.broadcasted_iota(jnp.int32, shape, dim)


def norm_kernel(hidden_ref, gain_ref, out_ref, rows_ref):
    local, steps, _ = hidden_ref.shape
    rows_ref[...] = jnp.zeros_like(rows_ref)
    for j in range(local):
        rows_ref[pl.ds(j * steps, steps), :] = hidden_ref[j]
    rows = rows_ref[...]
    mean_square = jnp.mean(rows * rows, axis=-1, keepdims=True)
    out_ref[...] = (rows * lax.rsqrt(mean_square + 1e-06) * gain_ref[...]).astype(BF16)


def norm_rows(hidden, gain):
    width = hidden.shape[2]
    return pl.pallas_call(
        norm_kernel,
        out_shape=jax.ShapeDtypeStruct((GROUP, width), BF16),
        in_specs=[vmem(), vmem()],
        out_specs=vmem(),
        scratch_shapes=[pltpu.VMEM((GROUP, width), F32)],
        compiler_params=pltpu.CompilerParams(vmem_limit_bytes=4 * MIB),
        name="norm_rows",
    )(hidden, gain.reshape(1, width))


def rotated(full, cosine, sine):
    heads = full.shape[1] // HD
    parts = []
    for h in range(heads):
        one = full[:, h * HD : (h + 1) * HD]
        parts.append(one * cosine + pltpu.roll(one, HD // 2, 1) * sine)
    return jnp.concatenate(parts, axis=1)


def attention_kernel(
    local,
    steps,
    lens_ref,
    slot_req_ref,
    slot_block_ref,
    rows_ref,
    cos_ref,
    sin_ref,
    query_hbm,
    key_hbm,
    value_hbm,
    key_in,
    value_in,
    part_ref,
    key_out,
    value_out,
    weights,
    key_buf,
    value_buf,
    spread,
    new_keys,
    new_values,
    slot_max,
    slot_total,
    slot_out,
    req_max,
    req_total,
    req_out,
    weight_sem,
    in_sem,
    out_sem,
):
    pool, block, width = key_buf.shape
    heads = width // HD
    per = heads * steps
    requests = req_max.shape[0]
    groups = requests // local
    chunks = [(c, min(c + CHUNK, pool)) for c in range(0, pool, CHUNK)]

    weight_copies = [
        pltpu.make_async_copy(src, weights.at[i], weight_sem.at[i])
        for i, src in enumerate((query_hbm, key_hbm, value_hbm))
    ]
    for copy in weight_copies:
        copy.start()

    def both(sources, targets, sems, i):
        low, high = chunks[i]
        return [
            pltpu.make_async_copy(
                src.at[pl.ds(low, high - low)], dst.at[pl.ds(low, high - low)], sems.at[n, i]
            )
            for n, (src, dst) in enumerate(zip(sources, targets))
        ]

    incoming = [both((key_in, value_in), (key_buf, value_buf), in_sem, i) for i in range(len(chunks))]
    outgoing = [both((key_buf, value_buf), (key_out, value_out), out_sem, i) for i in range(len(chunks))]
    for pair in incoming:
        for copy in pair:
            copy.start()

    rows = rows_ref[...]
    cosine = cos_ref[...]
    sine = sin_ref[...]
    weight_copies[0].wait()
    queries = rotated(dot_nn(rows, weights[0]), cosine, sine).astype(BF16)
    picked = iota((requests * per, rows.shape[0]), 0)
    request, inside = picked // per, picked % per
    source = request // local * GROUP + request % local * steps + inside % steps
    choose = (source == iota(picked.shape, 1)).astype(BF16)
    wide = dot_nn(choose, queries)
    head_of = iota(wide.shape, 0) % per // steps
    spread[...] = (
        jnp.where(head_of == iota(wide.shape, 1) // HD, wide, 0.0)
        .astype(BF16)
        .reshape(requests, per, width)
    )
    weight_copies[1].wait()
    new_keys[...] = rotated(dot_nn(rows, weights[1]), cosine, sine).astype(BF16).astype(F32)
    weight_copies[2].wait()
    new_values[...] = dot_nn(rows, weights[2]).astype(BF16).astype(F32)

    row_step = iota((per, block), 0) % steps
    position = iota((per, block), 1)
    scale = 1.0 / math.sqrt(HD)
    patch_rows = iota((16, width), 0)

    def slot_facts(s):
        wanted = slot_req_ref[s]
        request = jnp.maximum(wanted, 0)
        base = lens_ref[request] - slot_block_ref[s] * block
        return request, jnp.where(wanted >= 0, base, -4 * block)

    def patch(s, carry):
        request, base = slot_facts(s)

        @pl.when((base > -steps) & (base < block))
        def _():
            first = request // local * GROUP + request % local * steps
            for t in range(steps):
                row = base + t

                @pl.when((row >= 0) & (row < block))
                def _():
                    start = pl.multiple_of(row // 16 * 16, 16)
                    hit = patch_rows == row - start
                    for buf, new in ((key_buf, new_keys), (value_buf, new_values)):
                        old = buf[s, pl.ds(start, 16), :].astype(F32)
                        fresh = new[pl.ds(first + t, 1), :]
                        buf[s, pl.ds(start, 16), :] = jnp.where(hit, fresh, old).astype(BF16)

        return carry

    for i, (low, high) in enumerate(chunks):
        for copy in incoming[i]:
            copy.wait()
        lax.fori_loop(low, high, patch, 0)
        for copy in outgoing[i]:
            copy.start()
        for s in range(low, high):
            request, base = slot_facts(s)
            scores = dot_nt(spread[request], key_buf[s]) * scale
            allowed = position - row_step <= base
            scores = jnp.where(allowed, scores, NEG)
            top = jnp.max(scores, axis=-1, keepdims=True)
            weight = jnp.where(allowed, jnp.exp(scores - top), 0.0)
            total = jnp.sum(weight, axis=-1, keepdims=True)
            mixed = dot_nn(weight.astype(BF16), value_buf[s])
            result = mixed[:, :HD]
            lane_head = iota((per, HD), 0) // steps
            for h in range(1, heads):
                result = jnp.where(lane_head == h, mixed[:, h * HD : (h + 1) * HD], result)
            slot_max[s] = jnp.broadcast_to(top, (per, HD))
            slot_total[s] = jnp.broadcast_to(total, (per, HD))
            slot_out[s] = result

    req_max[...] = jnp.full_like(req_max, NEG)
    req_total[...] = jnp.zeros_like(req_total)
    req_out[...] = jnp.zeros_like(req_out)

    def find_max(s, carry):
        request = jnp.maximum(slot_req_ref[s], 0)
        req_max[request] = jnp.maximum(req_max[request], slot_max[s])
        return carry

    lax.fori_loop(0, pool, find_max, 0)

    def add_up(s, carry):
        request = jnp.maximum(slot_req_ref[s], 0)
        factor = jnp.exp(slot_max[s] - req_max[request])
        req_total[request] = req_total[request] + factor * slot_total[s]
        req_out[request] = req_out[request] + factor * slot_out[s]
        return carry

    lax.fori_loop(0, pool, add_up, 0)

    total = req_total[...]
    some = total > 0.0
    safe = jnp.where(some, total, 1.0)
    mean = jnp.where(some, req_out[...] / safe, 0.0).astype(BF16)
    level = jnp.where(some, req_max[...] + jnp.log(safe), NEG)
    high = level.astype(BF16).astype(F32)
    middle = (level - high).astype(BF16).astype(F32)
    low_part = (level - high - middle).astype(BF16).astype(F32)
    row = iota(level.shape, 1)
    lane = iota(level.shape, 2)
    packed = jnp.where(lane == row, high, 0.0)
    packed = packed + jnp.where(lane == row + per, middle, 0.0)
    packed = packed + jnp.where(lane == row + 2 * per, low_part, 0.0)
    packed = jnp.sum(packed, axis=1, keepdims=True)
    block_row = iota((16, HD), 0)
    for g in range(groups):
        levels = jnp.zeros((16, HD), F32)
        for j in range(local):
            b = g * local + j
            part_ref[g, pl.ds(j * per, per), :] = mean[b]
            levels = jnp.where(block_row == j, packed[b], levels)
        part_ref[g, pl.ds(local * per, 16), :] = levels.astype(BF16)
    for pair in outgoing:
        for copy in pair:
            copy.wait()


def attention(rows, cosine, sine, weights, caches, lens, slot_req, slot_block, local, steps):
    pool, block, width = caches[0].shape
    model = rows.shape[1]
    requests = lens.shape[0]
    per = width // HD * steps
    chunk_count = -(-pool // CHUNK)
    cache_shape = jax.ShapeDtypeStruct(caches[0].shape, BF16)
    return pl.pallas_call(
        functools.partial(attention_kernel, local, steps),
        out_shape=(
            jax.ShapeDtypeStruct((requests // local, local * per + 16, HD), BF16),
            cache_shape,
            cache_shape,
        ),
        in_specs=[smem()] * 3 + [vmem()] * 3 + [hbm()] * 5,
        out_specs=(vmem(), hbm(), hbm()),
        scratch_shapes=[
            pltpu.VMEM((3, model, width), BF16),
            pltpu.VMEM((pool, block, width), BF16),
            pltpu.VMEM((pool, block, width), BF16),
            pltpu.VMEM((requests, per, width), BF16),
            pltpu.VMEM((rows.shape[0], width), F32),
            pltpu.VMEM((rows.shape[0], width), F32),
            pltpu.VMEM((pool, per, HD), F32),
            pltpu.VMEM((pool, per, HD), F32),
            pltpu.VMEM((pool, per, HD), F32),
            pltpu.VMEM((requests, per, HD), F32),
            pltpu.VMEM((requests, per, HD), F32),
            pltpu.VMEM((requests, per, HD), F32),
            pltpu.SemaphoreType.DMA((3,)),
            pltpu.SemaphoreType.DMA((2, chunk_count)),
            pltpu.SemaphoreType.DMA((2, chunk_count)),
        ],
        compiler_params=pltpu.CompilerParams(vmem_limit_bytes=36 * MIB),
        name="attention",
    )(lens, slot_req, slot_block, rows, cosine, sine, *weights, *caches)


def merge_kernel(local, steps, part_ref, weight_ref, out_ref):
    holders = part_ref.shape[0]
    width = weight_ref.shape[0]
    heads = width // HD
    per = heads * steps
    count = local * per
    values = [part_ref[g, pl.ds(0, count), :].astype(F32) for g in range(holders)]
    row = iota((count, HD), 0)
    lane = iota((count, HD), 1)
    mine = (lane % per == row % per) & (lane < 3 * per)
    levels = []
    for g in range(holders):
        stat = part_ref[g, pl.ds(count, 16), :].astype(F32)
        wide = jnp.concatenate(
            [jnp.broadcast_to(stat[j : j + 1], (per, HD)) for j in range(local)], axis=0
        )
        levels.append(jnp.sum(jnp.where(mine, wide, 0.0), axis=-1, keepdims=True))
    top = functools.reduce(jnp.maximum, levels)
    shares = [jnp.exp(level - top) for level in levels]
    total = sum(shares)
    mixed = sum(share * value for share, value in zip(shares, values))
    attended = (mixed / total).astype(BF16)
    target = iota((GROUP, count), 0)
    source = iota((GROUP, count), 1)
    parts = []
    for h in range(heads):
        pick = (source == target // steps * per + h * steps + target % steps) & (
            target < local * steps
        )
        parts.append(dot_nn(pick.astype(BF16), attended).astype(BF16))
    out_ref[...] = dot_nn(jnp.concatenate(parts, axis=1), weight_ref[...]).astype(BF16)


def merge_project(parts, out_weight, local, steps):
    return pl.pallas_call(
        functools.partial(merge_kernel, local, steps),
        out_shape=jax.ShapeDtypeStruct((GROUP, out_weight.shape[1]), BF16),
        in_specs=[vmem(), vmem()],
        out_specs=vmem(),
        compiler_params=pltpu.CompilerParams(vmem_limit_bytes=8 * MIB),
        name="merge_project",
    )(parts, out_weight)


def second_norm_kernel(hidden_ref, left_ref, right_ref, gain_ref, ids_ref, gates_ref, rows_out, res_out, rows_ref):
    local, steps, width = hidden_ref.shape
    rows_ref[...] = jnp.zeros_like(rows_ref)
    for j in range(local):
        rows_ref[pl.ds(j * steps, steps), :] = hidden_ref[j]
    residual = rows_ref[...] + (left_ref[...].astype(F32) + right_ref[...].astype(F32))
    res_out[...] = residual
    mean_square = jnp.mean(residual * residual, axis=-1, keepdims=True)
    normed = residual * lax.rsqrt(mean_square + 1e-06) * gain_ref[...]
    rows_out[:, pl.ds(0, width)] = normed.astype(BF16)
    rows_ref[:, pl.ds(0, HD)] = jnp.zeros((GROUP, HD), F32)
    lane = iota((steps, HD), 1)
    for j in range(local):
        table = jnp.zeros((steps, HD), F32)
        for k in range(ids_ref.shape[2]):
            hit = lane % EXPERTS == ids_ref[j, :, k : k + 1]
            table = table + jnp.where(hit, gates_ref[j, :, k : k + 1], 0.0)
        rows_ref[pl.ds(j * steps, steps), pl.ds(0, HD)] = table
    table = rows_ref[:, pl.ds(0, HD)]
    high = table.astype(BF16)
    low = (table - high.astype(F32)).astype(BF16)
    rows_out[:, pl.ds(width, HD)] = jnp.where(iota((GROUP, HD), 1) < EXPERTS, high.astype(F32), low.astype(F32)).astype(BF16)


def second_norm(hidden, left, right, gain, ids, gates):
    width = hidden.shape[2]
    return pl.pallas_call(
        second_norm_kernel,
        out_shape=(
            jax.ShapeDtypeStruct((GROUP, width + HD), BF16),
            jax.ShapeDtypeStruct((GROUP, width), F32),
        ),
        in_specs=[vmem()] * 6,
        out_specs=(vmem(), vmem()),
        scratch_shapes=[pltpu.VMEM((GROUP, width), F32)],
        compiler_params=pltpu.CompilerParams(vmem_limit_bytes=4 * MIB),
        name="second_norm",
    )(hidden, left, right, gain.reshape(1, width), ids, gates)


def shared_kernel(rows_ref, gate_ref, up_ref, down_ref, out_ref):
    rows = rows_ref[:, pl.ds(0, down_ref.shape[1])]
    inner = jax.nn.silu(dot_nt(rows, gate_ref[...])) * dot_nt(rows, up_ref[...])
    out_ref[...] = dot_nn(inner.astype(BF16), down_ref[...])


def shared_experts(rows, gate, up, down):
    return pl.pallas_call(
        shared_kernel,
        out_shape=jax.ShapeDtypeStruct((GROUP, down.shape[1]), F32),
        in_specs=[vmem()] * 4,
        out_specs=vmem(),
        compiler_params=pltpu.CompilerParams(vmem_limit_bytes=16 * MIB),
        name="shared_experts",
    )(rows, gate, up, down)


def experts_kernel(tokens, place_ref, rows_ref, shared_ref, gate_ref, up_ref, down_ref, out_ref, total_ref):
    e = pl.program_id(0)
    count = pl.num_programs(0)
    width = down_ref.shape[2]
    seq_rank = place_ref[0]
    first = place_ref[1]

    @pl.when(e == 0)
    def _():
        total_ref[...] = jnp.zeros_like(total_ref)
        start = pl.multiple_of(seq_rank * GROUP, GROUP)
        total_ref[pl.ds(start, GROUP), :] = shared_ref[...]

    rows = rows_ref[:, pl.ds(0, width)]
    table = rows_ref[:, pl.ds(width, HD)].astype(F32)
    mine = iota(table.shape, 1) % EXPERTS == first + e
    share = jnp.sum(jnp.where(mine, table, 0.0), axis=-1, keepdims=True)
    gate = dot_nt(rows, gate_ref[0])
    up = dot_nt(rows, up_ref[0])
    inner = (jax.nn.silu(gate) * up * share).astype(BF16)
    total_ref[...] += dot_nn(inner, down_ref[0])

    @pl.when(e == count - 1)
    def _():
        groups = total_ref.shape[0] // GROUP
        pieces = out_ref.shape[0] // groups
        columns = width // pieces
        for g in range(groups):
            for p in range(pieces):
                out_ref[g * pieces + p] = total_ref[
                    pl.ds(g * GROUP, tokens), pl.ds(p * columns, columns)
                ].astype(BF16)


def routed_experts(place, rows, shared, gate, up, down, tokens, pieces):
    count, hidden, width = down.shape
    groups = rows.shape[0] // GROUP
    one = pl.BlockSpec((1, hidden, width), lambda e: (e, 0, 0))
    return pl.pallas_call(
        functools.partial(experts_kernel, tokens),
        grid=(count,),
        out_shape=jax.ShapeDtypeStruct((groups * pieces, tokens, width // pieces), BF16),
        in_specs=[smem(), vmem(), vmem(), one, one, one],
        out_specs=vmem(),
        scratch_shapes=[pltpu.VMEM((rows.shape[0], width), F32)],
        compiler_params=pltpu.CompilerParams(vmem_limit_bytes=24 * MIB),
        name="routed_experts",
    )(place, rows, shared, gate, up, down)


def last_kernel(rank_ref, res_ref, parts_ref, out_ref):
    local, steps, columns = out_ref.shape
    total = parts_ref[0].astype(F32)
    for i in range(1, parts_ref.shape[0]):
        total = total + parts_ref[i].astype(F32)
    start = pl.multiple_of(rank_ref[0] * columns, HD)
    total = total + res_ref[pl.ds(0, local * steps), pl.ds(start, columns)]
    for j in range(local):
        out_ref[j] = total[j * steps : (j + 1) * steps]


def last_sum(rank, residual, parts, local, steps):
    return pl.pallas_call(
        last_kernel,
        out_shape=jax.ShapeDtypeStruct((local, steps, parts.shape[2]), F32),
        in_specs=[smem(), vmem(), vmem()],
        out_specs=vmem(),
        compiler_params=pltpu.CompilerParams(vmem_limit_bytes=8 * MIB),
        name="last_sum",
    )(rank, residual, parts)


def partner(array, axis, bit):
    count = lax.axis_size(axis)
    return lax.ppermute(array, axis, [(i, i ^ bit) for i in range(count)])


def rotation_tables(lens, local, steps):
    half = HD // 2
    frequency = np.power(10000.0, -np.arange(half, dtype=np.float64) * (2.0 / HD)).astype(np.float32)
    both = jnp.asarray(np.concatenate([frequency, frequency]))
    sign = jnp.asarray(np.concatenate([-np.ones(half), np.ones(half)]).astype(np.float32))
    positions = lens.reshape(-1, local, 1) + jnp.arange(steps, dtype=jnp.int32)
    positions = positions.reshape(-1, local * steps)
    positions = jnp.pad(positions, ((0, 0), (0, GROUP - local * steps))).reshape(-1, 1)
    angles = positions.astype(F32) * both
    return jnp.cos(angles), jnp.sin(angles) * sign


def body(
    hidden_in,
    cache_lens,
    slot_request,
    slot_block,
    key_cache,
    value_cache,
    attn_gain,
    query_weight,
    key_weight,
    value_weight,
    out_weight,
    ffn_gain,
    expert_ids,
    expert_weights,
    gate_experts,
    up_experts,
    down_experts,
    gate_shared,
    up_shared,
    down_shared,
):
    local, steps, width = hidden_in.shape
    exp_count = lax.axis_size("exp")
    seq_rank = lax.axis_index("seq").astype(jnp.int32)
    exp_rank = lax.axis_index("exp").astype(jnp.int32)
    tokens = local * steps

    cosine, sine = rotation_tables(cache_lens, local, steps)
    normed = norm_rows(hidden_in, attn_gain)
    rows = lax.all_gather(normed, "seq", axis=0, tiled=True)
    parts, key_out, value_out = attention(
        rows,
        cosine,
        sine,
        (query_weight, key_weight, value_weight),
        (key_cache, value_cache),
        cache_lens,
        slot_request,
        slot_block,
        local,
        steps,
    )
    parts = lax.all_to_all(parts, "seq", split_axis=0, concat_axis=0, tiled=True)
    terms = merge_project(parts, out_weight, local, steps)
    other = partner(terms, "exp", 1)
    bit = 2
    while bit < exp_count:
        terms = (terms.astype(F32) + other.astype(F32)).astype(BF16)
        other = partner(terms, "exp", bit)
        bit *= 2
    ffn_in, residual = second_norm(
        hidden_in, terms, other, ffn_gain, expert_ids, expert_weights
    )
    shared = shared_experts(
        ffn_in, jnp.swapaxes(gate_shared, 0, 1), jnp.swapaxes(up_shared, 0, 1), down_shared
    )
    all_rows = lax.all_gather(ffn_in, "seq", axis=0, tiled=True)
    place = jnp.stack([seq_rank, seq_rank * gate_experts.shape[0]])
    sums = routed_experts(
        place,
        all_rows,
        shared,
        jnp.swapaxes(gate_experts, 1, 2),
        jnp.swapaxes(up_experts, 1, 2),
        down_experts,
        tokens,
        exp_count,
    )
    sums = lax.all_to_all(sums, ("seq", "exp"), split_axis=0, concat_axis=0, tiled=True)
    hidden_out = last_sum(exp_rank.reshape(1), residual, sums, local, steps)
    return hidden_out, key_out, value_out


def solution(mesh):
    in_specs = (
        P("seq", None, None),
        P(),
        P("seq"),
        P("seq"),
        P("seq", None, "exp"),
        P("seq", None, "exp"),
        P(),
        P(None, "exp"),
        P(None, "exp"),
        P(None, "exp"),
        P("exp", None),
        P(),
        P("seq", None, None),
        P("seq", None, None),
        P("seq", None, "exp"),
        P("seq", None, "exp"),
        P("seq", "exp", None),
        P(None, "exp"),
        P(None, "exp"),
        P("exp", None),
    )
    out_specs = (P("seq", None, "exp"), P("seq", None, "exp"), P("seq", None, "exp"))
    return jax.shard_map(body, mesh=mesh, in_specs=in_specs, out_specs=out_specs, check_vma=False)
```

time: 289 us -> 122 us (0.42); the launches traced: 284 us -> 122 us
  matrix products: 49.9 us -> 0 us
  waiting for transfers between devices: 59.2 us -> 18.7 us
  Pallas kernels: 0 us -> 37 us
  local copies, waits for them, and re-layouts: 57.9 us -> 24.3 us
  blocking collectives: 63.8 us -> 30.7 us
  other arithmetic: 33.7 us -> 1.09 us
  between operations: 14 us -> 0.74 us
  starting transfers between devices: 5.5 us -> 9.04 us
    dot_general x13 -> x0, matrix products: 49.1 us -> none  [the longest x1 13.4 us: body(): jnp.einsum('sekf,efd->sekd', inner, down_experts, preferred_element_type=...]
    pallas_call x0 -> x7, Pallas kernels: none -> 37 us  [the longest x1 19.4 us: attention(): pl.pallas_call(functools.partial(attention_kernel, local, steps), out_sha...]
    psum x1 -> x0, waiting for transfers between devices: 31.9 us -> none  [body(): residual = flat + lax.psum(head_terms, 'exp')]
    all_gather x5 -> x2, blocking collectives: 46.3 us -> 23.3 us  [the longest x1 12.1 us: body(): all_rows = lax.all_gather(ffn_in, 'seq', axis=0, tiled=True)]
    unnamed x30 -> x38, local copies, waits for them, and re-layouts: 3.58 us -> 23.3 us
    reduce_scatter x1 -> x0, waiting for transfers between devices: 17.8 us -> none  [body(): lax.psum_scatter((routed + shared_term).astype(jnp.bfloat16), 'exp', scat...]
    gather x12 -> x0, local copies, waits for them, and re-layouts: 14.8 us -> none  [the longest x8 9.97 us: append_rows(): new_rows[slot_req, step_index][:, None, :]]
    add x18 -> x1, other arithmetic: 11.6 us -> 0.01 us  [rotation_tables(): positions = lens.reshape(-1, local, 1) + jnp.arange(steps, dtype=jnp.int32)]
  transfers between devices with their start and end apart: 4 -> 3, of which waited for: 4 -> 3; matrix products, arithmetic and copies ran while one was open for 3% -> 0% of each run, Pallas kernels for 0% -> 0%
where the time goes in v1:
time: 122 us
  Pallas kernels  37 us (30%)
  blocking collectives  30.7 us (25%)
  local copies, waits for them, and re-layouts  24.3 us (20%)
  waiting for transfers between devices  18.7 us (15%)
  starting transfers between devices  9.04 us (7%)
    unnamed x38, local copies, waits for them, and re-layouts  23.3 us
    pallas_call x1, Pallas kernels, attention(): pl.pallas_call(functools.partial(attention_kernel, local, steps), out_sha...  19.4 us
    all_to_all x1, waiting for transfers between devices, body(): lax.all_to_all(sums, ('seq', 'exp'), split_axis=0, concat_axis=0, tiled=T...  15.3 us
    pallas_call x1, Pallas kernels, routed_experts(): pl.pallas_call(functools.partial(experts_kernel, tokens), grid=(count,),...  13.9 us
    all_gather x1, blocking collectives, body(): all_rows = lax.all_gather(ffn_in, 'seq', axis=0, tiled=True)  12.1 us
    all_gather x1, blocking collectives, body(): rows = lax.all_gather(normed, 'seq', axis=0, tiled=True)  11.2 us
    all_to_all x1, blocking collectives, body(): lax.all_to_all(parts, 'seq', split_axis=0, concat_axis=0, tiled=True)  7.45 us
    all_to_all x1, starting transfers between devices, body(): lax.all_to_all(sums, ('seq', 'exp'), split_axis=0, concat_axis=0, tiled=T...  5.36 us
  transfers between devices with their start and end apart: 3, of which 3 were waited for; matrix products, arithmetic and copies ran while one was open for 0% of the time, Pallas kernels for 0%

profile of v1, /device:TPU:1, one launch (start us, length us, event | category | flops | bytes accessed | tf_op | source)
XLA Modules:
  0.0 121.6 jit_solution(2942044691486335558)
XLA Ops:
  0.7 0.7 add.27
  1.5 0.1 copy.29
  1.7 0.9 copy-done.10
  2.6 0.7 copy-done.13
  3.3 0.1 norm_rows.1
  3.5 11.2 %all_gather.6.rows_ref = bf16[128,2048]{1,0:T(8,128)(2,1)S(1)} all-gather(bf16[16,2048]{1,0:T(8,128)(2,1)S(1)} %norm_rows.1), channel_id=1, replica_groups=mesh['seq'=8,'exp'=4] {'seq'}, dimensions={0}, use_global_device_ids=true | all-gather | bytes 589824 | tf_op jit(solution)/shard_map/all_gather | solution.py:520
  14.7 1.0 fusion
  15.7 2.7 %copy-done.2 = bf16[46,128,512]{2,1,0:T(8,128)(2,1)S(1)} copy-done((bf16[46,128,512]{2,1,0:T(8,128)(2,1)S(1)}, bf16[46,128,512]{2,1,0:T(8,128)(2,1)}, u32[]{:S(2)}) %copy-start.2) | copy-done | bytes 6029336
  18.4 1.6 %copy-done.7 = bf16[2048,512]{1,0:T(8,128)(2,1)S(1)} copy-done((bf16[2048,512]{1,0:T(8,128)(2,1)S(1)}, bf16[2048,512]{1,0:T(8,128)(2,1)}, u32[]{:S(2)}) %copy-start.7) | copy-done | bytes 2097176
  20.0 1.6 %copy-done.8 = bf16[2048,512]{1,0:T(8,128)(2,1)S(1)} copy-done((bf16[2048,512]{1,0:T(8,128)(2,1)S(1)}, bf16[2048,512]{1,0:T(8,128)(2,1)}, u32[]{:S(2)}) %copy-start.8) | copy-done | bytes 2097176
  21.6 1.6 %copy-done.9 = bf16[2048,512]{1,0:T(8,128)(2,1)S(1)} copy-done((bf16[2048,512]{1,0:T(8,128)(2,1)S(1)}, bf16[2048,512]{1,0:T(8,128)(2,1)}, u32[]{:S(2)}) %copy-start.9) | copy-done | bytes 2097176
  23.2 0.7 copy-done.16
  23.8 0.7 copy-done.17
  24.5 0.7 copy-done.18
  25.2 19.4 %attention.1 = (bf16[8,64,128]{2,1,0:T(8,128)(2,1)S(1)}, bf16[46,128,512]{2,1,0:T(8,128)(2,1)}, bf16[46,128,512]{2,1,0:T(8,128)(2,1)}) custom-call(s32[24]{0:T(128)S(1)} %copy-done.16, s32[46]{0:T(128)S(1)} %copy-done.17, s32[46]{0:T(128)S(1)} %copy-done.18, bf16[128,2048]{1,0:T(8,128)(2,1)S(1)} %all_gather.6.rows_ref, ...), custom_call_target="tpu_custom_call" | custom-call | tf_op jit(solution)/shard_map/attention/pallas_call | solution.py:269
  44.6 7.5 %all_to_all.10.part_ref = bf16[8,64,128]{2,1,0:T(8,128)(2,1)S(1)} all-to-all(bf16[8,64,128]{2,1,0:T(8,128)(2,1)S(1)} %get-tuple-element.8), channel_id=1, replica_groups=mesh['seq'=8,'exp'=4] {'seq'}, dimensions={0} | all-to-all | bytes 262144 | tf_op jit(solution)/shard_map/all_to_all | solution.py:533
  52.1 0.6 merge_project.1
  52.7 1.3 %collective-permute-start = (bf16[16,2048]{1,0:T(8,128)(2,1)S(1)}, bf16[16,2048]{1,0:T(8,128)(2,1)S(1)}, u32[]{:S(2)}, u32[]{:S(2)}) collective-permute-start(bf16[16,2048]{1,0:T(8,128)(2,1)S(1)} %merge_project.1), channel_id=1, source_target_pairs={{0,1},{1,0},{2,3},{3,2},{4,5},{5,4},{6,7},{7,6},{8,9},{9,8},{10,11... | collective-permute-start | bytes 196616 | tf_op jit(solution)/shard_map/ppermute | solution.py:475
  54.0 1.8 %collective-permute-done = bf16[16,2048]{1,0:T(8,128)(2,1)S(1)} collective-permute-done((bf16[16,2048]{1,0:T(8,128)(2,1)S(1)}, bf16[16,2048]{1,0:T(8,128)(2,1)S(1)}, u32[]{:S(2)}, u32[]{:S(2)}) %collective-permute-start) | collective-permute-done | bytes 65568 | tf_op jit(solution)/shard_map/ppermute | solution.py:475
  55.9 2.4 %collective-permute-start.1 = (bf16[16,2048]{1,0:T(8,128)(2,1)S(1)}, bf16[16,2048]{1,0:T(8,128)(2,1)S(1)}, u32[]{:S(2)}, u32[]{:S(2)}) collective-permute-start(bf16[16,2048]{1,0:T(8,128)(2,1)S(1)} %add_convert_fusion.left_ref), channel_id=1, source_target_pairs={{0,2},{1,3},{2,0},{3,1},{4,6},{5,7},{6,4},{7,5},{8,10},{9,11},{10,... | collective-permute-start | bytes 196616 | tf_op jit(solution)/shard_map/ppermute | solution.py:475
  58.3 1.6 %collective-permute-done.1.right_ref = bf16[16,2048]{1,0:T(8,128)(2,1)S(1)} collective-permute-done((bf16[16,2048]{1,0:T(8,128)(2,1)S(1)}, bf16[16,2048]{1,0:T(8,128)(2,1)S(1)}, u32[]{:S(2)}, u32[]{:S(2)}) %collective-permute-start.1) | collective-permute-done | bytes 65568 | tf_op jit(solution)/shard_map/ppermute | solution.py:475
  60.0 0.2 second_norm.1
  60.1 12.1 %all_gather.7.rows_ref = bf16[128,2176]{1,0:T(8,128)(2,1)S(1)} all-gather(bf16[16,2176]{1,0:T(8,128)(2,1)S(1)} %get-tuple-element.10.rows_ref), channel_id=1, replica_groups=mesh['seq'=8,'exp'=4] {'seq'}, dimensions={0}, use_global_device_ids=true | all-gather | bytes 626688 | tf_op jit(solution)/shard_map/all_gather | solution.py:547
  72.2 1.8 %copy-done.4 = bf16[2048,704]{0,1:T(8,128)(2,1)S(1)} copy-done((bf16[2048,704]{0,1:T(8,128)(2,1)S(1)}, bf16[2048,704]{0,1:T(8,128)(2,1)}, u32[]{:S(2)}) %copy-start.4) | copy-done | bytes 2883608
  74.0 1.8 %copy-done.5 = bf16[704,2048]{1,0:T(8,128)(2,1)S(1)} copy-done((bf16[704,2048]{1,0:T(8,128)(2,1)S(1)}, bf16[704,2048]{1,0:T(8,128)(2,1)}, u32[]{:S(2)}) %copy-start.5) | copy-done | bytes 2883608
  75.8 2.0 %shared_experts.1.shared_ref = f32[16,2048]{1,0:T(8,128)S(1)} custom-call(bf16[16,2176]{1,0:T(8,128)(2,1)S(1)} %get-tuple-element.10.rows_ref, bf16[704,2048]{1,0:T(8,128)(2,1)S(1)} %bitcast.13, bf16[704,2048]{1,0:T(8,128)(2,1)S(1)} %bitcast.14, bf16[704,2048]{1,0:T(8,128)(2,1)S(1)} %copy-done.5), custom_call_target="tpu_custom_call" | custom-call | tf_op jit(solution)/shard_map/shared_experts/pallas_call | solution.py:391
  77.8 4.3 %copy-done = bf16[8,2048,352]{1,2,0:T(8,128)(2,1)S(1)} copy-done((bf16[8,2048,352]{1,2,0:T(8,128)(2,1)S(1)}, bf16[8,2048,352]{1,2,0:T(8,128)(2,1)}, u32[]{:S(2)}) %copy-start) | copy-done | bytes 11534360
  82.1 4.3 %copy-done.1 = bf16[8,2048,352]{1,2,0:T(8,128)(2,1)S(1)} copy-done((bf16[8,2048,352]{1,2,0:T(8,128)(2,1)S(1)}, bf16[8,2048,352]{1,2,0:T(8,128)(2,1)}, u32[]{:S(2)}) %copy-start.1) | copy-done | bytes 11534360
  86.4 13.9 %routed_experts.1 = bf16[32,12,512]{2,1,0:T(8,128)(2,1)} custom-call(s32[2]{0:T(128)S(1)} %pad_add_fusion.place_ref, bf16[128,2176]{1,0:T(8,128)(2,1)S(1)} %all_gather.7.rows_ref, f32[16,2048]{1,0:T(8,128)S(1)} %shared_experts.1.shared_ref, bf16[8,352,2048]{2,1,0:T(8,128)(2,1)S(1)} %bitcast.11, bf16[8,352,2048]{2,1,0:T(8,128)(2,1)S(1)} %bitcast.12, ...), custom_call_target="tpu_custom_call" | custom-call | tf_op jit(solution)/shard_map/routed_experts/pallas_call | solution.py:439
  100.3 5.4 %all-to-all-start.1 = ((bf16[32,12,512]{2,1,0:T(8,128)(2,1)}), bf16[32,12,512]{2,1,0:T(8,128)(2,1)S(1)}, u32[]{:S(2)}, u32[]{:S(2)}) async-start(bf16[32,12,512]{2,1,0:T(8,128)(2,1)} %routed_experts.1), calls=%async_computation.1 | async-start | bytes 1048576 | tf_op jit(solution)/shard_map/all_to_all | solution.py:559
  105.6 15.3 %all-to-all-done.1.parts_ref = bf16[32,12,512]{2,1,0:T(8,128)(2,1)S(1)} async-done(((bf16[32,12,512]{2,1,0:T(8,128)(2,1)}), bf16[32,12,512]{2,1,0:T(8,128)(2,1)S(1)}, u32[]{:S(2)}, u32[]{:S(2)}) %all-to-all-start.1) | async-done | bytes 393248 | tf_op jit(solution)/shard_map/all_to_all | solution.py:559
  120.9 0.7 last_sum.1
  (35 shorter events, 0.4 us)
Async XLA Ops:
  1.7 0.9 copy-start.10
  2.6 0.7 copy-start.13
  15.7 2.7 %copy-start.2 = (bf16[46,128,512]{2,1,0:T(8,128)(2,1)S(1)}, bf16[46,128,512]{2,1,0:T(8,128)(2,1)}, u32[]{:S(2)}) copy-start(bf16[46,128,512]{2,1,0:T(8,128)(2,1)} %key_in.1) | copy-start | bytes 18087940
  18.4 1.6 %copy-start.7 = (bf16[2048,512]{1,0:T(8,128)(2,1)S(1)}, bf16[2048,512]{1,0:T(8,128)(2,1)}, u32[]{:S(2)}) copy-start(bf16[2048,512]{1,0:T(8,128)(2,1)} %query_hbm.1) | copy-start | bytes 6291460
  20.0 1.6 %copy-start.8 = (bf16[2048,512]{1,0:T(8,128)(2,1)S(1)}, bf16[2048,512]{1,0:T(8,128)(2,1)}, u32[]{:S(2)}) copy-start(bf16[2048,512]{1,0:T(8,128)(2,1)} %key_hbm.1) | copy-start | bytes 6291460
  21.6 1.6 %copy-start.9 = (bf16[2048,512]{1,0:T(8,128)(2,1)S(1)}, bf16[2048,512]{1,0:T(8,128)(2,1)}, u32[]{:S(2)}) copy-start(bf16[2048,512]{1,0:T(8,128)(2,1)} %value_hbm.1) | copy-start | bytes 6291460
  23.2 0.7 copy-start.16
  23.8 0.7 copy-start.17
  24.5 0.7 copy-start.18
  25.1 26.9 %copy-start.6 = (bf16[512,2048]{1,0:T(8,128)(2,1)S(1)}, bf16[512,2048]{1,0:T(8,128)(2,1)}, u32[]{:S(2)}) copy-start(bf16[512,2048]{1,0:T(8,128)(2,1)} %weight_ref.1) | copy-start | bytes 6291460
  25.1 34.8 %copy-start.11 = (f32[3,4,2048]{2,1,0:T(4,128)S(1)}, f32[3,4,2048]{2,1,0:T(4,128)}, u32[]{:S(2)}) copy-start(f32[3,4,2048]{2,1,0:T(4,128)} %hidden_ref.3) | copy-start | bytes 294916
  25.1 34.8 %copy-start.12 = (f32[2048]{0:T(1024)S(1)}, f32[2048]{0:T(1024)}, u32[]{:S(2)}) copy-start(f32[2048]{0:T(1024)} %param.33) | copy-start | bytes 24580
  25.1 34.8 %copy-start.14 = (s32[3,4,6]{2,1,0:T(4,128)S(1)}, s32[3,4,6]{2,1,0:T(4,128)}, u32[]{:S(2)}) copy-start(s32[3,4,6]{2,1,0:T(4,128)} %ids_ref.1) | copy-start | bytes 868
  25.1 34.8 %copy-start.15 = (f32[3,4,6]{2,1,0:T(4,128)S(1)}, f32[3,4,6]{2,1,0:T(4,128)}, u32[]{:S(2)}) copy-start(f32[3,4,6]{2,1,0:T(4,128)} %gates_ref.1) | copy-start | bytes 868
  25.2 47.0 %copy-start.3 = (bf16[2048,704]{0,1:T(8,128)(2,1)S(1)}, bf16[2048,704]{0,1:T(8,128)(2,1)}, u32[]{:S(2)}) copy-start(bf16[2048,704]{0,1:T(8,128)(2,1)} %param.39) | copy-start | bytes 8650756
  52.7 3.1 %collective-permute-start = (bf16[16,2048]{1,0:T(8,128)(2,1)S(1)}, bf16[16,2048]{1,0:T(8,128)(2,1)S(1)}, u32[]{:S(2)}, u32[]{:S(2)}) collective-permute-start(bf16[16,2048]{1,0:T(8,128)(2,1)S(1)} %merge_project.1), channel_id=1, source_target_pairs={{0,1},{1,0},{2,3},{3,2},{4,5},{5,4},{6,7},{7,6},{8,9},{9,8},{10,11... | collective-permute-start | bytes 196616 | tf_op jit(solution)/shard_map/ppermute | solution.py:475
  55.9 4.1 %collective-permute-start.1 = (bf16[16,2048]{1,0:T(8,128)(2,1)S(1)}, bf16[16,2048]{1,0:T(8,128)(2,1)S(1)}, u32[]{:S(2)}, u32[]{:S(2)}) collective-permute-start(bf16[16,2048]{1,0:T(8,128)(2,1)S(1)} %add_convert_fusion.left_ref), channel_id=1, source_target_pairs={{0,2},{1,3},{2,0},{3,1},{4,6},{5,7},{6,4},{7,5},{8,10},{9,11},{10,... | collective-permute-start | bytes 196616 | tf_op jit(solution)/shard_map/ppermute | solution.py:475
  72.2 1.8 %copy-start.4 = (bf16[2048,704]{0,1:T(8,128)(2,1)S(1)}, bf16[2048,704]{0,1:T(8,128)(2,1)}, u32[]{:S(2)}) copy-start(bf16[2048,704]{0,1:T(8,128)(2,1)} %param.40) | copy-start | bytes 8650756
  74.0 1.8 %copy-start.5 = (bf16[704,2048]{1,0:T(8,128)(2,1)S(1)}, bf16[704,2048]{1,0:T(8,128)(2,1)}, u32[]{:S(2)}) copy-start(bf16[704,2048]{1,0:T(8,128)(2,1)} %down_ref.2) | copy-start | bytes 8650756
  77.8 4.3 %copy-start = (bf16[8,2048,352]{1,2,0:T(8,128)(2,1)S(1)}, bf16[8,2048,352]{1,2,0:T(8,128)(2,1)}, u32[]{:S(2)}) copy-start(bf16[8,2048,352]{1,2,0:T(8,128)(2,1)} %param.36) | copy-start | bytes 34603012
  82.1 4.3 %copy-start.1 = (bf16[8,2048,352]{1,2,0:T(8,128)(2,1)S(1)}, bf16[8,2048,352]{1,2,0:T(8,128)(2,1)}, u32[]{:S(2)}) copy-start(bf16[8,2048,352]{1,2,0:T(8,128)(2,1)} %param.37) | copy-start | bytes 34603012
  100.3 20.7 %all-to-all-start.1 = ((bf16[32,12,512]{2,1,0:T(8,128)(2,1)}), bf16[32,12,512]{2,1,0:T(8,128)(2,1)S(1)}, u32[]{:S(2)}, u32[]{:S(2)}) async-start(bf16[32,12,512]{2,1,0:T(8,128)(2,1)} %routed_experts.1), calls=%async_computation.1 | async-start | bytes 1048576 | tf_op jit(solution)/shard_map/all_to_all | solution.py:559

commit v2 on v1

v2 whole, which is shorter than its diff:
```python
import functools
import math

import jax
import jax.numpy as jnp
import numpy as np
from jax import lax
from jax.experimental import pallas as pl
from jax.experimental.pallas import tpu as pltpu
from jax.sharding import PartitionSpec as P

HD = 128
EXPERTS = 64
GROUP = 16
BLOCK = 768
AHEAD = 3
CHUNK = 16
NEG = -1e30
MIB = 1 << 20
F32 = jnp.float32
BF16 = jnp.bfloat16


def vmem():
    return pl.BlockSpec(memory_space=pltpu.VMEM)


def smem():
    return pl.BlockSpec(memory_space=pltpu.SMEM)


def hbm():
    return pl.BlockSpec(memory_space=pl.ANY)


def far(array):
    return pltpu.with_memory_space_constraint(array, pltpu.HBM)


def dot_nt(a, b):
    return lax.dot_general(a, b, (((1,), (1,)), ((), ())), preferred_element_type=F32)


def dot_nn(a, b):
    return jnp.dot(a, b, preferred_element_type=F32)


def iota(shape, dim):
    return lax.broadcasted_iota(jnp.int32, shape, dim)


class Stream:
    def __init__(self, groups, ahead):
        self.groups = groups
        self.started = 0
        self.done = 0
        self.start_up_to(ahead)

    def start_up_to(self, count):
        while self.started < min(count, len(self.groups)):
            for copy in self.groups[self.started]:
                copy.start()
            self.started += 1

    def need(self, count):
        while self.done < count:
            for copy in self.groups[self.done]:
                copy.wait()
            self.done += 1
            self.start_up_to(self.started + 1)


def norm_kernel(hidden_hbm, gain_hbm, out_ref, hidden_ref, gain_ref, rows_ref, sem):
    copies = [
        pltpu.make_async_copy(hidden_hbm, hidden_ref, sem.at[0]),
        pltpu.make_async_copy(gain_hbm, gain_ref, sem.at[1]),
    ]
    for copy in copies:
        copy.start()
    local, steps, _ = hidden_ref.shape
    rows_ref[...] = jnp.zeros_like(rows_ref)
    for copy in copies:
        copy.wait()
    for j in range(local):
        rows_ref[pl.ds(j * steps, steps), :] = hidden_ref[j]
    rows = rows_ref[...]
    mean_square = jnp.mean(rows * rows, axis=-1, keepdims=True)
    out_ref[...] = (rows * lax.rsqrt(mean_square + 1e-06) * gain_ref[...]).astype(BF16)


def norm_rows(hidden, gain):
    width = hidden.shape[2]
    return pl.pallas_call(
        norm_kernel,
        out_shape=jax.ShapeDtypeStruct((GROUP, width), BF16),
        in_specs=[hbm(), hbm()],
        out_specs=vmem(),
        scratch_shapes=[
            pltpu.VMEM(hidden.shape, F32),
            pltpu.VMEM((1, width), F32),
            pltpu.VMEM((GROUP, width), F32),
            pltpu.SemaphoreType.DMA((2,)),
        ],
        compiler_params=pltpu.CompilerParams(vmem_limit_bytes=4 * MIB),
        name="norm_rows",
    )(far(hidden), far(gain.reshape(1, width)))


def rotated(full, cosine, sine):
    heads = full.shape[1] // HD
    parts = []
    for h in range(heads):
        one = full[:, h * HD : (h + 1) * HD]
        parts.append(one * cosine + pltpu.roll(one, HD // 2, 1) * sine)
    return jnp.concatenate(parts, axis=1)


def attention_kernel(
    local,
    steps,
    lens_ref,
    slot_req_ref,
    slot_block_ref,
    rows_ref,
    freq_ref,
    query_hbm,
    key_hbm,
    value_hbm,
    key_in,
    value_in,
    part_ref,
    key_out,
    value_out,
    weights,
    key_buf,
    value_buf,
    spread,
    new_keys,
    new_values,
    scores_buf,
    weight_buf,
    slot_max,
    slot_total,
    slot_out,
    req_max,
    req_total,
    req_out,
    weight_sem,
    in_sem,
    out_sem,
):
    pool, block, width = key_buf.shape
    heads = width // HD
    per = heads * steps
    requests = req_max.shape[0]
    groups = requests // local
    chunks = [(c, min(c + CHUNK, pool)) for c in range(0, pool, CHUNK)]

    weight_copies = [
        pltpu.make_async_copy(src, weights.at[i], weight_sem.at[i])
        for i, src in enumerate((query_hbm, key_hbm, value_hbm))
    ]

    def moves(source, target, sems, n):
        return [
            pltpu.make_async_copy(
                source.at[pl.ds(low, high - low)], target.at[pl.ds(low, high - low)], sems.at[n, i]
            )
            for i, (low, high) in enumerate(chunks)
        ]

    keys_in = moves(key_in, key_buf, in_sem, 0)
    values_in = moves(value_in, value_buf, in_sem, 1)
    keys_out = moves(key_buf, key_out, out_sem, 0)
    values_out = moves(value_buf, value_out, out_sem, 1)
    stream = Stream([[copy] for copy in weight_copies + keys_in + values_in], AHEAD)

    group_row = iota((GROUP, HD), 0)
    places = []
    for g in range(groups):
        place = group_row % steps
        for j in range(local):
            here = group_row // steps == j
            place = place + jnp.where(here, lens_ref[g * local + j], 0)
        places.append(place)
    angles = jnp.concatenate(places, axis=0).astype(F32) * freq_ref[...]
    cosine = jnp.cos(angles)
    sine = jnp.sin(angles)
    sine = jnp.where(iota(sine.shape, 1) < HD // 2, -sine, sine)

    rows = rows_ref[...]
    stream.need(1)
    queries = rotated(dot_nn(rows, weights[0]), cosine, sine).astype(BF16)
    picked = iota((requests * per, rows.shape[0]), 0)
    request, inside = picked // per, picked % per
    source = request // local * GROUP + request % local * steps + inside % steps
    choose = (source == iota(picked.shape, 1)).astype(BF16)
    wide = dot_nn(choose, queries)
    head_of = iota(wide.shape, 0) % per // steps
    spread[...] = (
        jnp.where(head_of == iota(wide.shape, 1) // HD, wide, 0.0)
        .astype(BF16)
        .reshape(requests, per, width)
    )
    stream.need(2)
    new_keys[...] = rotated(dot_nn(rows, weights[1]), cosine, sine).astype(BF16).astype(F32)
    stream.need(3)
    new_values[...] = dot_nn(rows, weights[2]).astype(BF16).astype(F32)

    patch_rows = iota((16, width), 0)

    def slot_facts(s):
        wanted = slot_req_ref[s]
        request = jnp.maximum(wanted, 0)
        base = lens_ref[request] - slot_block_ref[s] * block
        return request, jnp.where(wanted >= 0, base, -4 * block)

    def patch(buf, new, s):
        request, base = slot_facts(s)

        @pl.when((base > -steps) & (base < block))
        def _():
            first = request // local * GROUP + request % local * steps
            for t in range(steps):
                row = base + t

                @pl.when((row >= 0) & (row < block))
                def _():
                    start = pl.multiple_of(row // 16 * 16, 16)
                    hit = patch_rows == row - start
                    old = buf[s, pl.ds(start, 16), :].astype(F32)
                    fresh = new[pl.ds(first + t, 1), :]
                    buf[s, pl.ds(start, 16), :] = jnp.where(hit, fresh, old).astype(BF16)

    def patch_all(buf, new, low, high):
        def one(s, carry):
            patch(buf, new, s)
            return carry

        lax.fori_loop(low, high, one, 0)

    def pairs(low, high):
        return [(s, min(s + 2, high)) for s in range(low, high, 2)]

    for i, (low, high) in enumerate(chunks):
        stream.need(4 + i)
        patch_all(key_buf, new_keys, low, high)
        keys_out[i].start()
        for a, b in pairs(low, high):
            left = jnp.concatenate([spread[slot_facts(s)[0]] for s in range(a, b)], axis=0)
            right = key_buf[pl.ds(a, b - a)].reshape((b - a) * block, width)
            both = dot_nt(left, right)
            for s in range(a, b):
                n = s - a
                scores_buf[s] = both[n * per : (n + 1) * per, n * block : (n + 1) * block]

    scale = 1.0 / math.sqrt(HD)
    behind = iota((per, block), 1) - iota((per, block), 0) % steps
    for s in range(pool):
        allowed = behind <= slot_facts(s)[1]
        scores = jnp.where(allowed, scores_buf[s] * scale, NEG)
        top = jnp.max(scores, axis=-1, keepdims=True)
        weight = jnp.where(allowed, jnp.exp(scores - top), 0.0)
        slot_max[s] = jnp.broadcast_to(top, (per, HD))
        slot_total[s] = jnp.broadcast_to(jnp.sum(weight, axis=-1, keepdims=True), (per, HD))
        weight_buf[s] = weight.astype(BF16)

    req_max[...] = jnp.full_like(req_max, NEG)
    for s in range(pool):
        request = slot_facts(s)[0]
        req_max[request] = jnp.maximum(req_max[request], slot_max[s])

    lane_head = iota((per, HD), 0) // steps
    for i, (low, high) in enumerate(chunks):
        stream.need(4 + len(chunks) + i)
        patch_all(value_buf, new_values, low, high)
        values_out[i].start()
        for a, b in pairs(low, high):
            pieces = []
            for s in range(a, b):
                row = [jnp.zeros((per, block), BF16)] * (b - a)
                row[s - a] = weight_buf[s]
                pieces.append(jnp.concatenate(row, axis=1))
            left = jnp.concatenate(pieces, axis=0)
            mixed = dot_nn(left, value_buf[pl.ds(a, b - a)].reshape((b - a) * block, width))
            for s in range(a, b):
                mine = mixed[(s - a) * per : (s - a + 1) * per]
                result = mine[:, :HD]
                for h in range(1, heads):
                    result = jnp.where(lane_head == h, mine[:, h * HD : (h + 1) * HD], result)
                slot_out[s] = result

    for s in range(pool):
        factor = jnp.exp(slot_max[s] - req_max[slot_facts(s)[0]])
        slot_total[s] = factor * slot_total[s]
        slot_out[s] = factor * slot_out[s]
    req_total[...] = jnp.zeros_like(req_total)
    req_out[...] = jnp.zeros_like(req_out)
    for s in range(pool):
        request = slot_facts(s)[0]
        req_total[request] = req_total[request] + slot_total[s]
        req_out[request] = req_out[request] + slot_out[s]

    total = req_total[...]
    some = total > 0.0
    safe = jnp.where(some, total, 1.0)
    mean = jnp.where(some, req_out[...] / safe, 0.0).astype(BF16)
    level = jnp.where(some, req_max[...] + jnp.log(safe), NEG)
    high = level.astype(BF16).astype(F32)
    middle = (level - high).astype(BF16).astype(F32)
    low_part = (level - high - middle).astype(BF16).astype(F32)
    row = iota(level.shape, 1)
    lane = iota(level.shape, 2)
    packed = jnp.where(lane == row, high, 0.0)
    packed = packed + jnp.where(lane == row + per, middle, 0.0)
    packed = packed + jnp.where(lane == row + 2 * per, low_part, 0.0)
    packed = jnp.sum(packed, axis=1, keepdims=True)
    block_row = iota((16, HD), 0)
    for g in range(groups):
        levels = jnp.zeros((16, HD), F32)
        for j in range(local):
            b = g * local + j
            part_ref[g, pl.ds(j * per, per), :] = mean[b]
            levels = jnp.where(block_row == j, packed[b], levels)
        part_ref[g, pl.ds(local * per, 16), :] = levels.astype(BF16)
    for copy in keys_out + values_out:
        copy.wait()


def attention(rows, weights, caches, lens, slot_req, slot_block, local, steps):
    pool, block, width = caches[0].shape
    model = rows.shape[1]
    requests = lens.shape[0]
    per = width // HD * steps
    chunk_count = -(-pool // CHUNK)
    half = HD // 2
    frequency = np.power(10000.0, -np.arange(half, dtype=np.float64) * (2.0 / HD)).astype(np.float32)
    frequency = np.concatenate([frequency, frequency])[None]
    cache_shape = jax.ShapeDtypeStruct(caches[0].shape, BF16)
    slot_stat = pltpu.VMEM((pool, per, HD), F32)
    req_stat = pltpu.VMEM((requests, per, HD), F32)
    return pl.pallas_call(
        functools.partial(attention_kernel, local, steps),
        out_shape=(
            jax.ShapeDtypeStruct((requests // local, local * per + 16, HD), BF16),
            cache_shape,
            cache_shape,
        ),
        in_specs=[smem()] * 3 + [vmem()] * 2 + [hbm()] * 5,
        out_specs=(vmem(), hbm(), hbm()),
        scratch_shapes=[
            pltpu.VMEM((3, model, width), BF16),
            pltpu.VMEM((pool, block, width), BF16),
            pltpu.VMEM((pool, block, width), BF16),
            pltpu.VMEM((requests, per, width), BF16),
            pltpu.VMEM((rows.shape[0], width), F32),
            pltpu.VMEM((rows.shape[0], width), F32),
            pltpu.VMEM((pool, per, block), F32),
            pltpu.VMEM((pool, per, block), BF16),
            slot_stat,
            slot_stat,
            slot_stat,
            req_stat,
            req_stat,
            req_stat,
            pltpu.SemaphoreType.DMA((3,)),
            pltpu.SemaphoreType.DMA((2, chunk_count)),
            pltpu.SemaphoreType.DMA((2, chunk_count)),
        ],
        compiler_params=pltpu.CompilerParams(vmem_limit_bytes=40 * MIB),
        name="attention",
    )(
        far(lens),
        far(slot_req),
        far(slot_block),
        rows,
        jnp.asarray(frequency),
        *[far(array) for array in weights],
        *[far(array) for array in caches],
    )


def merge_kernel(local, steps, part_ref, weight_ref, out_ref):
    holders = part_ref.shape[0]
    width = weight_ref.shape[0]
    heads = width // HD
    per = heads * steps
    count = local * per
    values = [part_ref[g, pl.ds(0, count), :].astype(F32) for g in range(holders)]
    row = iota((count, HD), 0)
    lane = iota((count, HD), 1)
    mine = (lane % per == row % per) & (lane < 3 * per)
    levels = []
    for g in range(holders):
        stat = part_ref[g, pl.ds(count, 16), :].astype(F32)
        wide = jnp.concatenate(
            [jnp.broadcast_to(stat[j : j + 1], (per, HD)) for j in range(local)], axis=0
        )
        levels.append(jnp.sum(jnp.where(mine, wide, 0.0), axis=-1, keepdims=True))
    top = functools.reduce(jnp.maximum, levels)
    shares = [jnp.exp(level - top) for level in levels]
    total = sum(shares)
    mixed = sum(share * value for share, value in zip(shares, values))
    attended = (mixed / total).astype(BF16)
    target = iota((GROUP, count), 0)
    source = iota((GROUP, count), 1)
    parts = []
    for h in range(heads):
        pick = (source == target // steps * per + h * steps + target % steps) & (
            target < local * steps
        )
        parts.append(dot_nn(pick.astype(BF16), attended).astype(BF16))
    out_ref[...] = dot_nn(jnp.concatenate(parts, axis=1), weight_ref[...]).astype(BF16)


def merge_project(parts, out_weight, local, steps):
    return pl.pallas_call(
        functools.partial(merge_kernel, local, steps),
        out_shape=jax.ShapeDtypeStruct((GROUP, out_weight.shape[1]), BF16),
        in_specs=[vmem(), vmem()],
        out_specs=vmem(),
        compiler_params=pltpu.CompilerParams(vmem_limit_bytes=8 * MIB),
        name="merge_project",
    )(parts, out_weight)


def second_norm_kernel(hidden_ref, left_ref, right_ref, gain_ref, ids_ref, gates_ref, rows_out, res_out, rows_ref):
    local, steps, width = hidden_ref.shape
    rows_ref[...] = jnp.zeros_like(rows_ref)
    for j in range(local):
        rows_ref[pl.ds(j * steps, steps), :] = hidden_ref[j]
    residual = rows_ref[...] + (left_ref[...].astype(F32) + right_ref[...].astype(F32))
    res_out[...] = residual
    mean_square = jnp.mean(residual * residual, axis=-1, keepdims=True)
    normed = residual * lax.rsqrt(mean_square + 1e-06) * gain_ref[...]
    rows_out[:, pl.ds(0, width)] = normed.astype(BF16)
    rows_ref[:, pl.ds(0, HD)] = jnp.zeros((GROUP, HD), F32)
    lane = iota((steps, HD), 1)
    for j in range(local):
        table = jnp.zeros((steps, HD), F32)
        for k in range(ids_ref.shape[2]):
            hit = lane % EXPERTS == ids_ref[j, :, k : k + 1]
            table = table + jnp.where(hit, gates_ref[j, :, k : k + 1], 0.0)
        rows_ref[pl.ds(j * steps, steps), pl.ds(0, HD)] = table
    table = rows_ref[:, pl.ds(0, HD)]
    high = table.astype(BF16)
    low = (table - high.astype(F32)).astype(BF16)
    rows_out[:, pl.ds(width, HD)] = jnp.where(iota((GROUP, HD), 1) < EXPERTS, high.astype(F32), low.astype(F32)).astype(BF16)


def second_norm(hidden, left, right, gain, ids, gates):
    width = hidden.shape[2]
    return pl.pallas_call(
        second_norm_kernel,
        out_shape=(
            jax.ShapeDtypeStruct((GROUP, width + HD), BF16),
            jax.ShapeDtypeStruct((GROUP, width), F32),
        ),
        in_specs=[vmem()] * 6,
        out_specs=(vmem(), vmem()),
        scratch_shapes=[pltpu.VMEM((GROUP, width), F32)],
        compiler_params=pltpu.CompilerParams(vmem_limit_bytes=4 * MIB),
        name="second_norm",
    )(hidden, left, right, gain.reshape(1, width), ids, gates)


def shared_window(total, ranks):
    each = total // ranks
    length = max(-(-(r * each % 16 + each) // 16) * 16 for r in range(ranks))
    return each, length


def experts_kernel(
    tokens,
    count,
    ranks,
    rows_ref,
    gate_hbm,
    up_hbm,
    down_hbm,
    shared_gate_hbm,
    shared_up_hbm,
    shared_down_hbm,
    out_ref,
    gate_ref,
    up_ref,
    down_ref,
    inner_ref,
    total_ref,
    sem,
    shared_sem,
):
    hidden, width = gate_hbm.shape
    every = gate_ref.shape[0]
    each = hidden // count
    slim, length = shared_window(shared_gate_hbm.shape[0], ranks)
    seq_rank = lax.axis_index("seq")
    slim_low = seq_rank * slim
    slim_start = pl.multiple_of(
        jnp.minimum(slim_low // 16 * 16, shared_gate_hbm.shape[0] - length), 16
    )
    blocks = [(low, min(low + BLOCK, every)) for low in range(0, every, BLOCK)]

    def moves(source, extra, target, n):
        copies = []
        for i, (low, high) in enumerate(blocks):
            top = min(high, hidden)
            piece = [
                pltpu.make_async_copy(
                    source.at[pl.ds(low, top - low)], target.at[pl.ds(low, top - low)], sem.at[n, i]
                )
            ] if top > low else []
            if high == every:
                piece.append(
                    pltpu.make_async_copy(
                        extra.at[pl.ds(slim_start, length)],
                        target.at[pl.ds(hidden, length)],
                        shared_sem.at[n],
                    )
                )
            copies.append(piece)
        return copies

    gates = moves(gate_hbm, shared_gate_hbm, gate_ref, 0)
    ups = moves(up_hbm, shared_up_hbm, up_ref, 1)
    downs = moves(down_hbm, shared_down_hbm, down_ref, 2)
    stream = Stream([a + b for a, b in zip(gates, ups)] + downs, 2)

    first = seq_rank * count
    rows = rows_ref[:, pl.ds(0, width)]
    table = rows_ref[:, pl.ds(width, HD)]
    for i, (low, high) in enumerate(blocks):
        shape = (HD, high - low)
        unit = low + iota(shape, 1)
        expert = jnp.where(unit < hidden, first + unit // each, -1)
        share = dot_nn(table, (iota(shape, 0) % EXPERTS == expert).astype(BF16))
        if high > hidden:
            unit = low + iota(share.shape, 1) - hidden + slim_start
            mine = (unit >= slim_low) & (unit < slim_low + slim)
            in_shared = low + iota(share.shape, 1) >= hidden
            share = jnp.where(in_shared, mine.astype(F32), share)
        stream.need(i + 1)
        gate = dot_nt(rows, gate_ref[pl.ds(low, high - low), :])
        up = dot_nt(rows, up_ref[pl.ds(low, high - low), :])
        inner_ref[:, pl.ds(low, high - low)] = (jax.nn.silu(gate) * up * share).astype(BF16)

    groups = total_ref.shape[0] // GROUP
    pieces = out_ref.shape[0] // groups
    columns = width // pieces
    for i, (low, high) in enumerate(blocks):
        stream.need(len(blocks) + 1 + i)
        part = inner_ref[:, pl.ds(low, high - low)]
        for p in range(pieces):
            cut = pl.ds(p * columns, columns)
            sums = dot_nn(part, down_ref[pl.ds(low, high - low), cut])
            if i > 0:
                sums = sums + total_ref[:, cut]
            if i < len(blocks) - 1:
                total_ref[:, cut] = sums
            else:
                for g in range(groups):
                    out_ref[g * pieces + p] = sums[g * GROUP : g * GROUP + tokens].astype(BF16)


def all_experts(rows, routed, shared, tokens, pieces):
    count, each, width = routed[2].shape
    hidden = count * each
    groups = rows.shape[0] // GROUP
    every = hidden + shared_window(shared[2].shape[0], groups)[1]
    routed = [array.reshape(hidden, width) for array in routed]
    return pl.pallas_call(
        functools.partial(experts_kernel, tokens, count, groups),
        out_shape=jax.ShapeDtypeStruct((groups * pieces, tokens, width // pieces), BF16),
        in_specs=[vmem()] + [hbm()] * 6,
        out_specs=vmem(),
        scratch_shapes=[pltpu.VMEM((every, width), BF16)] * 3
        + [
            pltpu.VMEM((rows.shape[0], every), BF16),
            pltpu.VMEM((rows.shape[0], width), F32),
            pltpu.SemaphoreType.DMA((3, -(-every // BLOCK))),
            pltpu.SemaphoreType.DMA((3,)),
        ],
        compiler_params=pltpu.CompilerParams(vmem_limit_bytes=56 * MIB),
        name="experts",
    )(rows, *[far(array) for array in (*routed, *shared)])


def last_kernel(res_ref, parts_ref, out_ref):
    local, steps, columns = out_ref.shape
    total = parts_ref[0].astype(F32)
    for i in range(1, parts_ref.shape[0]):
        total = total + parts_ref[i].astype(F32)
    start = pl.multiple_of(lax.axis_index("exp") * columns, HD)
    total = total + res_ref[pl.ds(0, local * steps), pl.ds(start, columns)]
    for j in range(local):
        out_ref[j] = total[j * steps : (j + 1) * steps]


def last_sum(residual, parts, local, steps):
    return pl.pallas_call(
        last_kernel,
        out_shape=jax.ShapeDtypeStruct((local, steps, parts.shape[2]), F32),
        in_specs=[vmem(), vmem()],
        out_specs=vmem(),
        compiler_params=pltpu.CompilerParams(vmem_limit_bytes=8 * MIB),
        name="last_sum",
    )(residual, parts)


def partner(array, axis, bit):
    count = lax.axis_size(axis)
    return lax.ppermute(array, axis, [(i, i ^ bit) for i in range(count)])


def body(
    hidden_in,
    cache_lens,
    slot_request,
    slot_block,
    key_cache,
    value_cache,
    attn_gain,
    query_weight,
    key_weight,
    value_weight,
    out_weight,
    ffn_gain,
    expert_ids,
    expert_weights,
    gate_experts,
    up_experts,
    down_experts,
    gate_shared,
    up_shared,
    down_shared,
):
    local, steps, width = hidden_in.shape
    exp_count = lax.axis_size("exp")
    tokens = local * steps

    normed = norm_rows(hidden_in, attn_gain)
    rows = lax.all_gather(normed, "seq", axis=0, tiled=True)
    parts, key_out, value_out = attention(
        rows,
        (query_weight, key_weight, value_weight),
        (key_cache, value_cache),
        cache_lens,
        slot_request,
        slot_block,
        local,
        steps,
    )
    parts = lax.all_to_all(parts, "seq", split_axis=0, concat_axis=0, tiled=True)
    terms = merge_project(parts, out_weight, local, steps)
    other = partner(terms, "exp", 1)
    bit = 2
    while bit < exp_count:
        terms = (terms.astype(F32) + other.astype(F32)).astype(BF16)
        other = partner(terms, "exp", bit)
        bit *= 2
    ffn_in, residual = second_norm(
        hidden_in, terms, other, ffn_gain, expert_ids, expert_weights
    )
    all_rows = lax.all_gather(ffn_in, "seq", axis=0, tiled=True)
    sums = all_experts(
        all_rows,
        (jnp.swapaxes(gate_experts, 1, 2), jnp.swapaxes(up_experts, 1, 2), down_experts),
        (jnp.swapaxes(gate_shared, 0, 1), jnp.swapaxes(up_shared, 0, 1), down_shared),
        tokens,
        exp_count,
    )
    sums = lax.all_to_all(sums, ("seq", "exp"), split_axis=0, concat_axis=0, tiled=True)
    hidden_out = last_sum(residual, sums, local, steps)
    return hidden_out, key_out, value_out


def solution(mesh):
    in_specs = (
        P("seq", None, None),
        P(),
        P("seq"),
        P("seq"),
        P("seq", None, "exp"),
        P("seq", None, "exp"),
        P(),
        P(None, "exp"),
        P(None, "exp"),
        P(None, "exp"),
        P("exp", None),
        P(),
        P("seq", None, None),
        P("seq", None, None),
        P("seq", None, "exp"),
        P("seq", None, "exp"),
        P("seq", "exp", None),
        P(None, "exp"),
        P(None, "exp"),
        P("exp", None),
    )
    out_specs = (P("seq", None, "exp"), P("seq", None, "exp"), P("seq", None, "exp"))
    return jax.shard_map(body, mesh=mesh, in_specs=in_specs, out_specs=out_specs, check_vma=False)
```

time: 122 us -> 92.9 us (0.76)
  local copies, waits for them, and re-layouts: 24.3 us -> 0.68 us
  blocking collectives: 30.7 us -> 52.9 us
  waiting for transfers between devices: 18.7 us -> 3.46 us
  Pallas kernels: 37 us -> 31 us
  starting transfers between devices: 9.04 us -> 3.75 us
    unnamed x38 -> x12, local copies, waits for them, and re-layouts: 23.3 us -> 0.68 us
    all_to_all x0 -> x1, blocking collectives: none -> 20.8 us  [body(): lax.all_to_all(sums, ('seq', 'exp'), split_axis=0, concat_axis=0, tiled=T...]
    all_to_all x1 -> x0, waiting for transfers between devices: 15.3 us -> none  [body(): lax.all_to_all(sums, ('seq', 'exp'), split_axis=0, concat_axis=0, tiled=T...]
    pallas_call x1, Pallas kernels: 19.4 us -> 12 us  [attention(): pl.pallas_call(functools.partial(attention_kernel, local, steps), out_sha...]
    all_to_all x1 -> x0, starting transfers between devices: 5.36 us -> none  [body(): lax.all_to_all(sums, ('seq', 'exp'), split_axis=0, concat_axis=0, tiled=T...]
    pallas_call x2 -> x1, Pallas kernels: 15.9 us -> 16.5 us  [all_experts(): pl.pallas_call(functools.partial(experts_kernel, tokens, count, groups),...]
  transfers between devices with their start and end apart: 3 -> 2, of which waited for: 3 -> 2; matrix products, arithmetic and copies ran while one was open for 0% -> 0% of each run, Pallas kernels for 0% -> 0%
where the time goes in v2:
time: 92.9 us; the launch traced here: 92.5 us
  blocking collectives  52.9 us (57%)
  Pallas kernels  31 us (33%)
  starting transfers between devices  3.75 us (4%)
  waiting for transfers between devices  3.46 us (4%)
    all_to_all x1, blocking collectives, body(): lax.all_to_all(sums, ('seq', 'exp'), split_axis=0, concat_axis=0, tiled=T...  20.8 us
    pallas_call x1, Pallas kernels, all_experts(): pl.pallas_call(functools.partial(experts_kernel, tokens, count, groups),...  16.5 us
    all_gather x1, blocking collectives, body(): all_rows = lax.all_gather(ffn_in, 'seq', axis=0, tiled=True)  13.2 us
    pallas_call x1, Pallas kernels, attention(): pl.pallas_call(functools.partial(attention_kernel, local, steps), out_sha...  12 us
    all_gather x1, blocking collectives, body(): rows = lax.all_gather(normed, 'seq', axis=0, tiled=True)  11.2 us
    all_to_all x1, blocking collectives, body(): lax.all_to_all(parts, 'seq', split_axis=0, concat_axis=0, tiled=True)  7.76 us
    ppermute x2, starting transfers between devices, partner(): return lax.ppermute(array, axis, [(i, i ^ bit) for i in range(count)])  3.75 us
    ppermute x2, waiting for transfers between devices, partner(): return lax.ppermute(array, axis, [(i, i ^ bit) for i in range(count)])  3.46 us
  transfers between devices with their start and end apart: 2, of which 2 were waited for; matrix products, arithmetic and copies ran while one was open for 0% of the time, Pallas kernels for 0%

profile of v2, /device:TPU:1, one launch (start us, length us, event | category | flops | bytes accessed | tf_op | source)
XLA Modules:
  0.0 92.5 jit_solution(16981752341895973779)
XLA Ops:
  0.6 1.0 %norm_rows.1 = bf16[16,2048]{1,0:T(8,128)(2,1)S(1)} custom-call(f32[3,4,2048]{2,1,0:T(4,128)} %hidden_ref.1, f32[1,2048]{1,0:T(1,128)} %bitcast.17), custom_call_target="tpu_custom_call" | custom-call | tf_op jit(solution)/shard_map/norm_rows/pallas_call | solution.py:93
  1.7 11.2 %all_gather.6.rows_ref = bf16[128,2048]{1,0:T(8,128)(2,1)S(1)} all-gather(bf16[16,2048]{1,0:T(8,128)(2,1)S(1)} %norm_rows.1), channel_id=1, replica_groups=mesh['seq'=8,'exp'=4] {'seq'}, dimensions={0}, use_global_device_ids=true | all-gather | bytes 589824 | tf_op jit(solution)/shard_map/all_gather | solution.py:642
  12.9 0.0 copy-start.5
  12.9 0.7 copy-done.5
  13.6 0.0 copy-start
  13.6 0.0 copy-start.1
  13.6 0.0 copy-start.2
  13.6 0.0 copy-start.3
  13.6 0.0 copy-start.4
  13.6 12.0 %attention.1 = (bf16[8,64,128]{2,1,0:T(8,128)(2,1)S(1)}, bf16[46,128,512]{2,1,0:T(8,128)(2,1)}, bf16[46,128,512]{2,1,0:T(8,128)(2,1)}) custom-call(s32[24]{0:T(128)} %lens_ref.1, s32[46]{0:T(128)} %slot_req_ref.1, s32[46]{0:T(128)} %slot_block_ref.1, bf16[128,2048]{1,0:T(8,128)(2,1)S(1)} %all_gather.6.rows_ref, f32[1,128]{1,0:T(1,128)S(1)} %copy-done.5, ...), custom_call_target="tpu_custom_call" | custom-call | tf_op jit(solution)/shard_map/attention/pallas_call | solution.py:342
  25.6 7.8 %all_to_all.10.part_ref = bf16[8,64,128]{2,1,0:T(8,128)(2,1)S(1)} all-to-all(bf16[8,64,128]{2,1,0:T(8,128)(2,1)S(1)} %get-tuple-element.8), channel_id=1, replica_groups=mesh['seq'=8,'exp'=4] {'seq'}, dimensions={0} | all-to-all | bytes 262144 | tf_op jit(solution)/shard_map/all_to_all | solution.py:653
  33.3 0.0 copy-done
  33.3 0.6 merge_project.1
  34.0 1.3 %collective-permute-start = (bf16[16,2048]{1,0:T(8,128)(2,1)S(1)}, bf16[16,2048]{1,0:T(8,128)(2,1)S(1)}, u32[]{:S(2)}, u32[]{:S(2)}) collective-permute-start(bf16[16,2048]{1,0:T(8,128)(2,1)S(1)} %merge_project.1), channel_id=1, source_target_pairs={{0,1},{1,0},{2,3},{3,2},{4,5},{5,4},{6,7},{7,6},{8,9},{9,8},{10,11... | collective-permute-start | bytes 196616 | tf_op jit(solution)/shard_map/ppermute | solution.py:612
  35.3 1.8 %collective-permute-done = bf16[16,2048]{1,0:T(8,128)(2,1)S(1)} collective-permute-done((bf16[16,2048]{1,0:T(8,128)(2,1)S(1)}, bf16[16,2048]{1,0:T(8,128)(2,1)S(1)}, u32[]{:S(2)}, u32[]{:S(2)}) %collective-permute-start) | collective-permute-done | bytes 65568 | tf_op jit(solution)/shard_map/ppermute | solution.py:612
  37.1 2.4 %collective-permute-start.1 = (bf16[16,2048]{1,0:T(8,128)(2,1)S(1)}, bf16[16,2048]{1,0:T(8,128)(2,1)S(1)}, u32[]{:S(2)}, u32[]{:S(2)}) collective-permute-start(bf16[16,2048]{1,0:T(8,128)(2,1)S(1)} %add_convert_fusion.left_ref), channel_id=1, source_target_pairs={{0,2},{1,3},{2,0},{3,1},{4,6},{5,7},{6,4},{7,5},{8,10},{9,11},{10,... | collective-permute-start | bytes 196616 | tf_op jit(solution)/shard_map/ppermute | solution.py:612
  39.6 1.7 %collective-permute-done.1.right_ref = bf16[16,2048]{1,0:T(8,128)(2,1)S(1)} collective-permute-done((bf16[16,2048]{1,0:T(8,128)(2,1)S(1)}, bf16[16,2048]{1,0:T(8,128)(2,1)S(1)}, u32[]{:S(2)}, u32[]{:S(2)}) %collective-permute-start.1) | collective-permute-done | bytes 65568 | tf_op jit(solution)/shard_map/ppermute | solution.py:612
  41.2 0.0 copy-done.1
  41.2 0.0 copy-done.2
  41.2 0.0 copy-done.3
  41.2 0.0 copy-done.4
  41.2 0.2 second_norm.1
  41.4 13.2 %all_gather.7.rows_ref = bf16[128,2176]{1,0:T(8,128)(2,1)} all-gather(bf16[16,2176]{1,0:T(8,128)(2,1)S(1)} %get-tuple-element.10), channel_id=1, replica_groups=mesh['seq'=8,'exp'=4] {'seq'}, dimensions={0}, use_global_device_ids=true | all-gather | bytes 626688 | tf_op jit(solution)/shard_map/all_gather | solution.py:664
  54.6 16.5 %experts.1 = bf16[32,12,512]{2,1,0:T(8,128)(2,1)} custom-call(bf16[128,2176]{1,0:T(8,128)(2,1)} %all_gather.7.rows_ref, bf16[2816,2048]{1,0:T(8,128)(2,1)} %bitcast.12, bf16[2816,2048]{1,0:T(8,128)(2,1)} %bitcast.13, bf16[2816,2048]{1,0:T(8,128)(2,1)} %bitcast.14, bf16[704,2048]{1,0:T(8,128)(2,1)} %bitcast.15, bf16[704,2048]{1,0:T(8,128)(2,1)} %bitcast.16, ...), custom_call_target="tpu_custom_call" | custom-call | tf_op jit(solution)/shard_map/experts/pallas_call | solution.py:571
  71.1 20.8 %all_to_all.11.parts_ref = bf16[32,12,512]{2,1,0:T(8,128)(2,1)S(1)} all-to-all(bf16[32,12,512]{2,1,0:T(8,128)(2,1)} %experts.1), channel_id=1, replica_groups=mesh['seq'=8,'exp'=4] {'seq','exp'}, dimensions={0} | all-to-all | bytes 786432 | tf_op jit(solution)/shard_map/all_to_all | solution.py:672
  91.9 0.7 last_sum.1
  (1 shorter events, 0.0 us)
Async XLA Ops:
  12.9 0.7 copy-start.5
  13.6 19.8 %copy-start = (bf16[512,2048]{1,0:T(8,128)(2,1)S(1)}, bf16[512,2048]{1,0:T(8,128)(2,1)}, u32[]{:S(2)}) copy-start(bf16[512,2048]{1,0:T(8,128)(2,1)} %weight_ref.1) | copy-start | bytes 6291460
  13.6 27.7 %copy-start.1 = (f32[3,4,2048]{2,1,0:T(4,128)S(1)}, f32[3,4,2048]{2,1,0:T(4,128)}, u32[]{:S(2)}) copy-start(f32[3,4,2048]{2,1,0:T(4,128)} %hidden_ref.1) | copy-start | bytes 294916
  13.6 27.7 %copy-start.2 = (f32[2048]{0:T(1024)S(1)}, f32[2048]{0:T(1024)}, u32[]{:S(2)}) copy-start(f32[2048]{0:T(1024)} %param.32) | copy-start | bytes 24580
  13.6 27.7 %copy-start.3 = (s32[3,4,6]{2,1,0:T(4,128)S(1)}, s32[3,4,6]{2,1,0:T(4,128)}, u32[]{:S(2)}) copy-start(s32[3,4,6]{2,1,0:T(4,128)} %ids_ref.1) | copy-start | bytes 868
  13.6 27.7 %copy-start.4 = (f32[3,4,6]{2,1,0:T(4,128)S(1)}, f32[3,4,6]{2,1,0:T(4,128)}, u32[]{:S(2)}) copy-start(f32[3,4,6]{2,1,0:T(4,128)} %gates_ref.1) | copy-start | bytes 868
  34.0 3.1 %collective-permute-start = (bf16[16,2048]{1,0:T(8,128)(2,1)S(1)}, bf16[16,2048]{1,0:T(8,128)(2,1)S(1)}, u32[]{:S(2)}, u32[]{:S(2)}) collective-permute-start(bf16[16,2048]{1,0:T(8,128)(2,1)S(1)} %merge_project.1), channel_id=1, source_target_pairs={{0,1},{1,0},{2,3},{3,2},{4,5},{5,4},{6,7},{7,6},{8,9},{9,8},{10,11... | collective-permute-start | bytes 196616 | tf_op jit(solution)/shard_map/ppermute | solution.py:612
  37.1 4.1 %collective-permute-start.1 = (bf16[16,2048]{1,0:T(8,128)(2,1)S(1)}, bf16[16,2048]{1,0:T(8,128)(2,1)S(1)}, u32[]{:S(2)}, u32[]{:S(2)}) collective-permute-start(bf16[16,2048]{1,0:T(8,128)(2,1)S(1)} %add_convert_fusion.left_ref), channel_id=1, source_target_pairs={{0,2},{1,3},{2,0},{3,1},{4,6},{5,7},{6,4},{7,5},{8,10},{9,11},{10,... | collective-permute-start | bytes 196616 | tf_op jit(solution)/shard_map/ppermute | solution.py:612

commit v3 on v2

--- a/solution.py
+++ b/solution.py
@@ -13,6 +13,7 @@
 EXPERTS = 64
 GROUP = 16
 BLOCK = 768
+FETCHED = 2
 AHEAD = 3
 CHUNK = 16
 NEG = -1e30
@@ -35,6 +36,10 @@
 
 def far(array):
     return pltpu.with_memory_space_constraint(array, pltpu.HBM)
+
+
+def near(array):
+    return pltpu.with_memory_space_constraint(array, pltpu.VMEM)
 
 
 def dot_nt(a, b):
@@ -115,6 +120,79 @@
     return jnp.concatenate(parts, axis=1)
 
 
+def rotation(lens_ref, groups, local, steps):
+    group_row = iota((GROUP, HD), 0)
+    places = []
+    for g in range(groups):
+        place = group_row % steps
+        for j in range(local):
+            here = group_row // steps == j
+            place = place + jnp.where(here, lens_ref[g * local + j], 0)
+        places.append(place)
+    half = HD // 2
+    lane = iota((1, HD), 1) % half
+    frequency = jnp.zeros((1, HD), F32)
+    for i in range(half):
+        frequency = jnp.where(lane == i, float(np.float32(10000.0 ** (-i / half))), frequency)
+    angles = jnp.concatenate(places, axis=0).astype(F32) * frequency
+    sine = jnp.sin(angles)
+    return jnp.cos(angles), jnp.where(iota(sine.shape, 1) < half, -sine, sine)
+
+
+def spread_heads(queries, requests, local, steps):
+    per = queries.shape[1] // HD * steps
+    picked = iota((requests * per, queries.shape[0]), 0)
+    request, inside = picked // per, picked % per
+    source = request // local * GROUP + request % local * steps + inside % steps
+    choose = (source == iota(picked.shape, 1)).astype(BF16)
+    wide = dot_nn(choose, queries)
+    head_of = iota(wide.shape, 0) % per // steps
+    return jnp.where(head_of == iota(wide.shape, 1) // HD, wide, 0.0).astype(BF16)
+
+
+def own_head(mixed, steps):
+    rows, width = mixed.shape
+    heads = width // HD
+    head = iota((rows, HD), 0) % (heads * steps) // steps
+    result = mixed[:, :HD]
+    for h in range(1, heads):
+        result = jnp.where(head == h, mixed[:, h * HD : (h + 1) * HD], result)
+    return result
+
+
+def slot_place(lens_ref, slot_req_ref, slot_block_ref, s, block):
+    wanted = slot_req_ref[s]
+    request = jnp.maximum(wanted, 0)
+    base = lens_ref[request] - slot_block_ref[s] * block
+    return request, jnp.where(wanted >= 0, base, -4 * block)
+
+
+def patch_slots(slot_facts, local, steps, buf, new, low, high):
+    _, block, width = buf.shape
+    patch_rows = iota((16, width), 0)
+
+    def one(s, carry):
+        request, base = slot_facts(s)
+
+        @pl.when((base > -steps) & (base < block))
+        def _():
+            first = request // local * GROUP + request % local * steps
+            for t in range(steps):
+                row = base + t
+
+                @pl.when((row >= 0) & (row < block))
+                def _():
+                    start = pl.multiple_of(row // 16 * 16, 16)
+                    hit = patch_rows == row - start
+                    old = buf[s, pl.ds(start, 16), :].astype(F32)
+                    fresh = new[pl.ds(first + t, 1), :]
+                    buf[s, pl.ds(start, 16), :] = jnp.where(hit, fresh, old).astype(BF16)
+
+        return carry
+
+    lax.fori_loop(low, high, one, 0)
+
+
 def attention_kernel(
     local,
     steps,
@@ -122,21 +200,15 @@
     slot_req_ref,
     slot_block_ref,
     rows_ref,
-    freq_ref,
     query_hbm,
-    key_hbm,
-    value_hbm,
     key_in,
     value_in,
     part_ref,
-    key_out,
-    value_out,
-    weights,
+    queries_ref,
+    weight,
     key_buf,
     value_buf,
     spread,
-    new_keys,
-    new_values,
     scores_buf,
     weight_buf,
     slot_max,
@@ -147,7 +219,6 @@
     req_out,
     weight_sem,
     in_sem,
-    out_sem,
 ):
     pool, block, width = key_buf.shape
     heads = width // HD
@@ -156,10 +227,7 @@
     groups = requests // local
     chunks = [(c, min(c + CHUNK, pool)) for c in range(0, pool, CHUNK)]
 
-    weight_copies = [
-        pltpu.make_async_copy(src, weights.at[i], weight_sem.at[i])
-        for i, src in enumerate((query_hbm, key_hbm, value_hbm))
-    ]
+    weight_copy = pltpu.make_async_copy(query_hbm, weight, weight_sem.at[0])
 
     def moves(source, target, sems, n):
         return [
@@ -171,81 +239,22 @@
 
     keys_in = moves(key_in, key_buf, in_sem, 0)
     values_in = moves(value_in, value_buf, in_sem, 1)
-    keys_out = moves(key_buf, key_out, out_sem, 0)
-    values_out = moves(value_buf, value_out, out_sem, 1)
-    stream = Stream([[copy] for copy in weight_copies + keys_in + values_in], AHEAD)
-
-    group_row = iota((GROUP, HD), 0)
-    places = []
-    for g in range(groups):
-        place = group_row % steps
-        for j in range(local):
-            here = group_row // steps == j
-            place = place + jnp.where(here, lens_ref[g * local + j], 0)
-        places.append(place)
-    angles = jnp.concatenate(places, axis=0).astype(F32) * freq_ref[...]
-    cosine = jnp.cos(angles)
-    sine = jnp.sin(angles)
-    sine = jnp.where(iota(sine.shape, 1) < HD // 2, -sine, sine)
-
-    rows = rows_ref[...]
+    stream = Stream([[copy] for copy in [weight_copy] + keys_in + values_in], AHEAD)
+
+    cosine, sine = rotation(lens_ref, groups, local, steps)
     stream.need(1)
-    queries = rotated(dot_nn(rows, weights[0]), cosine, sine).astype(BF16)
-    picked = iota((requests * per, rows.shape[0]), 0)
-    request, inside = picked // per, picked % per
-    source = request // local * GROUP + request % local * steps + inside % steps
-    choose = (source == iota(picked.shape, 1)).astype(BF16)
-    wide = dot_nn(choose, queries)
-    head_of = iota(wide.shape, 0) % per // steps
-    spread[...] = (
-        jnp.where(head_of == iota(wide.shape, 1) // HD, wide, 0.0)
-        .astype(BF16)
-        .reshape(requests, per, width)
-    )
-    stream.need(2)
-    new_keys[...] = rotated(dot_nn(rows, weights[1]), cosine, sine).astype(BF16).astype(F32)
-    stream.need(3)
-    new_values[...] = dot_nn(rows, weights[2]).astype(BF16).astype(F32)
-
-    patch_rows = iota((16, width), 0)
+    queries = rotated(dot_nn(rows_ref[...], weight[...]), cosine, sine).astype(BF16)
+    queries_ref[...] = queries
+    spread[...] = spread_heads(queries, requests, local, steps).reshape(requests, per, width)
 
     def slot_facts(s):
-        wanted = slot_req_ref[s]
-        request = jnp.maximum(wanted, 0)
-        base = lens_ref[request] - slot_block_ref[s] * block
-        return request, jnp.where(wanted >= 0, base, -4 * block)
-
-    def patch(buf, new, s):
-        request, base = slot_facts(s)
-
-        @pl.when((base > -steps) & (base < block))
-        def _():
-            first = request // local * GROUP + request % local * steps
-            for t in range(steps):
-                row = base + t
-
-                @pl.when((row >= 0) & (row < block))
-                def _():
-                    start = pl.multiple_of(row // 16 * 16, 16)
-                    hit = patch_rows == row - start
-                    old = buf[s, pl.ds(start, 16), :].astype(F32)
-                    fresh = new[pl.ds(first + t, 1), :]
-                    buf[s, pl.ds(start, 16), :] = jnp.where(hit, fresh, old).astype(BF16)
-
-    def patch_all(buf, new, low, high):
-        def one(s, carry):
-            patch(buf, new, s)
-            return carry
-
-        lax.fori_loop(low, high, one, 0)
+        return slot_place(lens_ref, slot_req_ref, slot_block_ref, s, block)
 
     def pairs(low, high):
         return [(s, min(s + 2, high)) for s in range(low, high, 2)]
 
     for i, (low, high) in enumerate(chunks):
-        stream.need(4 + i)
-        patch_all(key_buf, new_keys, low, high)
-        keys_out[i].start()
+        stream.need(2 + i)
         for a, b in pairs(low, high):
             left = jnp.concatenate([spread[slot_facts(s)[0]] for s in range(a, b)], axis=0)
             right = key_buf[pl.ds(a, b - a)].reshape((b - a) * block, width)
@@ -255,9 +264,9 @@
                 scores_buf[s] = both[n * per : (n + 1) * per, n * block : (n + 1) * block]
 
     scale = 1.0 / math.sqrt(HD)
-    behind = iota((per, block), 1) - iota((per, block), 0) % steps
+    position = iota((per, block), 1)
     for s in range(pool):
-        allowed = behind <= slot_facts(s)[1]
+        allowed = position < slot_facts(s)[1]
         scores = jnp.where(allowed, scores_buf[s] * scale, NEG)
         top = jnp.max(scores, axis=-1, keepdims=True)
         weight = jnp.where(allowed, jnp.exp(scores - top), 0.0)
@@ -270,11 +279,8 @@
         request = slot_facts(s)[0]
         req_max[request] = jnp.maximum(req_max[request], slot_max[s])
 
-    lane_head = iota((per, HD), 0) // steps
     for i, (low, high) in enumerate(chunks):
-        stream.need(4 + len(chunks) + i)
-        patch_all(value_buf, new_values, low, high)
-        values_out[i].start()
+        stream.need(2 + len(chunks) + i)
         for a, b in pairs(low, high):
             pieces = []
             for s in range(a, b):
@@ -284,11 +290,7 @@
             left = jnp.concatenate(pieces, axis=0)
             mixed = dot_nn(left, value_buf[pl.ds(a, b - a)].reshape((b - a) * block, width))
             for s in range(a, b):
-                mine = mixed[(s - a) * per : (s - a + 1) * per]
-                result = mine[:, :HD]
-                for h in range(1, heads):
-                    result = jnp.where(lane_head == h, mine[:, h * HD : (h + 1) * HD], result)
-                slot_out[s] = result
+                slot_out[s] = own_head(mixed[(s - a) * per : (s - a + 1) * per], steps)
 
     for s in range(pool):
         factor = jnp.exp(slot_max[s] - req_max[slot_facts(s)[0]])
@@ -323,38 +325,30 @@
             part_ref[g, pl.ds(j * per, per), :] = mean[b]
             levels = jnp.where(block_row == j, packed[b], levels)
         part_ref[g, pl.ds(local * per, 16), :] = levels.astype(BF16)
-    for copy in keys_out + values_out:
-        copy.wait()
-
-
-def attention(rows, weights, caches, lens, slot_req, slot_block, local, steps):
+
+
+def attention(rows, weight, caches, lens, slot_req, slot_block, local, steps):
     pool, block, width = caches[0].shape
     model = rows.shape[1]
     requests = lens.shape[0]
     per = width // HD * steps
     chunk_count = -(-pool // CHUNK)
-    half = HD // 2
-    frequency = np.power(10000.0, -np.arange(half, dtype=np.float64) * (2.0 / HD)).astype(np.float32)
-    frequency = np.concatenate([frequency, frequency])[None]
-    cache_shape = jax.ShapeDtypeStruct(caches[0].shape, BF16)
+    new_shape = jax.ShapeDtypeStruct((rows.shape[0], width), BF16)
     slot_stat = pltpu.VMEM((pool, per, HD), F32)
     req_stat = pltpu.VMEM((requests, per, HD), F32)
     return pl.pallas_call(
         functools.partial(attention_kernel, local, steps),
         out_shape=(
             jax.ShapeDtypeStruct((requests // local, local * per + 16, HD), BF16),
-            cache_shape,
-            cache_shape,
+            new_shape,
         ),
-        in_specs=[smem()] * 3 + [vmem()] * 2 + [hbm()] * 5,
-        out_specs=(vmem(), hbm(), hbm()),
+        in_specs=[smem()] * 3 + [vmem()] + [hbm()] * 3,
+        out_specs=(vmem(), vmem()),
         scratch_shapes=[
-            pltpu.VMEM((3, model, width), BF16),
+            pltpu.VMEM((model, width), BF16),
             pltpu.VMEM((pool, block, width), BF16),
             pltpu.VMEM((pool, block, width), BF16),
             pltpu.VMEM((requests, per, width), BF16),
-            pltpu.VMEM((rows.shape[0], width), F32),
-            pltpu.VMEM((rows.shape[0], width), F32),
             pltpu.VMEM((pool, per, block), F32),
             pltpu.VMEM((pool, per, block), BF16),
             slot_stat,
@@ -363,24 +357,153 @@
             req_stat,
             req_stat,
             req_stat,
-            pltpu.SemaphoreType.DMA((3,)),
-            pltpu.SemaphoreType.DMA((2, chunk_count)),
+            pltpu.SemaphoreType.DMA((1,)),
             pltpu.SemaphoreType.DMA((2, chunk_count)),
         ],
-        compiler_params=pltpu.CompilerParams(vmem_limit_bytes=40 * MIB),
+        compiler_params=pltpu.CompilerParams(vmem_limit_bytes=28 * MIB),
         name="attention",
     )(
         far(lens),
         far(slot_req),
         far(slot_block),
         rows,
-        jnp.asarray(frequency),
-        *[far(array) for array in weights],
+        far(weight),
         *[far(array) for array in caches],
     )
 
 
-def merge_kernel(local, steps, part_ref, weight_ref, out_ref):
+def fresh_kernel(
+    local,
+    steps,
+    lens_ref,
+    rows_ref,
+    queries_ref,
+    key_hbm,
+    value_hbm,
+    keys_ref,
+    values_ref,
+    mean_ref,
+    level_ref,
+    weights,
+    sem,
+):
+    copies = [
+        pltpu.make_async_copy(source, weights.at[n], sem.at[n])
+        for n, source in enumerate((key_hbm, value_hbm))
+    ]
+    for copy in copies:
+        copy.start()
+    groups = rows_ref.shape[0] // GROUP
+    width = keys_ref.shape[1]
+    per = width // HD * steps
+    own = pl.ds(pl.multiple_of(lax.axis_index("seq") * GROUP, GROUP), GROUP)
+    spread = spread_heads(queries_ref[own, :], local, local, steps)
+    cosine, sine = rotation(lens_ref, groups, local, steps)
+    rows = rows_ref[...]
+    for copy in copies:
+        copy.wait()
+    keys_ref[...] = rotated(dot_nn(rows, weights[0]), cosine, sine).astype(BF16)
+    values_ref[...] = dot_nn(rows, weights[1]).astype(BF16)
+    scores = dot_nt(spread, keys_ref[own, :]) * (1.0 / math.sqrt(HD))
+    row = iota(scores.shape, 0)
+    column = iota(scores.shape, 1)
+    allowed = (column // steps == row // per) & (column % steps <= row % steps)
+    scores = jnp.where(allowed, scores, NEG)
+    top = jnp.max(scores, axis=-1, keepdims=True)
+    weight = jnp.where(allowed, jnp.exp(scores - top), 0.0)
+    total = jnp.sum(weight, axis=-1, keepdims=True)
+    mixed = own_head(dot_nn(weight.astype(BF16), values_ref[own, :]), steps)
+    mean_ref[...] = mixed / total
+    level_ref[...] = jnp.broadcast_to(top + jnp.log(total), level_ref.shape)
+
+
+def fresh_rows(rows, queries, weights, lens, local, steps):
+    model, width = weights[0].shape
+    count = local * (width // HD) * steps
+    new_shape = jax.ShapeDtypeStruct((rows.shape[0], width), BF16)
+    own_shape = jax.ShapeDtypeStruct((count, HD), F32)
+    return pl.pallas_call(
+        functools.partial(fresh_kernel, local, steps),
+        out_shape=(new_shape, new_shape, own_shape, own_shape),
+        in_specs=[smem()] + [vmem()] * 2 + [hbm()] * 2,
+        out_specs=(vmem(),) * 4,
+        scratch_shapes=[pltpu.VMEM((2, model, width), BF16), pltpu.SemaphoreType.DMA((2,))],
+        compiler_params=pltpu.CompilerParams(vmem_limit_bytes=12 * MIB),
+        cost_estimate=pl.CostEstimate(
+            flops=4 * rows.shape[0] * model * width,
+            bytes_accessed=4 * model * width,
+            transcendentals=0,
+        ),
+        name="fresh_rows",
+    )(far(lens), rows, queries, *[far(array) for array in weights])
+
+
+def cache_kernel(
+    local,
+    steps,
+    lens_ref,
+    slot_req_ref,
+    slot_block_ref,
+    keys_ref,
+    values_ref,
+    _,
+    key_in,
+    value_in,
+    key_out,
+    value_out,
+    new_keys,
+    new_values,
+    key_buf,
+    value_buf,
+    in_sem,
+    out_sem,
+):
+    pool, block, _ = key_in.shape
+    cuts = [(low, min(low + CHUNK, pool)) for low in range(0, pool, CHUNK)]
+    caches = ((key_in, key_buf, key_out, new_keys), (value_in, value_buf, value_out, new_values))
+    steps_of = [(n, i) for n in range(2) for i in range(len(cuts))]
+
+    def move(source, target, sem, n, i):
+        low, high = cuts[i]
+        span = pl.ds(low, high - low)
+        return pltpu.make_async_copy(source.at[span], target.at[span], sem.at[n, i])
+
+    stream = Stream([[move(caches[n][0], caches[n][1], in_sem, n, i)] for n, i in steps_of], AHEAD)
+    outs = [move(caches[n][1], caches[n][2], out_sem, n, i) for n, i in steps_of]
+    new_keys[...] = keys_ref[...].astype(F32)
+    new_values[...] = values_ref[...].astype(F32)
+
+    def slot_facts(s):
+        return slot_place(lens_ref, slot_req_ref, slot_block_ref, s, block)
+
+    for k, (n, i) in enumerate(steps_of):
+        stream.need(k + 1)
+        patch_slots(slot_facts, local, steps, caches[n][1], caches[n][3], *cuts[i])
+        outs[k].start()
+    for copy in outs:
+        copy.wait()
+
+
+def updated_caches(caches, keys, values, lens, slot_req, slot_block, after, local, steps):
+    pool, block, width = caches[0].shape
+    cache_shape = jax.ShapeDtypeStruct(caches[0].shape, BF16)
+    return pl.pallas_call(
+        functools.partial(cache_kernel, local, steps),
+        out_shape=(cache_shape, cache_shape),
+        in_specs=[smem()] * 3 + [vmem()] * 2 + [hbm()] * 3,
+        out_specs=(hbm(), hbm()),
+        scratch_shapes=[pltpu.VMEM(keys.shape, F32)] * 2
+        + [pltpu.VMEM((pool, block, width), BF16)] * 2
+        + [pltpu.SemaphoreType.DMA((2, -(-pool // CHUNK)))] * 2,
+        compiler_params=pltpu.CompilerParams(vmem_limit_bytes=20 * MIB),
+        cost_estimate=pl.CostEstimate(
+            flops=0, bytes_accessed=4 * 2 * pool * block * width, transcendentals=0
+        ),
+        name="updated_caches",
+    )(far(lens), far(slot_req), far(slot_block), keys, values, after, *[far(array) for array in caches])
+
+
+def merge_kernel(local, steps, part_ref, mean_ref, level_ref, weight_ref, out_ref):
     holders = part_ref.shape[0]
     width = weight_ref.shape[0]
     heads = width // HD
@@ -397,6 +520,8 @@
             [jnp.broadcast_to(stat[j : j + 1], (per, HD)) for j in range(local)], axis=0
         )
         levels.append(jnp.sum(jnp.where(mine, wide, 0.0), axis=-1, keepdims=True))
+    values.append(mean_ref[...])
+    levels.append(level_ref[:, :1])
     top = functools.reduce(jnp.maximum, levels)
     shares = [jnp.exp(level - top) for level in levels]
     total = sum(shares)
@@ -413,15 +538,15 @@
     out_ref[...] = dot_nn(jnp.concatenate(parts, axis=1), weight_ref[...]).astype(BF16)
 
 
-def merge_project(parts, out_weight, local, steps):
+def merge_project(parts, mean, level, out_weight, local, steps):
     return pl.pallas_call(
         functools.partial(merge_kernel, local, steps),
         out_shape=jax.ShapeDtypeStruct((GROUP, out_weight.shape[1]), BF16),
-        in_specs=[vmem(), vmem()],
+        in_specs=[vmem()] * 4,
         out_specs=vmem(),
         compiler_params=pltpu.CompilerParams(vmem_limit_bytes=8 * MIB),
         name="merge_project",
-    )(parts, out_weight)
+    )(parts, mean, level, out_weight)
 
 
 def second_norm_kernel(hidden_ref, left_ref, right_ref, gain_ref, ids_ref, gates_ref, rows_out, res_out, rows_ref):
@@ -470,10 +595,56 @@
     return each, length
 
 
+def expert_blocks(hidden, every):
+    blocks = [(low, min(low + BLOCK, every)) for low in range(0, every, BLOCK)]
+    return blocks, min(FETCHED, sum(high <= hidden for _, high in blocks))
+
+
+def fetch_kernel(low, rows, _, gate_hbm, up_hbm, gate_ref, up_ref, sem):
+    copies = [
+        pltpu.make_async_copy(source.at[pl.ds(low, rows)], target, sem.at[n])
+        for n, (source, target) in enumerate(((gate_hbm, gate_ref), (up_hbm, up_ref)))
+    ]
+    for copy in copies:
+        copy.start()
+    for copy in copies:
+        copy.wait()
+
+
+def fetch(block, gate, up, after):
+    low, high = block
+    shape = pltpu.VMEM((high - low, gate.shape[1]), BF16)
+    return pl.pallas_call(
+        functools.partial(fetch_kernel, low, high - low),
+        out_shape=(shape, shape),
+        in_specs=[hbm()] * 3,
+        out_specs=(vmem(), vmem()),
+        scratch_shapes=[pltpu.SemaphoreType.DMA((2,))],
+        compiler_params=pltpu.CompilerParams(vmem_limit_bytes=MIB),
+        cost_estimate=pl.CostEstimate(
+            flops=0, bytes_accessed=4 * (high - low) * gate.shape[1], transcendentals=0
+        ),
+        name="fetch_weights",
+    )(after, far(gate), far(up))
+
+
 def experts_kernel(
     tokens,
     count,
     ranks,
+    fetched,
+    rows_ref,
+    *refs,
+):
+    early = [(refs[2 * i], refs[2 * i + 1]) for i in range(fetched)]
+    streamed_experts(tokens, count, ranks, early, rows_ref, *refs[2 * fetched :])
+
+
+def streamed_experts(
+    tokens,
+    count,
+    ranks,
+    early,
     rows_ref,
     gate_hbm,
     up_hbm,
@@ -491,7 +662,7 @@
     shared_sem,
 ):
     hidden, width = gate_hbm.shape
-    every = gate_ref.shape[0]
+    every = down_ref.shape[0]
     each = hidden // count
     slim, length = shared_window(shared_gate_hbm.shape[0], ranks)
     seq_rank = lax.axis_index("seq")
@@ -499,31 +670,38 @@
     slim_start = pl.multiple_of(
         jnp.minimum(slim_low // 16 * 16, shared_gate_hbm.shape[0] - length), 16
     )
-    blocks = [(low, min(low + BLOCK, every)) for low in range(0, every, BLOCK)]
-
-    def moves(source, extra, target, n):
+    blocks, _ = expert_blocks(hidden, every)
+    skipped = blocks[len(early) - 1][1] if early else 0
+
+    def moves(source, extra, target, n, skip):
         copies = []
         for i, (low, high) in enumerate(blocks):
             top = min(high, hidden)
-            piece = [
-                pltpu.make_async_copy(
-                    source.at[pl.ds(low, top - low)], target.at[pl.ds(low, top - low)], sem.at[n, i]
+            piece = []
+            if low < skip:
+                continue
+            if top > low:
+                piece.append(
+                    pltpu.make_async_copy(
+                        source.at[pl.ds(low, top - low)],
+                        target.at[pl.ds(low - skip, top - low)],
+                        sem.at[n, i],
+                    )
                 )
-            ] if top > low else []
             if high == every:
                 piece.append(
                     pltpu.make_async_copy(
                         extra.at[pl.ds(slim_start, length)],
-                        target.at[pl.ds(hidden, length)],
+                        target.at[pl.ds(hidden - skip, length)],
                         shared_sem.at[n],
                     )
                 )
             copies.append(piece)
         return copies
 
-    gates = moves(gate_hbm, shared_gate_hbm, gate_ref, 0)
-    ups = moves(up_hbm, shared_up_hbm, up_ref, 1)
-    downs = moves(down_hbm, shared_down_hbm, down_ref, 2)
+    gates = moves(gate_hbm, shared_gate_hbm, gate_ref, 0, skipped)
+    ups = moves(up_hbm, shared_up_hbm, up_ref, 1, skipped)
+    downs = moves(down_hbm, shared_down_hbm, down_ref, 2, 0)
     stream = Stream([a + b for a, b in zip(gates, ups)] + downs, 2)
 
     first = seq_rank * count
@@ -539,16 +717,21 @@
             mine = (unit >= slim_low) & (unit < slim_low + slim)
             in_shared = low + iota(share.shape, 1) >= hidden
             share = jnp.where(in_shared, mine.astype(F32), share)
-        stream.need(i + 1)
-        gate = dot_nt(rows, gate_ref[pl.ds(low, high - low), :])
-        up = dot_nt(rows, up_ref[pl.ds(low, high - low), :])
+        if i < len(early):
+            gate_block, up_block = (ref[...] for ref in early[i])
+        else:
+            stream.need(i + 1 - len(early))
+            gate_block = gate_ref[pl.ds(low - skipped, high - low), :]
+            up_block = up_ref[pl.ds(low - skipped, high - low), :]
+        gate = dot_nt(rows, gate_block)
+        up = dot_nt(rows, up_block)
         inner_ref[:, pl.ds(low, high - low)] = (jax.nn.silu(gate) * up * share).astype(BF16)
 
     groups = total_ref.shape[0] // GROUP
     pieces = out_ref.shape[0] // groups
     columns = width // pieces
     for i, (low, high) in enumerate(blocks):
-        stream.need(len(blocks) + 1 + i)
+        stream.need(len(gates) + 1 + i)
         part = inner_ref[:, pl.ds(low, high - low)]
         for p in range(pieces):
             cut = pl.ds(p * columns, columns)
@@ -562,27 +745,32 @@
                     out_ref[g * pieces + p] = sums[g * GROUP : g * GROUP + tokens].astype(BF16)
 
 
-def all_experts(rows, routed, shared, tokens, pieces):
+def all_experts(rows, early, routed, shared, tokens, pieces):
     count, each, width = routed[2].shape
     hidden = count * each
     groups = rows.shape[0] // GROUP
     every = hidden + shared_window(shared[2].shape[0], groups)[1]
     routed = [array.reshape(hidden, width) for array in routed]
+    early = [array for pair in early for array in pair]
+    rest = every - sum(array.shape[0] for array in early) // 2
     return pl.pallas_call(
-        functools.partial(experts_kernel, tokens, count, groups),
+        functools.partial(experts_kernel, tokens, count, groups, len(early) // 2),
         out_shape=jax.ShapeDtypeStruct((groups * pieces, tokens, width // pieces), BF16),
-        in_specs=[vmem()] + [hbm()] * 6,
+        in_specs=[vmem()] * (1 + len(early)) + [hbm()] * 6,
         out_specs=vmem(),
-        scratch_shapes=[pltpu.VMEM((every, width), BF16)] * 3
+        scratch_shapes=[pltpu.VMEM((rest, width), BF16)] * 2
         + [
+            pltpu.VMEM((every, width), BF16),
             pltpu.VMEM((rows.shape[0], every), BF16),
             pltpu.VMEM((rows.shape[0], width), F32),
             pltpu.SemaphoreType.DMA((3, -(-every // BLOCK))),
             pltpu.SemaphoreType.DMA((3,)),
         ],
-        compiler_params=pltpu.CompilerParams(vmem_limit_bytes=56 * MIB),
+        compiler_params=pltpu.CompilerParams(
+            vmem_limit_bytes=(2 * rest + every) * width * 2 + 8 * MIB
+        ),
         name="experts",
-    )(rows, *[far(array) for array in (*routed, *shared)])
+    )(rows, *[near(array) for array in early], *[far(array) for array in (*routed, *shared)])
 
 
 def last_kernel(res_ref, parts_ref, out_ref):
@@ -640,9 +828,9 @@
 
     normed = norm_rows(hidden_in, attn_gain)
     rows = lax.all_gather(normed, "seq", axis=0, tiled=True)
-    parts, key_out, value_out = attention(
+    parts, queries = attention(
         rows,
-        (query_weight, key_weight, value_weight),
+        query_weight,
         (key_cache, value_cache),
         cache_lens,
         slot_request,
@@ -651,23 +839,49 @@
         steps,
     )
     parts = lax.all_to_all(parts, "seq", split_axis=0, concat_axis=0, tiled=True)
-    terms = merge_project(parts, out_weight, local, steps)
+    new_keys, new_values, mean, level = fresh_rows(
+        rows, queries, (key_weight, value_weight), cache_lens, local, steps
+    )
+    terms = merge_project(parts, mean, level, out_weight, local, steps)
+    gate_rows = jnp.swapaxes(gate_experts, 1, 2).reshape(-1, width)
+    up_rows = jnp.swapaxes(up_experts, 1, 2).reshape(-1, width)
+    hidden = gate_rows.shape[0]
+    extra = shared_window(down_shared.shape[0], lax.axis_size("seq"))[1]
+    blocks, fetched = expert_blocks(hidden, hidden + extra)
+    early = []
     other = partner(terms, "exp", 1)
     bit = 2
     while bit < exp_count:
+        if len(early) < fetched:
+            early.append(fetch(blocks[len(early)], gate_rows, up_rows, terms))
+            other, early[-1] = lax.optimization_barrier((other, early[-1]))
         terms = (terms.astype(F32) + other.astype(F32)).astype(BF16)
         other = partner(terms, "exp", bit)
         bit *= 2
+    while len(early) < fetched:
+        early.append(fetch(blocks[len(early)], gate_rows, up_rows, terms))
     ffn_in, residual = second_norm(
         hidden_in, terms, other, ffn_gain, expert_ids, expert_weights
     )
     all_rows = lax.all_gather(ffn_in, "seq", axis=0, tiled=True)
     sums = all_experts(
         all_rows,
+        early,
         (jnp.swapaxes(gate_experts, 1, 2), jnp.swapaxes(up_experts, 1, 2), down_experts),
         (jnp.swapaxes(gate_shared, 0, 1), jnp.swapaxes(up_shared, 0, 1), down_shared),
         tokens,
         exp_count,
+    )
+    key_out, value_out = updated_caches(
+        (key_cache, value_cache),
+        new_keys,
+        new_values,
+        cache_lens,
+        slot_request,
+        slot_block,
+        sums,
+        local,
+        steps,
     )
     sums = lax.all_to_all(sums, ("seq", "exp"), split_axis=0, concat_axis=0, tiled=True)
     hidden_out = last_sum(residual, sums, local, steps)

time: 92.9 us -> 85 us (0.915)
  blocking collectives: 52.9 us -> 21.8 us
  Pallas kernels: 31 us -> 42.9 us
  starting transfers between devices: 3.75 us -> 12.1 us
  waiting for transfers between devices: 3.46 us -> 6.81 us
    all_to_all x2 -> x0, blocking collectives: 28.5 us -> none  [the longest x1 20.8 us: body(): lax.all_to_all(sums, ('seq', 'exp'), split_axis=0, concat_axis=0, tiled=T...]
    pallas_call x1 -> x5, Pallas kernels: 16.5 us -> 31.5 us  [the longest x1 12.6 us: all_experts(): pl.pallas_call(functools.partial(experts_kernel, tokens, count, groups, l...]
    all_to_all x0 -> x2, starting transfers between devices: none -> 8.45 us  [the longest x1 4.89 us: body(): lax.all_to_all(sums, ('seq', 'exp'), split_axis=0, concat_axis=0, tiled=T...]
    all_to_all x0 -> x2, waiting for transfers between devices: none -> 6.8 us  [the longest x1 5.98 us: body(): lax.all_to_all(sums, ('seq', 'exp'), split_axis=0, concat_axis=0, tiled=T...]
    ppermute x2, waiting for transfers between devices: 3.46 us -> 0.01 us  [partner(): return lax.ppermute(array, axis, [(i, i ^ bit) for i in range(count)])]
    pallas_call x1, Pallas kernels: 12 us -> 8.83 us  [attention(): pl.pallas_call(functools.partial(attention_kernel, local, steps), out_sha...]
    all_gather x1, blocking collectives: 13.2 us -> 10.6 us  [body(): all_rows = lax.all_gather(ffn_in, 'seq', axis=0, tiled=True)]
  transfers between devices with their start and end apart: 2 -> 4, of which waited for: 2 -> 2; matrix products, arithmetic and copies ran while one was open for 0% -> 0% of each run, Pallas kernels for 0% -> 22%
where the time goes in v3:
time: 85 us; the launch traced here: 84.5 us
  Pallas kernels  42.9 us (50%)
  blocking collectives  21.8 us (26%)
  starting transfers between devices  12.1 us (14%)
  waiting for transfers between devices  6.81 us (8%)
    pallas_call x1, Pallas kernels, all_experts(): pl.pallas_call(functools.partial(experts_kernel, tokens, count, groups, l...  12.6 us
    all_gather x1, blocking collectives, body(): rows = lax.all_gather(normed, 'seq', axis=0, tiled=True)  11.2 us
    all_gather x1, blocking collectives, body(): all_rows = lax.all_gather(ffn_in, 'seq', axis=0, tiled=True)  10.6 us
    pallas_call x1, Pallas kernels, updated_caches(): pl.pallas_call(functools.partial(cache_kernel, local, steps), out_shape=(...  9.31 us
    pallas_call x1, Pallas kernels, attention(): pl.pallas_call(functools.partial(attention_kernel, local, steps), out_sha...  8.83 us
    all_to_all x1, waiting for transfers between devices, body(): lax.all_to_all(sums, ('seq', 'exp'), split_axis=0, concat_axis=0, tiled=T...  5.98 us
    pallas_call x2, Pallas kernels, fetch(): pl.pallas_call(functools.partial(fetch_kernel, low, high - low), out_shap...  5.72 us
    all_to_all x1, starting transfers between devices, body(): lax.all_to_all(sums, ('seq', 'exp'), split_axis=0, concat_axis=0, tiled=T...  4.89 us
  transfers between devices with their start and end apart: 4, of which 2 were waited for; matrix products, arithmetic and copies ran while one was open for 0% of the time, Pallas kernels for 22%

profile of v3, /device:TPU:1, one launch (start us, length us, event | category | flops | bytes accessed | tf_op | source)
XLA Modules:
  0.0 84.5 jit_solution(15907214869803262031)
XLA Ops:
  0.6 1.0 %norm_rows.1 = bf16[16,2048]{1,0:T(8,128)(2,1)S(1)} custom-call(f32[3,4,2048]{2,1,0:T(4,128)} %hidden_ref.1, f32[1,2048]{1,0:T(1,128)} %bitcast.21), custom_call_target="tpu_custom_call" | custom-call | tf_op jit(solution)/shard_map/norm_rows/pallas_call | solution.py:98
  1.7 11.2 %all_gather.6.rows_ref = bf16[128,2048]{1,0:T(8,128)(2,1)S(1)} all-gather(bf16[16,2048]{1,0:T(8,128)(2,1)S(1)} %norm_rows.1), channel_id=1, replica_groups=mesh['seq'=8,'exp'=4] {'seq'}, dimensions={0}, use_global_device_ids=true | all-gather | bytes 589824 | tf_op jit(solution)/shard_map/all_gather | solution.py:830
  12.9 8.8 %attention.1 = (bf16[8,64,128]{2,1,0:T(8,128)(2,1)}, bf16[128,512]{1,0:T(8,128)(2,1)S(1)}) custom-call(s32[24]{0:T(128)} %lens_ref.5, s32[46]{0:T(128)} %slot_req_ref.3, s32[46]{0:T(128)} %slot_block_ref.3, bf16[128,2048]{1,0:T(8,128)(2,1)S(1)} %all_gather.6.rows_ref, bf16[2048,512]{1,0:T(8,128)(2,1)} %query_hbm.1, bf16[46,128,512]{2,1,0:T(8,128)(2,1)} %key_in.3, ...), custom_call_target="tpu_custom_call" | custom-call | tf_op jit(solution)/shard_map/attention/pallas_call | solution.py:339
  21.7 0.0 copy-start
  21.7 3.6 %all-to-all-start = ((bf16[8,64,128]{2,1,0:T(8,128)(2,1)}), bf16[8,64,128]{2,1,0:T(8,128)(2,1)S(1)}, u32[]{:S(2)}, u32[]{:S(2)}) async-start(bf16[8,64,128]{2,1,0:T(8,128)(2,1)} %get-tuple-element.20), calls=%async_computation | async-start | bytes 262144 | tf_op jit(solution)/shard_map/all_to_all | solution.py:841
  25.3 3.9 %fresh_rows.1 = (bf16[128,512]{1,0:T(8,128)(2,1)S(1)}, bf16[128,512]{1,0:T(8,128)(2,1)S(1)}, f32[48,128]{1,0:T(8,128)S(1)}, f32[48,128]{1,0:T(8,128)S(1)}) custom-call(s32[24]{0:T(128)} %lens_ref.5, bf16[128,2048]{1,0:T(8,128)(2,1)S(1)} %all_gather.6.rows_ref, bf16[128,512]{1,0:T(8,128)(2,1)S(1)} %get-tuple-element.21.queries_ref, ...), custom_call_target="tpu_custom_call" | custom-call | flops 536870912 | bytes 4194304 | tf_op jit(solution)/shard_map/fresh_rows/pallas_call | solution.py:425
  29.2 0.8 all-to-all-done.part_ref
  30.0 0.0 copy-done
  30.0 0.7 merge_project.1._
  30.7 1.3 %collective-permute-start = (bf16[16,2048]{1,0:T(8,128)(2,1)S(1)}, bf16[16,2048]{1,0:T(8,128)(2,1)S(1)}, u32[]{:S(2)}, u32[]{:S(2)}) collective-permute-start(bf16[16,2048]{1,0:T(8,128)(2,1)S(1)} %merge_project.1._), channel_id=1, source_target_pairs={{0,1},{1,0},{2,3},{3,2},{4,5},{5,4},{6,7},{7,6},{8,9},{9,8},{10,11... | collective-permute-start | bytes 196616 | tf_op jit(solution)/shard_map/ppermute | solution.py:800
  32.1 2.9 %fetch_weights.2 = (bf16[768,2048]{1,0:T(8,128)(2,1)S(1)}, bf16[768,2048]{1,0:T(8,128)(2,1)S(1)}) custom-call(bf16[16,2048]{1,0:T(8,128)(2,1)S(1)} %merge_project.1._, bf16[2816,2048]{1,0:T(8,128)(2,1)} %bitcast.12, bf16[2816,2048]{1,0:T(8,128)(2,1)} %bitcast.15), custom_call_target="tpu_custom_call" | custom-call | bytes 6291456 | tf_op jit(solution)/shard_map/fetch_weights/pallas_call | solution.py:617
  34.9 0.0 collective-permute-done
  35.0 0.0 copy-start.1
  35.0 0.0 copy-start.2
  35.0 0.0 copy-start.3
  35.0 0.0 copy-start.4
  35.0 2.4 %collective-permute-start.1 = (bf16[16,2048]{1,0:T(8,128)(2,1)S(1)}, bf16[16,2048]{1,0:T(8,128)(2,1)S(1)}, u32[]{:S(2)}, u32[]{:S(2)}) collective-permute-start(bf16[16,2048]{1,0:T(8,128)(2,1)S(1)} %add_convert_fusion.left_ref._), channel_id=1, source_target_pairs={{0,2},{1,3},{2,0},{3,1},{4,6},{5,7},{6,4},{7,5},{8,10},{9,11},{10,... | collective-permute-start | bytes 196616 | tf_op jit(solution)/shard_map/ppermute | solution.py:800
  37.4 2.9 %fetch_weights.3 = (bf16[768,2048]{1,0:T(8,128)(2,1)S(1)}, bf16[768,2048]{1,0:T(8,128)(2,1)S(1)}) custom-call(bf16[16,2048]{1,0:T(8,128)(2,1)S(1)} %add_convert_fusion.left_ref._, bf16[2816,2048]{1,0:T(8,128)(2,1)} %bitcast.13, bf16[2816,2048]{1,0:T(8,128)(2,1)} %bitcast.16), custom_call_target="tpu_custom_call" | custom-call | bytes 6291456 | tf_op jit(solution)/shard_map/fetch_weights/pallas_call | solution.py:617
  40.3 0.0 collective-permute-done.1.right_ref
  40.3 0.0 copy-done.1
  40.3 0.0 copy-done.2
  40.3 0.0 copy-done.3
  40.3 0.0 copy-done.4
  40.3 0.2 second_norm.1
  40.5 10.6 %all_gather.7.rows_ref = bf16[128,2176]{1,0:T(8,128)(2,1)S(1)} all-gather(bf16[16,2176]{1,0:T(8,128)(2,1)S(1)} %get-tuple-element.28), channel_id=1, replica_groups=mesh['seq'=8,'exp'=4] {'seq'}, dimensions={0}, use_global_device_ids=true | all-gather | bytes 626688 | tf_op jit(solution)/shard_map/all_gather | solution.py:866
  51.1 12.6 %experts.1._ = bf16[32,12,512]{2,1,0:T(8,128)(2,1)} custom-call(bf16[128,2176]{1,0:T(8,128)(2,1)S(1)} %all_gather.7.rows_ref, bf16[768,2048]{1,0:T(8,128)(2,1)S(1)} %get-tuple-element.29.refs_0_, bf16[768,2048]{1,0:T(8,128)(2,1)S(1)} %get-tuple-element.30.refs_1_, bf16[768,2048]{1,0:T(8,128)(2,1)S(1)} %get-tuple-element.31.refs_2_, ...), custom_call_target="tpu_custom_call" | custom-call | tf_op jit(solution)/shard_map/experts/pallas_call | solution.py:756
  63.6 4.9 %all-to-all-start.1 = ((bf16[32,12,512]{2,1,0:T(8,128)(2,1)}), bf16[32,12,512]{2,1,0:T(8,128)(2,1)S(1)}, u32[]{:S(2)}, u32[]{:S(2)}) async-start(bf16[32,12,512]{2,1,0:T(8,128)(2,1)} %experts.1._), calls=%async_computation.1 | async-start | bytes 1048576 | tf_op jit(solution)/shard_map/all_to_all | solution.py:886
  68.5 9.3 %updated_caches.1 = (bf16[46,128,512]{2,1,0:T(8,128)(2,1)}, bf16[46,128,512]{2,1,0:T(8,128)(2,1)}) custom-call(s32[24]{0:T(128)} %lens_ref.5, s32[46]{0:T(128)} %slot_req_ref.3, s32[46]{0:T(128)} %slot_block_ref.3, bf16[128,512]{1,0:T(8,128)(2,1)S(1)} %get-tuple-element.33.keys_ref, bf16[128,512]{1,0:T(8,128)(2,1)S(1)} %get-tuple-element.34.values_ref, ...), custom_call_target="tpu_custom_call" | custom-call | bytes 24117248 | tf_op jit(solution)/shard_map/updated_caches/pallas_call | solution.py:490
  77.8 6.0 %all-to-all-done.1.parts_ref = bf16[32,12,512]{2,1,0:T(8,128)(2,1)S(1)} async-done(((bf16[32,12,512]{2,1,0:T(8,128)(2,1)}), bf16[32,12,512]{2,1,0:T(8,128)(2,1)S(1)}, u32[]{:S(2)}, u32[]{:S(2)}) %all-to-all-start.1) | async-done | bytes 393248 | tf_op jit(solution)/shard_map/all_to_all | solution.py:886
  83.8 0.7 last_sum.1
  (1 shorter events, 0.0 us)
Async XLA Ops:
  21.7 8.3 %copy-start = (bf16[512,2048]{1,0:T(8,128)(2,1)S(1)}, bf16[512,2048]{1,0:T(8,128)(2,1)}, u32[]{:S(2)}) copy-start(bf16[512,2048]{1,0:T(8,128)(2,1)} %weight_ref.1) | copy-start | bytes 6291460
  21.7 8.3 %all-to-all-start = ((bf16[8,64,128]{2,1,0:T(8,128)(2,1)}), bf16[8,64,128]{2,1,0:T(8,128)(2,1)S(1)}, u32[]{:S(2)}, u32[]{:S(2)}) async-start(bf16[8,64,128]{2,1,0:T(8,128)(2,1)} %get-tuple-element.20), calls=%async_computation | async-start | bytes 262144 | tf_op jit(solution)/shard_map/all_to_all | solution.py:841
  30.7 4.2 %collective-permute-start = (bf16[16,2048]{1,0:T(8,128)(2,1)S(1)}, bf16[16,2048]{1,0:T(8,128)(2,1)S(1)}, u32[]{:S(2)}, u32[]{:S(2)}) collective-permute-start(bf16[16,2048]{1,0:T(8,128)(2,1)S(1)} %merge_project.1._), channel_id=1, source_target_pairs={{0,1},{1,0},{2,3},{3,2},{4,5},{5,4},{6,7},{7,6},{8,9},{9,8},{10,11... | collective-permute-start | bytes 196616 | tf_op jit(solution)/shard_map/ppermute | solution.py:800
  35.0 5.3 %copy-start.1 = (f32[3,4,2048]{2,1,0:T(4,128)S(1)}, f32[3,4,2048]{2,1,0:T(4,128)}, u32[]{:S(2)}) copy-start(f32[3,4,2048]{2,1,0:T(4,128)} %hidden_ref.1) | copy-start | bytes 294916
  35.0 5.3 %copy-start.2 = (f32[2048]{0:T(1024)S(1)}, f32[2048]{0:T(1024)}, u32[]{:S(2)}) copy-start(f32[2048]{0:T(1024)} %param.31) | copy-start | bytes 24580
  35.0 5.3 %copy-start.3 = (s32[3,4,6]{2,1,0:T(4,128)S(1)}, s32[3,4,6]{2,1,0:T(4,128)}, u32[]{:S(2)}) copy-start(s32[3,4,6]{2,1,0:T(4,128)} %ids_ref.1) | copy-start | bytes 868
  35.0 5.3 %copy-start.4 = (f32[3,4,6]{2,1,0:T(4,128)S(1)}, f32[3,4,6]{2,1,0:T(4,128)}, u32[]{:S(2)}) copy-start(f32[3,4,6]{2,1,0:T(4,128)} %gates_ref.1) | copy-start | bytes 868
  35.0 5.3 %collective-permute-start.1 = (bf16[16,2048]{1,0:T(8,128)(2,1)S(1)}, bf16[16,2048]{1,0:T(8,128)(2,1)S(1)}, u32[]{:S(2)}, u32[]{:S(2)}) collective-permute-start(bf16[16,2048]{1,0:T(8,128)(2,1)S(1)} %add_convert_fusion.left_ref._), channel_id=1, source_target_pairs={{0,2},{1,3},{2,0},{3,1},{4,6},{5,7},{6,4},{7,5},{8,10},{9,11},{10,... | collective-permute-start | bytes 196616 | tf_op jit(solution)/shard_map/ppermute | solution.py:800
  63.6 20.2 %all-to-all-start.1 = ((bf16[32,12,512]{2,1,0:T(8,128)(2,1)}), bf16[32,12,512]{2,1,0:T(8,128)(2,1)S(1)}, u32[]{:S(2)}, u32[]{:S(2)}) async-start(bf16[32,12,512]{2,1,0:T(8,128)(2,1)} %experts.1._), calls=%async_computation.1 | async-start | bytes 1048576 | tf_op jit(solution)/shard_map/all_to_all | solution.py:886

commit v4 on v3

--- a/solution.py
+++ b/solution.py
@@ -14,8 +14,8 @@
 GROUP = 16
 BLOCK = 768
 FETCHED = 2
-AHEAD = 3
-CHUNK = 16
+AHEAD = 2
+CHUNK = 46
 NEG = -1e30
 MIB = 1 << 20
 F32 = jnp.float32
@@ -196,9 +196,9 @@
 def attention_kernel(
     local,
     steps,
-    lens_ref,
-    slot_req_ref,
-    slot_block_ref,
+    lens_hbm,
+    slot_req_hbm,
+    slot_block_hbm,
     rows_ref,
     query_hbm,
     key_in,
@@ -217,8 +217,12 @@
     req_max,
     req_total,
     req_out,
+    lens_ref,
+    slot_req_ref,
+    slot_block_ref,
     weight_sem,
     in_sem,
+    small_sem,
 ):
     pool, block, width = key_buf.shape
     heads = width // HD
@@ -239,7 +243,21 @@
 
     keys_in = moves(key_in, key_buf, in_sem, 0)
     values_in = moves(value_in, value_buf, in_sem, 1)
+    small_copies = [
+        pltpu.make_async_copy(source, target, small_sem.at[i])
+        for i, (source, target) in enumerate(
+            (
+                (lens_hbm, lens_ref),
+                (slot_req_hbm, slot_req_ref),
+                (slot_block_hbm, slot_block_ref),
+            )
+        )
+    ]
+    for copy in small_copies:
+        copy.start()
     stream = Stream([[copy] for copy in [weight_copy] + keys_in + values_in], AHEAD)
+    for copy in small_copies:
+        copy.wait()
 
     cosine, sine = rotation(lens_ref, groups, local, steps)
     stream.need(1)
@@ -342,7 +360,7 @@
             jax.ShapeDtypeStruct((requests // local, local * per + 16, HD), BF16),
             new_shape,
         ),
-        in_specs=[smem()] * 3 + [vmem()] + [hbm()] * 3,
+        in_specs=[hbm()] * 3 + [vmem()] + [hbm()] * 3,
         out_specs=(vmem(), vmem()),
         scratch_shapes=[
             pltpu.VMEM((model, width), BF16),
@@ -357,8 +375,12 @@
             req_stat,
             req_stat,
             req_stat,
+            pltpu.SMEM(lens.shape, jnp.int32),
+            pltpu.SMEM(slot_req.shape, jnp.int32),
+            pltpu.SMEM(slot_block.shape, jnp.int32),
             pltpu.SemaphoreType.DMA((1,)),
             pltpu.SemaphoreType.DMA((2, chunk_count)),
+            pltpu.SemaphoreType.DMA((3,)),
         ],
         compiler_params=pltpu.CompilerParams(vmem_limit_bytes=28 * MIB),
         name="attention",
@@ -628,6 +650,10 @@
     )(after, far(gate), far(up))
 
 
+def packs(tokens, columns):
+    return tokens == 12 and columns == 4 * HD
+
+
 def experts_kernel(
     tokens,
     count,
@@ -740,6 +766,16 @@
                 sums = sums + total_ref[:, cut]
             if i < len(blocks) - 1:
                 total_ref[:, cut] = sums
+            elif packs(tokens, columns):
+                last = sums[:, 3 * HD :]
+                body_row = iota(last.shape, 0) % GROUP < tokens
+                for c in range(3):
+                    moved = pltpu.roll(last, tokens - 4 * c, 0)
+                    tile = jnp.where(body_row, sums[:, c * HD : (c + 1) * HD], moved).astype(BF16)
+                    for g in range(groups):
+                        out_ref[g * pieces + p, pl.ds(c * GROUP, GROUP), :] = tile[
+                            g * GROUP : (g + 1) * GROUP
+                        ]
             else:
                 for g in range(groups):
                     out_ref[g * pieces + p] = sums[g * GROUP : g * GROUP + tokens].astype(BF16)
@@ -752,10 +788,13 @@
     every = hidden + shared_window(shared[2].shape[0], groups)[1]
     routed = [array.reshape(hidden, width) for array in routed]
     early = [array for pair in early for array in pair]
+    shape = (tokens, width // pieces)
+    if packs(*shape):
+        shape = (3 * GROUP, HD)
     rest = every - sum(array.shape[0] for array in early) // 2
     return pl.pallas_call(
         functools.partial(experts_kernel, tokens, count, groups, len(early) // 2),
-        out_shape=jax.ShapeDtypeStruct((groups * pieces, tokens, width // pieces), BF16),
+        out_shape=jax.ShapeDtypeStruct((groups * pieces, *shape), BF16),
         in_specs=[vmem()] * (1 + len(early)) + [hbm()] * 6,
         out_specs=vmem(),
         scratch_shapes=[pltpu.VMEM((rest, width), BF16)] * 2
@@ -778,16 +817,23 @@
     total = parts_ref[0].astype(F32)
     for i in range(1, parts_ref.shape[0]):
         total = total + parts_ref[i].astype(F32)
-    start = pl.multiple_of(lax.axis_index("exp") * columns, HD)
-    total = total + res_ref[pl.ds(0, local * steps), pl.ds(start, columns)]
+    cut = pl.ds(pl.multiple_of(lax.axis_index("exp") * columns, HD), columns)
     for j in range(local):
-        out_ref[j] = total[j * steps : (j + 1) * steps]
-
-
-def last_sum(residual, parts, local, steps):
+        rows = slice(j * steps, (j + 1) * steps)
+        own = res_ref[pl.ds(j * steps, steps), cut]
+        if packs(local * steps, columns):
+            for c in range(4):
+                start = c * GROUP + j * steps if c < 3 else j * GROUP + local * steps
+                lanes = slice(c * HD, (c + 1) * HD)
+                out_ref[j, :, lanes] = own[:, lanes] + total[start : start + steps]
+        else:
+            out_ref[j] = own + total[rows]
+
+
+def last_sum(residual, parts, local, steps, columns):
     return pl.pallas_call(
         last_kernel,
-        out_shape=jax.ShapeDtypeStruct((local, steps, parts.shape[2]), F32),
+        out_shape=jax.ShapeDtypeStruct((local, steps, columns), F32),
         in_specs=[vmem(), vmem()],
         out_specs=vmem(),
         compiler_params=pltpu.CompilerParams(vmem_limit_bytes=8 * MIB),
@@ -884,7 +930,7 @@
         steps,
     )
     sums = lax.all_to_all(sums, ("seq", "exp"), split_axis=0, concat_axis=0, tiled=True)
-    hidden_out = last_sum(residual, sums, local, steps)
+    hidden_out = last_sum(residual, sums, local, steps, width // exp_count)
     return hidden_out, key_out, value_out
 
 

time: 85 us -> 81.1 us (0.954)
  waiting for transfers between devices: 6.81 us -> 4.5 us
  Pallas kernels: 42.9 us -> 41.4 us
    all_to_all x1, waiting for transfers between devices: 5.98 us -> 3.68 us  [body(): lax.all_to_all(sums, ('seq', 'exp'), split_axis=0, concat_axis=0, tiled=T...]
    pallas_call x1, Pallas kernels: 8.83 us -> 7.52 us  [attention(): pl.pallas_call(functools.partial(attention_kernel, local, steps), out_sha...]
  transfers between devices with their start and end apart: 4 -> 4, of which waited for: 2 -> 2; matrix products, arithmetic and copies ran while one was open for 0% -> 0% of each run, Pallas kernels for 22% -> 23%
where the time goes in v4:
time: 81.1 us; the launch traced here: 80.7 us
  Pallas kernels  41.4 us (51%)
  blocking collectives  21.8 us (27%)
  starting transfers between devices  12.2 us (15%)
  waiting for transfers between devices  4.5 us (6%)
    pallas_call x1, Pallas kernels, all_experts(): pl.pallas_call(functools.partial(experts_kernel, tokens, count, groups, l...  12.5 us
    all_gather x1, blocking collectives, body(): rows = lax.all_gather(normed, 'seq', axis=0, tiled=True)  11.2 us
    all_gather x1, blocking collectives, body(): all_rows = lax.all_gather(ffn_in, 'seq', axis=0, tiled=True)  10.6 us
    pallas_call x1, Pallas kernels, updated_caches(): pl.pallas_call(functools.partial(cache_kernel, local, steps), out_shape=(...  9.06 us
    pallas_call x1, Pallas kernels, attention(): pl.pallas_call(functools.partial(attention_kernel, local, steps), out_sha...  7.52 us
    pallas_call x2, Pallas kernels, fetch(): pl.pallas_call(functools.partial(fetch_kernel, low, high - low), out_shap...  5.72 us
    all_to_all x1, starting transfers between devices, body(): lax.all_to_all(sums, ('seq', 'exp'), split_axis=0, concat_axis=0, tiled=T...  4.89 us
    pallas_call x1, Pallas kernels, fresh_rows(): pl.pallas_call(functools.partial(fresh_kernel, local, steps), out_shape=(...  3.87 us
  transfers between devices with their start and end apart: 4, of which 2 were waited for; matrix products, arithmetic and copies ran while one was open for 0% of the time, Pallas kernels for 23%

profile of v4, /device:TPU:1, one launch (start us, length us, event | category | flops | bytes accessed | tf_op | source)
XLA Modules:
  0.0 80.7 jit_solution(18446121273086897576)
XLA Ops:
  0.6 1.0 %norm_rows.1 = bf16[16,2048]{1,0:T(8,128)(2,1)S(1)} custom-call(f32[3,4,2048]{2,1,0:T(4,128)} %hidden_ref.1, f32[1,2048]{1,0:T(1,128)} %bitcast.21), custom_call_target="tpu_custom_call" | custom-call | tf_op jit(solution)/shard_map/norm_rows/pallas_call | solution.py:98
  1.7 11.2 %all_gather.6.rows_ref = bf16[128,2048]{1,0:T(8,128)(2,1)S(1)} all-gather(bf16[16,2048]{1,0:T(8,128)(2,1)S(1)} %norm_rows.1), channel_id=1, replica_groups=mesh['seq'=8,'exp'=4] {'seq'}, dimensions={0}, use_global_device_ids=true | all-gather | bytes 589824 | tf_op jit(solution)/shard_map/all_gather | solution.py:876
  12.9 7.5 %attention.1 = (bf16[8,64,128]{2,1,0:T(8,128)(2,1)}, bf16[128,512]{1,0:T(8,128)(2,1)S(1)}) custom-call(s32[24]{0:T(128)} %lens_ref.3, s32[46]{0:T(128)} %slot_req_ref.1, s32[46]{0:T(128)} %slot_block_ref.1, bf16[128,2048]{1,0:T(8,128)(2,1)S(1)} %all_gather.6.rows_ref, bf16[2048,512]{1,0:T(8,128)(2,1)} %query_hbm.1, bf16[46,128,512]{2,1,0:T(8,128)(2,1)} %key_in.3, ...), custom_call_target="tpu_custom_call" | custom-call | tf_op jit(solution)/shard_map/attention/pallas_call | solution.py:357
  20.4 0.0 copy-start
  20.4 3.6 %all-to-all-start = ((bf16[8,64,128]{2,1,0:T(8,128)(2,1)}), bf16[8,64,128]{2,1,0:T(8,128)(2,1)S(1)}, u32[]{:S(2)}, u32[]{:S(2)}) async-start(bf16[8,64,128]{2,1,0:T(8,128)(2,1)} %get-tuple-element.20), calls=%async_computation | async-start | bytes 262144 | tf_op jit(solution)/shard_map/all_to_all | solution.py:887
  24.0 3.9 %fresh_rows.1 = (bf16[128,512]{1,0:T(8,128)(2,1)S(1)}, bf16[128,512]{1,0:T(8,128)(2,1)S(1)}, f32[48,128]{1,0:T(8,128)S(1)}, f32[48,128]{1,0:T(8,128)S(1)}) custom-call(s32[24]{0:T(128)} %lens_ref.3, bf16[128,2048]{1,0:T(8,128)(2,1)S(1)} %all_gather.6.rows_ref, bf16[128,512]{1,0:T(8,128)(2,1)S(1)} %get-tuple-element.21.queries_ref, ...), custom_call_target="tpu_custom_call" | custom-call | flops 536870912 | bytes 4194304 | tf_op jit(solution)/shard_map/fresh_rows/pallas_call | solution.py:447
  27.9 0.8 %all-to-all-done.part_ref = bf16[8,64,128]{2,1,0:T(8,128)(2,1)S(1)} async-done(((bf16[8,64,128]{2,1,0:T(8,128)(2,1)}), bf16[8,64,128]{2,1,0:T(8,128)(2,1)S(1)}, u32[]{:S(2)}, u32[]{:S(2)}) %all-to-all-start) | async-done | bytes 131104 | tf_op jit(solution)/shard_map/all_to_all | solution.py:887
  28.7 0.0 copy-done
  28.7 0.7 merge_project.1._
  29.5 1.3 %collective-permute-start = (bf16[16,2048]{1,0:T(8,128)(2,1)S(1)}, bf16[16,2048]{1,0:T(8,128)(2,1)S(1)}, u32[]{:S(2)}, u32[]{:S(2)}) collective-permute-start(bf16[16,2048]{1,0:T(8,128)(2,1)S(1)} %merge_project.1._), channel_id=1, source_target_pairs={{0,1},{1,0},{2,3},{3,2},{4,5},{5,4},{6,7},{7,6},{8,9},{9,8},{10,11... | collective-permute-start | bytes 196616 | tf_op jit(solution)/shard_map/ppermute | solution.py:846
  30.8 2.9 %fetch_weights.2 = (bf16[768,2048]{1,0:T(8,128)(2,1)S(1)}, bf16[768,2048]{1,0:T(8,128)(2,1)S(1)}) custom-call(bf16[16,2048]{1,0:T(8,128)(2,1)S(1)} %merge_project.1._, bf16[2816,2048]{1,0:T(8,128)(2,1)} %bitcast.12, bf16[2816,2048]{1,0:T(8,128)(2,1)} %bitcast.15), custom_call_target="tpu_custom_call" | custom-call | bytes 6291456 | tf_op jit(solution)/shard_map/fetch_weights/pallas_call | solution.py:639
  33.6 0.0 collective-permute-done
  33.7 0.0 copy-start.1
  33.7 0.0 copy-start.2
  33.7 0.0 copy-start.3
  33.7 0.0 copy-start.4
  33.7 2.4 %collective-permute-start.1 = (bf16[16,2048]{1,0:T(8,128)(2,1)S(1)}, bf16[16,2048]{1,0:T(8,128)(2,1)S(1)}, u32[]{:S(2)}, u32[]{:S(2)}) collective-permute-start(bf16[16,2048]{1,0:T(8,128)(2,1)S(1)} %add_convert_fusion.left_ref._), channel_id=1, source_target_pairs={{0,2},{1,3},{2,0},{3,1},{4,6},{5,7},{6,4},{7,5},{8,10},{9,11},{10,... | collective-permute-start | bytes 196616 | tf_op jit(solution)/shard_map/ppermute | solution.py:846
  36.1 2.9 %fetch_weights.3 = (bf16[768,2048]{1,0:T(8,128)(2,1)S(1)}, bf16[768,2048]{1,0:T(8,128)(2,1)S(1)}) custom-call(bf16[16,2048]{1,0:T(8,128)(2,1)S(1)} %add_convert_fusion.left_ref._, bf16[2816,2048]{1,0:T(8,128)(2,1)} %bitcast.13, bf16[2816,2048]{1,0:T(8,128)(2,1)} %bitcast.16), custom_call_target="tpu_custom_call" | custom-call | bytes 6291456 | tf_op jit(solution)/shard_map/fetch_weights/pallas_call | solution.py:639
  39.0 0.0 collective-permute-done.1.right_ref
  39.0 0.0 copy-done.1
  39.0 0.0 copy-done.2
  39.0 0.0 copy-done.3
  39.0 0.0 copy-done.4
  39.0 0.2 second_norm.1
  39.2 10.6 %all_gather.7.rows_ref = bf16[128,2176]{1,0:T(8,128)(2,1)S(1)} all-gather(bf16[16,2176]{1,0:T(8,128)(2,1)S(1)} %get-tuple-element.28), channel_id=1, replica_groups=mesh['seq'=8,'exp'=4] {'seq'}, dimensions={0}, use_global_device_ids=true | all-gather | bytes 626688 | tf_op jit(solution)/shard_map/all_gather | solution.py:912
  49.8 12.5 %experts.1._ = bf16[32,48,128]{2,1,0:T(8,128)(2,1)} custom-call(bf16[128,2176]{1,0:T(8,128)(2,1)S(1)} %all_gather.7.rows_ref, bf16[768,2048]{1,0:T(8,128)(2,1)S(1)} %get-tuple-element.29.refs_0_, bf16[768,2048]{1,0:T(8,128)(2,1)S(1)} %get-tuple-element.30.refs_1_, bf16[768,2048]{1,0:T(8,128)(2,1)S(1)} %get-tuple-element.31.refs_2_, ...), custom_call_target="tpu_custom_call" | custom-call | tf_op jit(solution)/shard_map/experts/pallas_call | solution.py:795
  62.3 4.9 %all-to-all-start.1 = ((bf16[32,48,128]{2,1,0:T(8,128)(2,1)}), bf16[32,48,128]{2,1,0:T(8,128)(2,1)S(1)}, u32[]{:S(2)}, u32[]{:S(2)}) async-start(bf16[32,48,128]{2,1,0:T(8,128)(2,1)} %experts.1._), calls=%async_computation.1 | async-start | bytes 786432 | tf_op jit(solution)/shard_map/all_to_all | solution.py:932
  67.2 9.1 %updated_caches.1 = (bf16[46,128,512]{2,1,0:T(8,128)(2,1)}, bf16[46,128,512]{2,1,0:T(8,128)(2,1)}) custom-call(s32[24]{0:T(128)} %lens_ref.3, s32[46]{0:T(128)} %slot_req_ref.1, s32[46]{0:T(128)} %slot_block_ref.1, bf16[128,512]{1,0:T(8,128)(2,1)S(1)} %get-tuple-element.33.keys_ref, bf16[128,512]{1,0:T(8,128)(2,1)S(1)} %get-tuple-element.34.values_ref, ...), custom_call_target="tpu_custom_call" | custom-call | bytes 24117248 | tf_op jit(solution)/shard_map/updated_caches/pallas_call | solution.py:512
  76.3 3.7 %all-to-all-done.1.parts_ref = bf16[32,48,128]{2,1,0:T(8,128)(2,1)S(1)} async-done(((bf16[32,48,128]{2,1,0:T(8,128)(2,1)}), bf16[32,48,128]{2,1,0:T(8,128)(2,1)S(1)}, u32[]{:S(2)}, u32[]{:S(2)}) %all-to-all-start.1) | async-done | bytes 393248 | tf_op jit(solution)/shard_map/all_to_all | solution.py:932
  80.0 0.7 last_sum.1
  (1 shorter events, 0.0 us)
Async XLA Ops:
  20.4 8.3 %copy-start = (bf16[512,2048]{1,0:T(8,128)(2,1)S(1)}, bf16[512,2048]{1,0:T(8,128)(2,1)}, u32[]{:S(2)}) copy-start(bf16[512,2048]{1,0:T(8,128)(2,1)} %weight_ref.1) | copy-start | bytes 6291460
  20.4 8.3 %all-to-all-start = ((bf16[8,64,128]{2,1,0:T(8,128)(2,1)}), bf16[8,64,128]{2,1,0:T(8,128)(2,1)S(1)}, u32[]{:S(2)}, u32[]{:S(2)}) async-start(bf16[8,64,128]{2,1,0:T(8,128)(2,1)} %get-tuple-element.20), calls=%async_computation | async-start | bytes 262144 | tf_op jit(solution)/shard_map/all_to_all | solution.py:887
  29.5 4.2 %collective-permute-start = (bf16[16,2048]{1,0:T(8,128)(2,1)S(1)}, bf16[16,2048]{1,0:T(8,128)(2,1)S(1)}, u32[]{:S(2)}, u32[]{:S(2)}) collective-permute-start(bf16[16,2048]{1,0:T(8,128)(2,1)S(1)} %merge_project.1._), channel_id=1, source_target_pairs={{0,1},{1,0},{2,3},{3,2},{4,5},{5,4},{6,7},{7,6},{8,9},{9,8},{10,11... | collective-permute-start | bytes 196616 | tf_op jit(solution)/shard_map/ppermute | solution.py:846
  33.7 5.3 %copy-start.1 = (f32[3,4,2048]{2,1,0:T(4,128)S(1)}, f32[3,4,2048]{2,1,0:T(4,128)}, u32[]{:S(2)}) copy-start(f32[3,4,2048]{2,1,0:T(4,128)} %hidden_ref.1) | copy-start | bytes 294916
  33.7 5.3 %copy-start.2 = (f32[2048]{0:T(1024)S(1)}, f32[2048]{0:T(1024)}, u32[]{:S(2)}) copy-start(f32[2048]{0:T(1024)} %param.31) | copy-start | bytes 24580
  33.7 5.3 %copy-start.3 = (s32[3,4,6]{2,1,0:T(4,128)S(1)}, s32[3,4,6]{2,1,0:T(4,128)}, u32[]{:S(2)}) copy-start(s32[3,4,6]{2,1,0:T(4,128)} %ids_ref.1) | copy-start | bytes 868
  33.7 5.3 %copy-start.4 = (f32[3,4,6]{2,1,0:T(4,128)S(1)}, f32[3,4,6]{2,1,0:T(4,128)}, u32[]{:S(2)}) copy-start(f32[3,4,6]{2,1,0:T(4,128)} %gates_ref.1) | copy-start | bytes 868
  33.7 5.2 %collective-permute-start.1 = (bf16[16,2048]{1,0:T(8,128)(2,1)S(1)}, bf16[16,2048]{1,0:T(8,128)(2,1)S(1)}, u32[]{:S(2)}, u32[]{:S(2)}) collective-permute-start(bf16[16,2048]{1,0:T(8,128)(2,1)S(1)} %add_convert_fusion.left_ref._), channel_id=1, source_target_pairs={{0,2},{1,3},{2,0},{3,1},{4,6},{5,7},{6,4},{7,5},{8,10},{9,11},{10,... | collective-permute-start | bytes 196616 | tf_op jit(solution)/shard_map/ppermute | solution.py:846
  62.3 17.6 %all-to-all-start.1 = ((bf16[32,48,128]{2,1,0:T(8,128)(2,1)}), bf16[32,48,128]{2,1,0:T(8,128)(2,1)S(1)}, u32[]{:S(2)}, u32[]{:S(2)}) async-start(bf16[32,48,128]{2,1,0:T(8,128)(2,1)} %experts.1._), calls=%async_computation.1 | async-start | bytes 786432 | tf_op jit(solution)/shard_map/all_to_all | solution.py:932

commit v5 on v4

--- a/solution.py
+++ b/solution.py
@@ -674,21 +674,21 @@
     rows_ref,
     gate_hbm,
     up_hbm,
-    down_hbm,
+    down_ref,
     shared_gate_hbm,
     shared_up_hbm,
     shared_down_hbm,
     out_ref,
     gate_ref,
     up_ref,
-    down_ref,
+    shared_down_ref,
     inner_ref,
     total_ref,
     sem,
     shared_sem,
 ):
     hidden, width = gate_hbm.shape
-    every = down_ref.shape[0]
+    every = hidden + shared_down_ref.shape[0]
     each = hidden // count
     slim, length = shared_window(shared_gate_hbm.shape[0], ranks)
     seq_rank = lax.axis_index("seq")
@@ -727,8 +727,10 @@
 
     gates = moves(gate_hbm, shared_gate_hbm, gate_ref, 0, skipped)
     ups = moves(up_hbm, shared_up_hbm, up_ref, 1, skipped)
-    downs = moves(down_hbm, shared_down_hbm, down_ref, 2, 0)
-    stream = Stream([a + b for a, b in zip(gates, ups)] + downs, 2)
+    shared_down = pltpu.make_async_copy(
+        shared_down_hbm.at[pl.ds(slim_start, length)], shared_down_ref, shared_sem.at[2]
+    )
+    stream = Stream([a + b for a, b in zip(gates, ups)] + [[shared_down]], 3)
 
     first = seq_rank * count
     rows = rows_ref[:, pl.ds(0, width)]
@@ -757,11 +759,16 @@
     pieces = out_ref.shape[0] // groups
     columns = width // pieces
     for i, (low, high) in enumerate(blocks):
-        stream.need(len(gates) + 1 + i)
-        part = inner_ref[:, pl.ds(low, high - low)]
+        top = min(high, hidden)
+        part = inner_ref[:, pl.ds(low, top - low)]
+        if high == every:
+            stream.need(len(gates) + 1)
+            extra = inner_ref[:, pl.ds(hidden, length)]
         for p in range(pieces):
             cut = pl.ds(p * columns, columns)
-            sums = dot_nn(part, down_ref[pl.ds(low, high - low), cut])
+            sums = dot_nn(part, down_ref[pl.ds(low, top - low), cut])
+            if high == every:
+                sums = sums + dot_nn(extra, shared_down_ref[:, cut])
             if i > 0:
                 sums = sums + total_ref[:, cut]
             if i < len(blocks) - 1:
@@ -795,21 +802,21 @@
     return pl.pallas_call(
         functools.partial(experts_kernel, tokens, count, groups, len(early) // 2),
         out_shape=jax.ShapeDtypeStruct((groups * pieces, *shape), BF16),
-        in_specs=[vmem()] * (1 + len(early)) + [hbm()] * 6,
+        in_specs=[vmem()] * (1 + len(early)) + [hbm()] * 2 + [vmem()] + [hbm()] * 3,
         out_specs=vmem(),
         scratch_shapes=[pltpu.VMEM((rest, width), BF16)] * 2
         + [
-            pltpu.VMEM((every, width), BF16),
+            pltpu.VMEM((every - hidden, width), BF16),
             pltpu.VMEM((rows.shape[0], every), BF16),
             pltpu.VMEM((rows.shape[0], width), F32),
             pltpu.SemaphoreType.DMA((3, -(-every // BLOCK))),
             pltpu.SemaphoreType.DMA((3,)),
         ],
         compiler_params=pltpu.CompilerParams(
-            vmem_limit_bytes=(2 * rest + every) * width * 2 + 8 * MIB
+            vmem_limit_bytes=2 * rest * width * 2 + 8 * MIB
         ),
         name="experts",
-    )(rows, *[near(array) for array in early], *[far(array) for array in (*routed, *shared)])
+    )(rows, *[near(array) for array in early], far(routed[0]), far(routed[1]), near(routed[2]), *[far(array) for array in shared])
 
 
 def last_kernel(res_ref, parts_ref, out_ref):

time: 81.1 us -> 79.6 us (0.982)
    pallas_call x1, Pallas kernels: 12.5 us -> 11 us  [all_experts(): pl.pallas_call(functools.partial(experts_kernel, tokens, count, groups, l...]
  transfers between devices with their start and end apart: 4 -> 4, of which waited for: 2 -> 2; matrix products, arithmetic and copies ran while one was open for 0% -> 0% of each run, Pallas kernels for 23% -> 25%
where the time goes in v5:
time: 79.6 us; the launch traced here: 79.2 us
  Pallas kernels  40.6 us (51%)
  blocking collectives  21.6 us (27%)
  starting transfers between devices  11.6 us (15%)
  waiting for transfers between devices  4.49 us (6%)
  between operations  0.84 us (1%)
    all_gather x1, blocking collectives, body(): rows = lax.all_gather(normed, 'seq', axis=0, tiled=True)  11.2 us
    pallas_call x1, Pallas kernels, all_experts(): pl.pallas_call(functools.partial(experts_kernel, tokens, count, groups, l...  11 us
    all_gather x1, blocking collectives, body(): all_rows = lax.all_gather(ffn_in, 'seq', axis=0, tiled=True)  10.4 us
    pallas_call x1, Pallas kernels, updated_caches(): pl.pallas_call(functools.partial(cache_kernel, local, steps), out_shape=(...  9.07 us
    pallas_call x1, Pallas kernels, attention(): pl.pallas_call(functools.partial(attention_kernel, local, steps), out_sha...  7.52 us
    pallas_call x2, Pallas kernels, fetch(): pl.pallas_call(functools.partial(fetch_kernel, low, high - low), out_shap...  6.49 us
    all_to_all x1, starting transfers between devices, body(): lax.all_to_all(sums, ('seq', 'exp'), split_axis=0, concat_axis=0, tiled=T...  4.29 us
    pallas_call x1, Pallas kernels, fresh_rows(): pl.pallas_call(functools.partial(fresh_kernel, local, steps), out_shape=(...  3.88 us
  transfers between devices with their start and end apart: 4, of which 2 were waited for; matrix products, arithmetic and copies ran while one was open for 0% of the time, Pallas kernels for 25%

profile of v5, /device:TPU:1, one launch (start us, length us, event | category | flops | bytes accessed | tf_op | source)
XLA Modules:
  0.0 79.2 jit_solution(12422670406605768458)
XLA Ops:
  0.6 1.0 %norm_rows.1 = bf16[16,2048]{1,0:T(8,128)(2,1)S(1)} custom-call(f32[3,4,2048]{2,1,0:T(4,128)} %hidden_ref.1, f32[1,2048]{1,0:T(1,128)} %bitcast.23), custom_call_target="tpu_custom_call" | custom-call | tf_op jit(solution)/shard_map/norm_rows/pallas_call | solution.py:98
  1.7 11.2 %all_gather.6.rows_ref = bf16[128,2048]{1,0:T(8,128)(2,1)S(1)} all-gather(bf16[16,2048]{1,0:T(8,128)(2,1)S(1)} %norm_rows.1), channel_id=1, replica_groups=mesh['seq'=8,'exp'=4] {'seq'}, dimensions={0}, use_global_device_ids=true | all-gather | bytes 589824 | tf_op jit(solution)/shard_map/all_gather | solution.py:883
  12.9 7.5 %attention.1 = (bf16[8,64,128]{2,1,0:T(8,128)(2,1)}, bf16[128,512]{1,0:T(8,128)(2,1)S(1)}) custom-call(s32[24]{0:T(128)} %lens_ref.3, s32[46]{0:T(128)} %slot_req_ref.1, s32[46]{0:T(128)} %slot_block_ref.1, bf16[128,2048]{1,0:T(8,128)(2,1)S(1)} %all_gather.6.rows_ref, bf16[2048,512]{1,0:T(8,128)(2,1)} %query_hbm.1, bf16[46,128,512]{2,1,0:T(8,128)(2,1)} %key_in.3, ...), custom_call_target="tpu_custom_call" | custom-call | tf_op jit(solution)/shard_map/attention/pallas_call | solution.py:357
  20.4 0.0 copy-start
  20.4 3.6 %all-to-all-start = ((bf16[8,64,128]{2,1,0:T(8,128)(2,1)}), bf16[8,64,128]{2,1,0:T(8,128)(2,1)S(1)}, u32[]{:S(2)}, u32[]{:S(2)}) async-start(bf16[8,64,128]{2,1,0:T(8,128)(2,1)} %get-tuple-element.20), calls=%async_computation | async-start | bytes 262144 | tf_op jit(solution)/shard_map/all_to_all | solution.py:894
  24.0 3.9 %fresh_rows.1 = (bf16[128,512]{1,0:T(8,128)(2,1)S(1)}, bf16[128,512]{1,0:T(8,128)(2,1)S(1)}, f32[48,128]{1,0:T(8,128)S(1)}, f32[48,128]{1,0:T(8,128)S(1)}) custom-call(s32[24]{0:T(128)} %lens_ref.3, bf16[128,2048]{1,0:T(8,128)(2,1)S(1)} %all_gather.6.rows_ref, bf16[128,512]{1,0:T(8,128)(2,1)S(1)} %get-tuple-element.21.queries_ref, ...), custom_call_target="tpu_custom_call" | custom-call | flops 536870912 | bytes 4194304 | tf_op jit(solution)/shard_map/fresh_rows/pallas_call | solution.py:447
  27.9 0.8 %all-to-all-done.part_ref = bf16[8,64,128]{2,1,0:T(8,128)(2,1)S(1)} async-done(((bf16[8,64,128]{2,1,0:T(8,128)(2,1)}), bf16[8,64,128]{2,1,0:T(8,128)(2,1)S(1)}, u32[]{:S(2)}, u32[]{:S(2)}) %all-to-all-start) | async-done | bytes 131104 | tf_op jit(solution)/shard_map/all_to_all | solution.py:894
  28.7 0.0 copy-done
  28.7 0.7 merge_project.1._
  29.5 1.3 %collective-permute-start = (bf16[16,2048]{1,0:T(8,128)(2,1)S(1)}, bf16[16,2048]{1,0:T(8,128)(2,1)S(1)}, u32[]{:S(2)}, u32[]{:S(2)}) collective-permute-start(bf16[16,2048]{1,0:T(8,128)(2,1)S(1)} %merge_project.1._), channel_id=1, source_target_pairs={{0,1},{1,0},{2,3},{3,2},{4,5},{5,4},{6,7},{7,6},{8,9},{9,8},{10,11... | collective-permute-start | bytes 196616 | tf_op jit(solution)/shard_map/ppermute | solution.py:853
  30.8 2.9 %fetch_weights.2 = (bf16[768,2048]{1,0:T(8,128)(2,1)S(1)}, bf16[768,2048]{1,0:T(8,128)(2,1)S(1)}) custom-call(bf16[16,2048]{1,0:T(8,128)(2,1)S(1)} %merge_project.1._, bf16[2816,2048]{1,0:T(8,128)(2,1)} %bitcast.15, bf16[2816,2048]{1,0:T(8,128)(2,1)} %bitcast.18), custom_call_target="tpu_custom_call" | custom-call | bytes 6291456 | tf_op jit(solution)/shard_map/fetch_weights/pallas_call | solution.py:639
  33.6 0.0 collective-permute-done
  33.6 0.0 slice-start
  33.7 0.0 copy-start.1
  33.7 0.0 copy-start.2
  33.7 0.0 copy-start.3
  33.7 0.0 copy-start.4
  33.7 0.0 slice-start.1
  33.8 0.0 slice-start.2
  33.8 2.4 %collective-permute-start.1 = (bf16[16,2048]{1,0:T(8,128)(2,1)S(1)}, bf16[16,2048]{1,0:T(8,128)(2,1)S(1)}, u32[]{:S(2)}, u32[]{:S(2)}) collective-permute-start(bf16[16,2048]{1,0:T(8,128)(2,1)S(1)} %add_convert_fusion.left_ref._), channel_id=1, source_target_pairs={{0,2},{1,3},{2,0},{3,1},{4,6},{5,7},{6,4},{7,5},{8,10},{9,11},{10,... | collective-permute-start | bytes 196616 | tf_op jit(solution)/shard_map/ppermute | solution.py:853
  36.1 3.6 %fetch_weights.3 = (bf16[768,2048]{1,0:T(8,128)(2,1)S(1)}, bf16[768,2048]{1,0:T(8,128)(2,1)S(1)}) custom-call(bf16[16,2048]{1,0:T(8,128)(2,1)S(1)} %add_convert_fusion.left_ref._, bf16[2816,2048]{1,0:T(8,128)(2,1)} %bitcast.16, bf16[2816,2048]{1,0:T(8,128)(2,1)} %bitcast.19), custom_call_target="tpu_custom_call" | custom-call | bytes 6291456 | tf_op jit(solution)/shard_map/fetch_weights/pallas_call | solution.py:639
  39.8 0.0 collective-permute-done.1.right_ref
  39.8 0.0 copy-done.1
  39.8 0.0 copy-done.2
  39.8 0.2 second_norm.1
  40.0 10.4 %all_gather.7.rows_ref = bf16[128,2176]{1,0:T(8,128)(2,1)S(1)} all-gather(bf16[16,2176]{1,0:T(8,128)(2,1)S(1)} %get-tuple-element.28), channel_id=1, replica_groups=mesh['seq'=8,'exp'=4] {'seq'}, dimensions={0}, use_global_device_ids=true | all-gather | bytes 626688 | tf_op jit(solution)/shard_map/all_gather | solution.py:919
  50.4 0.0 slice-done.2
  50.4 11.0 %experts.1._ = bf16[32,48,128]{2,1,0:T(8,128)(2,1)} custom-call(bf16[128,2176]{1,0:T(8,128)(2,1)S(1)} %all_gather.7.rows_ref, bf16[768,2048]{1,0:T(8,128)(2,1)S(1)} %get-tuple-element.29.refs_0_, bf16[768,2048]{1,0:T(8,128)(2,1)S(1)} %get-tuple-element.30.refs_1_, bf16[768,2048]{1,0:T(8,128)(2,1)S(1)} %get-tuple-element.31.refs_2_, ...), custom_call_target="tpu_custom_call" | custom-call | tf_op jit(solution)/shard_map/experts/pallas_call | solution.py:802
  61.4 4.3 %all-to-all-start.1 = ((bf16[32,48,128]{2,1,0:T(8,128)(2,1)}), bf16[32,48,128]{2,1,0:T(8,128)(2,1)S(1)}, u32[]{:S(2)}, u32[]{:S(2)}) async-start(bf16[32,48,128]{2,1,0:T(8,128)(2,1)} %experts.1._), calls=%async_computation.1 | async-start | bytes 786432 | tf_op jit(solution)/shard_map/all_to_all | solution.py:939
  65.7 9.1 %updated_caches.1 = (bf16[46,128,512]{2,1,0:T(8,128)(2,1)}, bf16[46,128,512]{2,1,0:T(8,128)(2,1)}) custom-call(s32[24]{0:T(128)} %lens_ref.3, s32[46]{0:T(128)} %slot_req_ref.1, s32[46]{0:T(128)} %slot_block_ref.1, bf16[128,512]{1,0:T(8,128)(2,1)S(1)} %get-tuple-element.33.keys_ref, bf16[128,512]{1,0:T(8,128)(2,1)S(1)} %get-tuple-element.34.values_ref, ...), custom_call_target="tpu_custom_call" | custom-call | bytes 24117248 | tf_op jit(solution)/shard_map/updated_caches/pallas_call | solution.py:512
  74.8 3.7 %all-to-all-done.1.parts_ref = bf16[32,48,128]{2,1,0:T(8,128)(2,1)S(1)} async-done(((bf16[32,48,128]{2,1,0:T(8,128)(2,1)}), bf16[32,48,128]{2,1,0:T(8,128)(2,1)S(1)}, u32[]{:S(2)}, u32[]{:S(2)}) %all-to-all-start.1) | async-done | bytes 393248 | tf_op jit(solution)/shard_map/all_to_all | solution.py:939
  78.5 0.7 last_sum.1
  (6 shorter events, 0.0 us)
Async XLA Ops:
  20.4 8.3 %copy-start = (bf16[512,2048]{1,0:T(8,128)(2,1)S(1)}, bf16[512,2048]{1,0:T(8,128)(2,1)}, u32[]{:S(2)}) copy-start(bf16[512,2048]{1,0:T(8,128)(2,1)} %weight_ref.1) | copy-start | bytes 6291460
  20.4 8.3 %all-to-all-start = ((bf16[8,64,128]{2,1,0:T(8,128)(2,1)}), bf16[8,64,128]{2,1,0:T(8,128)(2,1)S(1)}, u32[]{:S(2)}, u32[]{:S(2)}) async-start(bf16[8,64,128]{2,1,0:T(8,128)(2,1)} %get-tuple-element.20), calls=%async_computation | async-start | bytes 262144 | tf_op jit(solution)/shard_map/all_to_all | solution.py:894
  29.5 4.2 %collective-permute-start = (bf16[16,2048]{1,0:T(8,128)(2,1)S(1)}, bf16[16,2048]{1,0:T(8,128)(2,1)S(1)}, u32[]{:S(2)}, u32[]{:S(2)}) collective-permute-start(bf16[16,2048]{1,0:T(8,128)(2,1)S(1)} %merge_project.1._), channel_id=1, source_target_pairs={{0,1},{1,0},{2,3},{3,2},{4,5},{5,4},{6,7},{7,6},{8,9},{9,8},{10,11... | collective-permute-start | bytes 196616 | tf_op jit(solution)/shard_map/ppermute | solution.py:853
  33.6 16.7 %slice-start = ((s8[11534336]{0:T(1024)(128)(4,1)}), s8[4194304]{0:T(1024)(128)(4,1)S(1)}, s32[]{:S(2)}) async-start(s8[11534336]{0:T(1024)(128)(4,1)} %bitcast.11), calls=%async_computation.2 | async-start | bytes 8388608
  33.7 6.1 %copy-start.1 = (f32[3,4,2048]{2,1,0:T(4,128)S(1)}, f32[3,4,2048]{2,1,0:T(4,128)}, u32[]{:S(2)}) copy-start(f32[3,4,2048]{2,1,0:T(4,128)} %hidden_ref.1) | copy-start | bytes 294916
  33.7 6.1 %copy-start.2 = (f32[2048]{0:T(1024)S(1)}, f32[2048]{0:T(1024)}, u32[]{:S(2)}) copy-start(f32[2048]{0:T(1024)} %param.31) | copy-start | bytes 24580
  33.7 6.1 %copy-start.3 = (s32[3,4,6]{2,1,0:T(4,128)S(1)}, s32[3,4,6]{2,1,0:T(4,128)}, u32[]{:S(2)}) copy-start(s32[3,4,6]{2,1,0:T(4,128)} %ids_ref.1) | copy-start | bytes 868
  33.7 6.1 %copy-start.4 = (f32[3,4,6]{2,1,0:T(4,128)S(1)}, f32[3,4,6]{2,1,0:T(4,128)}, u32[]{:S(2)}) copy-start(f32[3,4,6]{2,1,0:T(4,128)} %gates_ref.1) | copy-start | bytes 868
  33.7 16.6 %slice-start.1 = ((s8[11534336]{0:T(1024)(128)(4,1)}), s8[4194304]{0:T(1024)(128)(4,1)S(1)}, s32[]{:S(2)}) async-start(s8[11534336]{0:T(1024)(128)(4,1)} %bitcast.11), calls=%async_computation.3 | async-start | bytes 8388608
  33.8 16.6 %slice-start.2 = ((s8[11534336]{0:T(1024)(128)(4,1)}), s8[3145728]{0:T(1024)(128)(4,1)S(1)}, s32[]{:S(2)}) async-start(s8[11534336]{0:T(1024)(128)(4,1)} %bitcast.11), calls=%async_computation.4 | async-start | bytes 6291456
  33.8 6.0 %collective-permute-start.1 = (bf16[16,2048]{1,0:T(8,128)(2,1)S(1)}, bf16[16,2048]{1,0:T(8,128)(2,1)S(1)}, u32[]{:S(2)}, u32[]{:S(2)}) collective-permute-start(bf16[16,2048]{1,0:T(8,128)(2,1)S(1)} %add_convert_fusion.left_ref._), channel_id=1, source_target_pairs={{0,2},{1,3},{2,0},{3,1},{4,6},{5,7},{6,4},{7,5},{8,10},{9,11},{10,... | collective-permute-start | bytes 196616 | tf_op jit(solution)/shard_map/ppermute | solution.py:853
  61.4 17.0 %all-to-all-start.1 = ((bf16[32,48,128]{2,1,0:T(8,128)(2,1)}), bf16[32,48,128]{2,1,0:T(8,128)(2,1)S(1)}, u32[]{:S(2)}, u32[]{:S(2)}) async-start(bf16[32,48,128]{2,1,0:T(8,128)(2,1)} %experts.1._), calls=%async_computation.1 | async-start | bytes 786432 | tf_op jit(solution)/shard_map/all_to_all | solution.py:939
